TPU v7x, 256 devices: a whole 4x4x8 slice. The times are simulated.
256 devices in a mesh: queue: 64 (over z, y, core), head: 4 (over x).
Axes of the slice: x: 4, y: 4, z: 8, core: 2. Of those that a mesh axis runs over, the one named last changes fastest.
Arguments:
- latents: bfloat16 [12288, 1536], P('queue', 'head'), may hold values from -6 to 6
- fresh_frame: bfloat16 [384, 1536], P(None, 'head'), may hold values from -6 to 6
- noise_level: int32 [32], replicated, may hold values from 0 to 127, as said below
- offset: int32 [1], replicated, may hold values from 0 to 131071
- mod_table: float32 [128, 3, 1536], replicated, may hold values from -4 to 4
- w_qkv: bfloat16 [1536, 3, 1536], P(None, None, 'head'), may hold values from -1 to 1
- w_out: bfloat16 [1536, 1536], P('head'), may hold values from -0.15625 to 0.15625
- q_gain: float32 [1536], P('head'), may hold values from 1 to 3
- k_gain: float32 [1536], P('head'), may hold values from 1 to 3
Outputs:
- advanced: bfloat16 [12288, 1536], P('queue', 'head')
Inputs may be any that keep to these rules, and one draw needn't show every extreme that they name: `noise_level`: entry p lies in p * 4 to (p + 1) * 4 - 1.
All inputs are finite; a program needn't handle non-finite values.
Results may differ from a plain program's by a relative error of at most 0.011.
Values may be sent and summed in bfloat16 or wider, within the bound.
No kernel may reach another device: no remote copies, remote signals or barrier semaphores. Data moves between devices by JAX's collectives and lax.ppermute only.
A program may use at most 128 MiB of HBM per device.

v0:
```python
import jax
import jax.numpy as jnp
from jax import lax
from jax.sharding import PartitionSpec as P

D = 1536
DH = 128


def passed_along(block, axis, distance):
    devices = range(lax.axis_size(axis))
    route = [((i - distance) % len(devices), i) for i in devices]
    return lax.ppermute(block, axis, route)


def attend(carried, queries, key_block, value_block, allowed):
    run_max, run_total, running = carried
    key_count = key_block.shape[0]
    head_count = queries.shape[1]
    key_heads = key_block.reshape(key_count, head_count, DH)
    value_heads = value_block.reshape(key_count, head_count, DH)
    scores = jnp.einsum(
        "qhd,khd->hqk", queries, key_heads, preferred_element_type=jnp.float32
    ) * DH ** (-0.5)
    scores = jnp.where(allowed[None, None, :], scores, -jnp.inf)
    new_max = jnp.maximum(run_max, jnp.max(scores, axis=2))
    rescale = jnp.exp(run_max - new_max)
    exp_scores = jnp.exp(scores - new_max[:, :, None])
    new_total = run_total * rescale + jnp.sum(exp_scores, axis=2)
    added = jnp.einsum(
        "hqk,khd->hqd",
        exp_scores.astype(jnp.bfloat16),
        value_heads,
        preferred_element_type=jnp.float32,
    )
    return (new_max, new_total, running * rescale[:, :, None] + added)


def local(latents, fresh_frame, noise_level, offset, mod_table, w_qkv, w_out, q_gain, k_gain):
    slabs = lax.axis_size("queue")
    frames = slabs // 2
    my_slab = lax.axis_index("queue")
    my_frame = my_slab // 2
    position = jnp.mod(my_frame - offset[0], frames)
    my_level = noise_level[position]
    modulation = lax.dynamic_index_in_dim(mod_table, my_level, 0, keepdims=False)
    whole = lax.all_gather(latents, "head", axis=1, tiled=True).astype(jnp.float32)
    row_count = whole.shape[0]
    centered = whole - jnp.mean(whole, axis=1, keepdims=True)
    variance = jnp.mean(centered * centered, axis=1, keepdims=True)
    normed = centered * lax.rsqrt(variance + 1e-06)
    modded = (normed * (1.0 + modulation[1]) + modulation[0]).astype(jnp.bfloat16)
    local_width = w_qkv.shape[2]
    projected = jnp.dot(
        modded, w_qkv.reshape(w_qkv.shape[0], 3 * local_width), preferred_element_type=jnp.float32
    )
    projected = projected.reshape(row_count, 3, local_width)
    query_raw = projected[:, 0]
    key_raw = projected[:, 1]
    values = projected[:, 2].astype(jnp.bfloat16)
    query_sq, key_sq = lax.psum(
        (jnp.sum(query_raw * query_raw, axis=1), jnp.sum(key_raw * key_raw, axis=1)), "head"
    )
    queries = (query_raw * lax.rsqrt(query_sq / D + 1e-06)[:, None] * q_gain).astype(jnp.bfloat16)
    key_normed = (key_raw * lax.rsqrt(key_sq / D + 1e-06)[:, None] * k_gain).astype(jnp.bfloat16)
    head_count = local_width // DH
    query_heads = queries.reshape(row_count, head_count, DH)
    start_state = (
        jnp.full((head_count, row_count), -1e30, jnp.float32),
        jnp.zeros((head_count, row_count), jnp.float32),
        jnp.zeros((head_count, row_count, DH), jnp.float32),
    )
    all_rows = jnp.ones((row_count,), dtype=bool)
    carried = attend(start_state, query_heads, key_normed, values, all_rows)
    stacked = jnp.stack((key_normed, values))

    def pass_step(turn, loop_state):
        pieces, state_now = loop_state
        pieces = passed_along(pieces, "queue", 1)
        key_slab = jnp.mod(my_slab - turn, slabs)
        key_pos = jnp.mod(key_slab // 2 - offset[0], frames)

        def use_piece(state_in):
            return attend(state_in, query_heads, pieces[0], pieces[1], all_rows)

        def keep_state(state_in):
            return state_in

        state_now = lax.cond(key_pos <= position, use_piece, keep_state, state_now)
        return (pieces, state_now)

    stacked, carried = lax.fori_loop(1, slabs, pass_step, (stacked, carried))
    run_max, run_total, running = carried
    attn = (
        jnp.transpose(running / run_total[:, :, None], (1, 0, 2))
        .reshape(row_count, local_width)
        .astype(jnp.bfloat16)
    )
    partial_out = jnp.dot(attn, w_out, preferred_element_type=jnp.float32)
    proj = lax.psum_scatter(
        partial_out.astype(jnp.bfloat16), "head", scatter_dimension=1, tiled=True
    ).astype(jnp.float32)
    feature_start = lax.axis_index("head") * local_width
    gate_local = lax.dynamic_slice_in_dim(modulation[2], feature_start, local_width)
    updated = (latents.astype(jnp.float32) + gate_local * proj).astype(jnp.bfloat16)
    moved = passed_along(updated, "queue", -2)
    entry_slot = jnp.mod(offset[0] - 1, frames)
    fresh_half = lax.dynamic_slice_in_dim(fresh_frame, my_slab % 2 * row_count, row_count, 0)
    return jnp.where(my_frame == entry_slot, fresh_half, moved)


def solution(mesh):
    return jax.shard_map(
        local,
        mesh=mesh,
        in_specs=(
            P("queue", "head"),
            P(None, "head"),
            P(),
            P(),
            P(),
            P(None, None, "head"),
            P("head", None),
            P("head"),
            P("head"),
        ),
        out_specs=P("queue", "head"),
        check_vma=False,
    )
```

profile of v0, /device:TPU:24, one launch (start us, length us, event | category | flops | bytes accessed | tf_op | source)
XLA Modules:
  0.0 732.1 jit_solution(15780978132263024809)
XLA Ops:
  9.9 13.7 %all_gather.3 = bf16[192,1536]{1,0:T(8,128)(2,1)S(1)} all-gather(bf16[192,384]{1,0:T(8,128)(2,1)} %param.13), channel_id=1, replica_groups=mesh['queue'=64,'head'=4] {'head'}, dimensions={1}, use_global_device_ids=true | all-gather | bytes 737280 | tf_op jit(solution)/shard_map/all_gather | solution.py:47
  36.1 10.9 %all-reduce = (f32[192]{0:T(256)S(1)}, f32[192]{0:T(256)S(1)}) all-reduce(f32[192]{0:T(256)S(1)} %get-tuple-element.327, f32[192]{0:T(256)S(1)} %get-tuple-element.326), channel_id=1, replica_groups=mesh['queue'=64,'head'=4] {'head'}, use_global_device_ids=true, to_apply=%region_3.4 | all-reduce | flops 384 | bytes 3072 | tf_op jit(solution)/shard_map/psum | solution.py:61
  48.7 610.9 %while.22 = (s32[]{:T(128)}, bf16[2,192,384]{2,1,0:T(8,128)(2,1)S(1)}, f32[3,192]{1,0:T(4,128)S(1)}, f32[3,192]{1,0:T(4,128)S(1)}, f32[3,192,128]{2,1,0:T(8,128)...) while((s32[]{:T(128)}, ...), condition=%wide.region_13.14_spmd, body=%wide.region_8.13_spmd.sunk | while | flops 57435304 | bytes 5345971 | solution.py:92
  85.5 7.1 collective-permute-start
  104.2 7.1 collective-permute-start
  113.5 7.1 collective-permute-start
  132.2 7.1 collective-permute-start
  141.5 7.1 collective-permute-start
  160.2 7.1 collective-permute-start
  169.5 7.1 collective-permute-start
  188.2 7.1 collective-permute-start
  197.5 7.1 collective-permute-start
  216.2 7.1 collective-permute-start
  244.2 7.1 collective-permute-start
  308.1 7.2 collective-permute-done
  317.4 8.4 %collective-permute-done = bf16[2,192,384]{2,1,0:T(8,128)(2,1)S(1)} collective-permute-done((bf16[2,192,384]{2,1,0:T(8,128)(2,1)S(1)}, bf16[2,192,384]{2,1,0:T(8,128)(2,1)S(1)}, u32[]{:S(2)}, u32[]{:S(2)}) %collective-permute-start) | collective-permute-done | bytes 294944 | tf_op jit(solution)/shard_map/while/body/eval_jaxpr/ppermute | solution.py:13
  327.6 8.8 %collective-permute-done = bf16[2,192,384]{2,1,0:T(8,128)(2,1)S(1)} collective-permute-done((bf16[2,192,384]{2,1,0:T(8,128)(2,1)S(1)}, bf16[2,192,384]{2,1,0:T(8,128)(2,1)S(1)}, u32[]{:S(2)}, u32[]{:S(2)}) %collective-permute-start) | collective-permute-done | bytes 294944 | tf_op jit(solution)/shard_map/while/body/eval_jaxpr/ppermute | solution.py:13
  338.1 8.7 %collective-permute-done = bf16[2,192,384]{2,1,0:T(8,128)(2,1)S(1)} collective-permute-done((bf16[2,192,384]{2,1,0:T(8,128)(2,1)S(1)}, bf16[2,192,384]{2,1,0:T(8,128)(2,1)S(1)}, u32[]{:S(2)}, u32[]{:S(2)}) %collective-permute-start) | collective-permute-done | bytes 294944 | tf_op jit(solution)/shard_map/while/body/eval_jaxpr/ppermute | solution.py:13
  348.7 8.7 %collective-permute-done = bf16[2,192,384]{2,1,0:T(8,128)(2,1)S(1)} collective-permute-done((bf16[2,192,384]{2,1,0:T(8,128)(2,1)S(1)}, bf16[2,192,384]{2,1,0:T(8,128)(2,1)S(1)}, u32[]{:S(2)}, u32[]{:S(2)}) %collective-permute-start) | collective-permute-done | bytes 294944 | tf_op jit(solution)/shard_map/while/body/eval_jaxpr/ppermute | solution.py:13
  359.2 8.8 %collective-permute-done = bf16[2,192,384]{2,1,0:T(8,128)(2,1)S(1)} collective-permute-done((bf16[2,192,384]{2,1,0:T(8,128)(2,1)S(1)}, bf16[2,192,384]{2,1,0:T(8,128)(2,1)S(1)}, u32[]{:S(2)}, u32[]{:S(2)}) %collective-permute-start) | collective-permute-done | bytes 294944 | tf_op jit(solution)/shard_map/while/body/eval_jaxpr/ppermute | solution.py:13
  369.8 8.8 %collective-permute-done = bf16[2,192,384]{2,1,0:T(8,128)(2,1)S(1)} collective-permute-done((bf16[2,192,384]{2,1,0:T(8,128)(2,1)S(1)}, bf16[2,192,384]{2,1,0:T(8,128)(2,1)S(1)}, u32[]{:S(2)}, u32[]{:S(2)}) %collective-permute-start) | collective-permute-done | bytes 294944 | tf_op jit(solution)/shard_map/while/body/eval_jaxpr/ppermute | solution.py:13
  380.3 8.7 %collective-permute-done = bf16[2,192,384]{2,1,0:T(8,128)(2,1)S(1)} collective-permute-done((bf16[2,192,384]{2,1,0:T(8,128)(2,1)S(1)}, bf16[2,192,384]{2,1,0:T(8,128)(2,1)S(1)}, u32[]{:S(2)}, u32[]{:S(2)}) %collective-permute-start) | collective-permute-done | bytes 294944 | tf_op jit(solution)/shard_map/while/body/eval_jaxpr/ppermute | solution.py:13
  390.9 8.7 %collective-permute-done = bf16[2,192,384]{2,1,0:T(8,128)(2,1)S(1)} collective-permute-done((bf16[2,192,384]{2,1,0:T(8,128)(2,1)S(1)}, bf16[2,192,384]{2,1,0:T(8,128)(2,1)S(1)}, u32[]{:S(2)}, u32[]{:S(2)}) %collective-permute-start) | collective-permute-done | bytes 294944 | tf_op jit(solution)/shard_map/while/body/eval_jaxpr/ppermute | solution.py:13
  401.4 8.8 %collective-permute-done = bf16[2,192,384]{2,1,0:T(8,128)(2,1)S(1)} collective-permute-done((bf16[2,192,384]{2,1,0:T(8,128)(2,1)S(1)}, bf16[2,192,384]{2,1,0:T(8,128)(2,1)S(1)}, u32[]{:S(2)}, u32[]{:S(2)}) %collective-permute-start) | collective-permute-done | bytes 294944 | tf_op jit(solution)/shard_map/while/body/eval_jaxpr/ppermute | solution.py:13
  412.0 8.8 %collective-permute-done = bf16[2,192,384]{2,1,0:T(8,128)(2,1)S(1)} collective-permute-done((bf16[2,192,384]{2,1,0:T(8,128)(2,1)S(1)}, bf16[2,192,384]{2,1,0:T(8,128)(2,1)S(1)}, u32[]{:S(2)}, u32[]{:S(2)}) %collective-permute-start) | collective-permute-done | bytes 294944 | tf_op jit(solution)/shard_map/while/body/eval_jaxpr/ppermute | solution.py:13
  422.5 8.7 %collective-permute-done = bf16[2,192,384]{2,1,0:T(8,128)(2,1)S(1)} collective-permute-done((bf16[2,192,384]{2,1,0:T(8,128)(2,1)S(1)}, bf16[2,192,384]{2,1,0:T(8,128)(2,1)S(1)}, u32[]{:S(2)}, u32[]{:S(2)}) %collective-permute-start) | collective-permute-done | bytes 294944 | tf_op jit(solution)/shard_map/while/body/eval_jaxpr/ppermute | solution.py:13
  433.1 8.7 %collective-permute-done = bf16[2,192,384]{2,1,0:T(8,128)(2,1)S(1)} collective-permute-done((bf16[2,192,384]{2,1,0:T(8,128)(2,1)S(1)}, bf16[2,192,384]{2,1,0:T(8,128)(2,1)S(1)}, u32[]{:S(2)}, u32[]{:S(2)}) %collective-permute-start) | collective-permute-done | bytes 294944 | tf_op jit(solution)/shard_map/while/body/eval_jaxpr/ppermute | solution.py:13
  443.6 8.8 %collective-permute-done = bf16[2,192,384]{2,1,0:T(8,128)(2,1)S(1)} collective-permute-done((bf16[2,192,384]{2,1,0:T(8,128)(2,1)S(1)}, bf16[2,192,384]{2,1,0:T(8,128)(2,1)S(1)}, u32[]{:S(2)}, u32[]{:S(2)}) %collective-permute-start) | collective-permute-done | bytes 294944 | tf_op jit(solution)/shard_map/while/body/eval_jaxpr/ppermute | solution.py:13
  454.1 8.8 %collective-permute-done = bf16[2,192,384]{2,1,0:T(8,128)(2,1)S(1)} collective-permute-done((bf16[2,192,384]{2,1,0:T(8,128)(2,1)S(1)}, bf16[2,192,384]{2,1,0:T(8,128)(2,1)S(1)}, u32[]{:S(2)}, u32[]{:S(2)}) %collective-permute-start) | collective-permute-done | bytes 294944 | tf_op jit(solution)/shard_map/while/body/eval_jaxpr/ppermute | solution.py:13
  464.7 8.7 %collective-permute-done = bf16[2,192,384]{2,1,0:T(8,128)(2,1)S(1)} collective-permute-done((bf16[2,192,384]{2,1,0:T(8,128)(2,1)S(1)}, bf16[2,192,384]{2,1,0:T(8,128)(2,1)S(1)}, u32[]{:S(2)}, u32[]{:S(2)}) %collective-permute-start) | collective-permute-done | bytes 294944 | tf_op jit(solution)/shard_map/while/body/eval_jaxpr/ppermute | solution.py:13
  475.2 8.7 %collective-permute-done = bf16[2,192,384]{2,1,0:T(8,128)(2,1)S(1)} collective-permute-done((bf16[2,192,384]{2,1,0:T(8,128)(2,1)S(1)}, bf16[2,192,384]{2,1,0:T(8,128)(2,1)S(1)}, u32[]{:S(2)}, u32[]{:S(2)}) %collective-permute-start) | collective-permute-done | bytes 294944 | tf_op jit(solution)/shard_map/while/body/eval_jaxpr/ppermute | solution.py:13
  485.8 8.8 %collective-permute-done = bf16[2,192,384]{2,1,0:T(8,128)(2,1)S(1)} collective-permute-done((bf16[2,192,384]{2,1,0:T(8,128)(2,1)S(1)}, bf16[2,192,384]{2,1,0:T(8,128)(2,1)S(1)}, u32[]{:S(2)}, u32[]{:S(2)}) %collective-permute-start) | collective-permute-done | bytes 294944 | tf_op jit(solution)/shard_map/while/body/eval_jaxpr/ppermute | solution.py:13
  496.3 8.8 %collective-permute-done = bf16[2,192,384]{2,1,0:T(8,128)(2,1)S(1)} collective-permute-done((bf16[2,192,384]{2,1,0:T(8,128)(2,1)S(1)}, bf16[2,192,384]{2,1,0:T(8,128)(2,1)S(1)}, u32[]{:S(2)}, u32[]{:S(2)}) %collective-permute-start) | collective-permute-done | bytes 294944 | tf_op jit(solution)/shard_map/while/body/eval_jaxpr/ppermute | solution.py:13
  506.9 8.7 %collective-permute-done = bf16[2,192,384]{2,1,0:T(8,128)(2,1)S(1)} collective-permute-done((bf16[2,192,384]{2,1,0:T(8,128)(2,1)S(1)}, bf16[2,192,384]{2,1,0:T(8,128)(2,1)S(1)}, u32[]{:S(2)}, u32[]{:S(2)}) %collective-permute-start) | collective-permute-done | bytes 294944 | tf_op jit(solution)/shard_map/while/body/eval_jaxpr/ppermute | solution.py:13
  517.4 8.7 %collective-permute-done = bf16[2,192,384]{2,1,0:T(8,128)(2,1)S(1)} collective-permute-done((bf16[2,192,384]{2,1,0:T(8,128)(2,1)S(1)}, bf16[2,192,384]{2,1,0:T(8,128)(2,1)S(1)}, u32[]{:S(2)}, u32[]{:S(2)}) %collective-permute-start) | collective-permute-done | bytes 294944 | tf_op jit(solution)/shard_map/while/body/eval_jaxpr/ppermute | solution.py:13
  528.0 8.8 %collective-permute-done = bf16[2,192,384]{2,1,0:T(8,128)(2,1)S(1)} collective-permute-done((bf16[2,192,384]{2,1,0:T(8,128)(2,1)S(1)}, bf16[2,192,384]{2,1,0:T(8,128)(2,1)S(1)}, u32[]{:S(2)}, u32[]{:S(2)}) %collective-permute-start) | collective-permute-done | bytes 294944 | tf_op jit(solution)/shard_map/while/body/eval_jaxpr/ppermute | solution.py:13
  538.5 8.8 %collective-permute-done = bf16[2,192,384]{2,1,0:T(8,128)(2,1)S(1)} collective-permute-done((bf16[2,192,384]{2,1,0:T(8,128)(2,1)S(1)}, bf16[2,192,384]{2,1,0:T(8,128)(2,1)S(1)}, u32[]{:S(2)}, u32[]{:S(2)}) %collective-permute-start) | collective-permute-done | bytes 294944 | tf_op jit(solution)/shard_map/while/body/eval_jaxpr/ppermute | solution.py:13
  549.1 8.7 %collective-permute-done = bf16[2,192,384]{2,1,0:T(8,128)(2,1)S(1)} collective-permute-done((bf16[2,192,384]{2,1,0:T(8,128)(2,1)S(1)}, bf16[2,192,384]{2,1,0:T(8,128)(2,1)S(1)}, u32[]{:S(2)}, u32[]{:S(2)}) %collective-permute-start) | collective-permute-done | bytes 294944 | tf_op jit(solution)/shard_map/while/body/eval_jaxpr/ppermute | solution.py:13
  573.1 8.7 %collective-permute-done = bf16[2,192,384]{2,1,0:T(8,128)(2,1)S(1)} collective-permute-done((bf16[2,192,384]{2,1,0:T(8,128)(2,1)S(1)}, bf16[2,192,384]{2,1,0:T(8,128)(2,1)S(1)}, u32[]{:S(2)}, u32[]{:S(2)}) %collective-permute-start) | collective-permute-done | bytes 294944 | tf_op jit(solution)/shard_map/while/body/eval_jaxpr/ppermute | solution.py:13
  582.7 8.7 %collective-permute-done = bf16[2,192,384]{2,1,0:T(8,128)(2,1)S(1)} collective-permute-done((bf16[2,192,384]{2,1,0:T(8,128)(2,1)S(1)}, bf16[2,192,384]{2,1,0:T(8,128)(2,1)S(1)}, u32[]{:S(2)}, u32[]{:S(2)}) %collective-permute-start) | collective-permute-done | bytes 294944 | tf_op jit(solution)/shard_map/while/body/eval_jaxpr/ppermute | solution.py:13
  592.3 8.7 %collective-permute-done = bf16[2,192,384]{2,1,0:T(8,128)(2,1)S(1)} collective-permute-done((bf16[2,192,384]{2,1,0:T(8,128)(2,1)S(1)}, bf16[2,192,384]{2,1,0:T(8,128)(2,1)S(1)}, u32[]{:S(2)}, u32[]{:S(2)}) %collective-permute-start) | collective-permute-done | bytes 294944 | tf_op jit(solution)/shard_map/while/body/eval_jaxpr/ppermute | solution.py:13
  601.9 8.7 %collective-permute-done = bf16[2,192,384]{2,1,0:T(8,128)(2,1)S(1)} collective-permute-done((bf16[2,192,384]{2,1,0:T(8,128)(2,1)S(1)}, bf16[2,192,384]{2,1,0:T(8,128)(2,1)S(1)}, u32[]{:S(2)}, u32[]{:S(2)}) %collective-permute-start) | collective-permute-done | bytes 294944 | tf_op jit(solution)/shard_map/while/body/eval_jaxpr/ppermute | solution.py:13
  611.5 8.7 %collective-permute-done = bf16[2,192,384]{2,1,0:T(8,128)(2,1)S(1)} collective-permute-done((bf16[2,192,384]{2,1,0:T(8,128)(2,1)S(1)}, bf16[2,192,384]{2,1,0:T(8,128)(2,1)S(1)}, u32[]{:S(2)}, u32[]{:S(2)}) %collective-permute-start) | collective-permute-done | bytes 294944 | tf_op jit(solution)/shard_map/while/body/eval_jaxpr/ppermute | solution.py:13
  621.1 8.7 %collective-permute-done = bf16[2,192,384]{2,1,0:T(8,128)(2,1)S(1)} collective-permute-done((bf16[2,192,384]{2,1,0:T(8,128)(2,1)S(1)}, bf16[2,192,384]{2,1,0:T(8,128)(2,1)S(1)}, u32[]{:S(2)}, u32[]{:S(2)}) %collective-permute-start) | collective-permute-done | bytes 294944 | tf_op jit(solution)/shard_map/while/body/eval_jaxpr/ppermute | solution.py:13
  630.7 8.7 %collective-permute-done = bf16[2,192,384]{2,1,0:T(8,128)(2,1)S(1)} collective-permute-done((bf16[2,192,384]{2,1,0:T(8,128)(2,1)S(1)}, bf16[2,192,384]{2,1,0:T(8,128)(2,1)S(1)}, u32[]{:S(2)}, u32[]{:S(2)}) %collective-permute-start) | collective-permute-done | bytes 294944 | tf_op jit(solution)/shard_map/while/body/eval_jaxpr/ppermute | solution.py:13
  640.3 8.7 %collective-permute-done = bf16[2,192,384]{2,1,0:T(8,128)(2,1)S(1)} collective-permute-done((bf16[2,192,384]{2,1,0:T(8,128)(2,1)S(1)}, bf16[2,192,384]{2,1,0:T(8,128)(2,1)S(1)}, u32[]{:S(2)}, u32[]{:S(2)}) %collective-permute-start) | collective-permute-done | bytes 294944 | tf_op jit(solution)/shard_map/while/body/eval_jaxpr/ppermute | solution.py:13
  649.9 8.7 %collective-permute-done = bf16[2,192,384]{2,1,0:T(8,128)(2,1)S(1)} collective-permute-done((bf16[2,192,384]{2,1,0:T(8,128)(2,1)S(1)}, bf16[2,192,384]{2,1,0:T(8,128)(2,1)S(1)}, u32[]{:S(2)}, u32[]{:S(2)}) %collective-permute-start) | collective-permute-done | bytes 294944 | tf_op jit(solution)/shard_map/while/body/eval_jaxpr/ppermute | solution.py:13
  662.2 53.9 %reduce-scatter.4.cloned.1.call-done = bf16[384,192]{1,0:T(8,128)(2,1)} async-done(((bf16[1536,192]{1,0:T(8,128)(2,1)}), bf16[384,192]{1,0:T(8,128)(2,1)}) %reduce-scatter.4.cloned.1.call-update) | async-done | bytes 147472
  (732 shorter events, 274.3 us)
Async XLA Ops:
  6.5 709.6 %reduce-scatter.4.cloned.1.call-start = ((), (), s32[]{:S(2)}) async-start(), calls=%async_computation.1 | async-start | bytes 983040
  104.2 8.3 %collective-permute-start = (bf16[2,192,384]{2,1,0:T(8,128)(2,1)S(1)}, bf16[2,192,384]{2,1,0:T(8,128)(2,1)S(1)}, u32[]{:S(2)}, u32[]{:S(2)}) collective-permute-start(bf16[2,192,384]{2,1,0:T(8,128)(2,1)S(1)} %get-tuple-element.446), channel_id=1, source_target_pairs={{252,0},{0,4},{4,8},{8,12},{12,16},{16,20},{20,24},{24,28},{28,32}... | collective-permute-start | bytes 884744 | tf_op jit(solution)/shard_map/while/body/eval_jaxpr/ppermute | solution.py:13
  113.5 8.3 %collective-permute-start = (bf16[2,192,384]{2,1,0:T(8,128)(2,1)S(1)}, bf16[2,192,384]{2,1,0:T(8,128)(2,1)S(1)}, u32[]{:S(2)}, u32[]{:S(2)}) collective-permute-start(bf16[2,192,384]{2,1,0:T(8,128)(2,1)S(1)} %get-tuple-element.446), channel_id=1, source_target_pairs={{252,0},{0,4},{4,8},{8,12},{12,16},{16,20},{20,24},{24,28},{28,32}... | collective-permute-start | bytes 884744 | tf_op jit(solution)/shard_map/while/body/eval_jaxpr/ppermute | solution.py:13
  132.2 8.3 %collective-permute-start = (bf16[2,192,384]{2,1,0:T(8,128)(2,1)S(1)}, bf16[2,192,384]{2,1,0:T(8,128)(2,1)S(1)}, u32[]{:S(2)}, u32[]{:S(2)}) collective-permute-start(bf16[2,192,384]{2,1,0:T(8,128)(2,1)S(1)} %get-tuple-element.446), channel_id=1, source_target_pairs={{252,0},{0,4},{4,8},{8,12},{12,16},{16,20},{20,24},{24,28},{28,32}... | collective-permute-start | bytes 884744 | tf_op jit(solution)/shard_map/while/body/eval_jaxpr/ppermute | solution.py:13
  141.5 8.3 %collective-permute-start = (bf16[2,192,384]{2,1,0:T(8,128)(2,1)S(1)}, bf16[2,192,384]{2,1,0:T(8,128)(2,1)S(1)}, u32[]{:S(2)}, u32[]{:S(2)}) collective-permute-start(bf16[2,192,384]{2,1,0:T(8,128)(2,1)S(1)} %get-tuple-element.446), channel_id=1, source_target_pairs={{252,0},{0,4},{4,8},{8,12},{12,16},{16,20},{20,24},{24,28},{28,32}... | collective-permute-start | bytes 884744 | tf_op jit(solution)/shard_map/while/body/eval_jaxpr/ppermute | solution.py:13
  160.2 8.3 %collective-permute-start = (bf16[2,192,384]{2,1,0:T(8,128)(2,1)S(1)}, bf16[2,192,384]{2,1,0:T(8,128)(2,1)S(1)}, u32[]{:S(2)}, u32[]{:S(2)}) collective-permute-start(bf16[2,192,384]{2,1,0:T(8,128)(2,1)S(1)} %get-tuple-element.446), channel_id=1, source_target_pairs={{252,0},{0,4},{4,8},{8,12},{12,16},{16,20},{20,24},{24,28},{28,32}... | collective-permute-start | bytes 884744 | tf_op jit(solution)/shard_map/while/body/eval_jaxpr/ppermute | solution.py:13
  169.5 8.3 %collective-permute-start = (bf16[2,192,384]{2,1,0:T(8,128)(2,1)S(1)}, bf16[2,192,384]{2,1,0:T(8,128)(2,1)S(1)}, u32[]{:S(2)}, u32[]{:S(2)}) collective-permute-start(bf16[2,192,384]{2,1,0:T(8,128)(2,1)S(1)} %get-tuple-element.446), channel_id=1, source_target_pairs={{252,0},{0,4},{4,8},{8,12},{12,16},{16,20},{20,24},{24,28},{28,32}... | collective-permute-start | bytes 884744 | tf_op jit(solution)/shard_map/while/body/eval_jaxpr/ppermute | solution.py:13
  188.2 8.3 %collective-permute-start = (bf16[2,192,384]{2,1,0:T(8,128)(2,1)S(1)}, bf16[2,192,384]{2,1,0:T(8,128)(2,1)S(1)}, u32[]{:S(2)}, u32[]{:S(2)}) collective-permute-start(bf16[2,192,384]{2,1,0:T(8,128)(2,1)S(1)} %get-tuple-element.446), channel_id=1, source_target_pairs={{252,0},{0,4},{4,8},{8,12},{12,16},{16,20},{20,24},{24,28},{28,32}... | collective-permute-start | bytes 884744 | tf_op jit(solution)/shard_map/while/body/eval_jaxpr/ppermute | solution.py:13
  216.2 8.3 %collective-permute-start = (bf16[2,192,384]{2,1,0:T(8,128)(2,1)S(1)}, bf16[2,192,384]{2,1,0:T(8,128)(2,1)S(1)}, u32[]{:S(2)}, u32[]{:S(2)}) collective-permute-start(bf16[2,192,384]{2,1,0:T(8,128)(2,1)S(1)} %get-tuple-element.446), channel_id=1, source_target_pairs={{252,0},{0,4},{4,8},{8,12},{12,16},{16,20},{20,24},{24,28},{28,32}... | collective-permute-start | bytes 884744 | tf_op jit(solution)/shard_map/while/body/eval_jaxpr/ppermute | solution.py:13
  244.2 8.3 %collective-permute-start = (bf16[2,192,384]{2,1,0:T(8,128)(2,1)S(1)}, bf16[2,192,384]{2,1,0:T(8,128)(2,1)S(1)}, u32[]{:S(2)}, u32[]{:S(2)}) collective-permute-start(bf16[2,192,384]{2,1,0:T(8,128)(2,1)S(1)} %get-tuple-element.446), channel_id=1, source_target_pairs={{252,0},{0,4},{4,8},{8,12},{12,16},{16,20},{20,24},{24,28},{28,32}... | collective-permute-start | bytes 884744 | tf_op jit(solution)/shard_map/while/body/eval_jaxpr/ppermute | solution.py:13
  253.6 8.9 %collective-permute-start = (bf16[2,192,384]{2,1,0:T(8,128)(2,1)S(1)}, bf16[2,192,384]{2,1,0:T(8,128)(2,1)S(1)}, u32[]{:S(2)}, u32[]{:S(2)}) collective-permute-start(bf16[2,192,384]{2,1,0:T(8,128)(2,1)S(1)} %get-tuple-element.446), channel_id=1, source_target_pairs={{252,0},{0,4},{4,8},{8,12},{12,16},{16,20},{20,24},{24,28},{28,32}... | collective-permute-start | bytes 884744 | tf_op jit(solution)/shard_map/while/body/eval_jaxpr/ppermute | solution.py:13
  263.5 9.5 %collective-permute-start = (bf16[2,192,384]{2,1,0:T(8,128)(2,1)S(1)}, bf16[2,192,384]{2,1,0:T(8,128)(2,1)S(1)}, u32[]{:S(2)}, u32[]{:S(2)}) collective-permute-start(bf16[2,192,384]{2,1,0:T(8,128)(2,1)S(1)} %get-tuple-element.446), channel_id=1, source_target_pairs={{252,0},{0,4},{4,8},{8,12},{12,16},{16,20},{20,24},{24,28},{28,32}... | collective-permute-start | bytes 884744 | tf_op jit(solution)/shard_map/while/body/eval_jaxpr/ppermute | solution.py:13
  274.0 9.5 %collective-permute-start = (bf16[2,192,384]{2,1,0:T(8,128)(2,1)S(1)}, bf16[2,192,384]{2,1,0:T(8,128)(2,1)S(1)}, u32[]{:S(2)}, u32[]{:S(2)}) collective-permute-start(bf16[2,192,384]{2,1,0:T(8,128)(2,1)S(1)} %get-tuple-element.446), channel_id=1, source_target_pairs={{252,0},{0,4},{4,8},{8,12},{12,16},{16,20},{20,24},{24,28},{28,32}... | collective-permute-start | bytes 884744 | tf_op jit(solution)/shard_map/while/body/eval_jaxpr/ppermute | solution.py:13
  284.6 9.5 %collective-permute-start = (bf16[2,192,384]{2,1,0:T(8,128)(2,1)S(1)}, bf16[2,192,384]{2,1,0:T(8,128)(2,1)S(1)}, u32[]{:S(2)}, u32[]{:S(2)}) collective-permute-start(bf16[2,192,384]{2,1,0:T(8,128)(2,1)S(1)} %get-tuple-element.446), channel_id=1, source_target_pairs={{252,0},{0,4},{4,8},{8,12},{12,16},{16,20},{20,24},{24,28},{28,32}... | collective-permute-start | bytes 884744 | tf_op jit(solution)/shard_map/while/body/eval_jaxpr/ppermute | solution.py:13
  295.1 9.5 %collective-permute-start = (bf16[2,192,384]{2,1,0:T(8,128)(2,1)S(1)}, bf16[2,192,384]{2,1,0:T(8,128)(2,1)S(1)}, u32[]{:S(2)}, u32[]{:S(2)}) collective-permute-start(bf16[2,192,384]{2,1,0:T(8,128)(2,1)S(1)} %get-tuple-element.446), channel_id=1, source_target_pairs={{252,0},{0,4},{4,8},{8,12},{12,16},{16,20},{20,24},{24,28},{28,32}... | collective-permute-start | bytes 884744 | tf_op jit(solution)/shard_map/while/body/eval_jaxpr/ppermute | solution.py:13
  305.7 9.5 %collective-permute-start = (bf16[2,192,384]{2,1,0:T(8,128)(2,1)S(1)}, bf16[2,192,384]{2,1,0:T(8,128)(2,1)S(1)}, u32[]{:S(2)}, u32[]{:S(2)}) collective-permute-start(bf16[2,192,384]{2,1,0:T(8,128)(2,1)S(1)} %get-tuple-element.446), channel_id=1, source_target_pairs={{252,0},{0,4},{4,8},{8,12},{12,16},{16,20},{20,24},{24,28},{28,32}... | collective-permute-start | bytes 884744 | tf_op jit(solution)/shard_map/while/body/eval_jaxpr/ppermute | solution.py:13
  316.2 9.5 %collective-permute-start = (bf16[2,192,384]{2,1,0:T(8,128)(2,1)S(1)}, bf16[2,192,384]{2,1,0:T(8,128)(2,1)S(1)}, u32[]{:S(2)}, u32[]{:S(2)}) collective-permute-start(bf16[2,192,384]{2,1,0:T(8,128)(2,1)S(1)} %get-tuple-element.446), channel_id=1, source_target_pairs={{252,0},{0,4},{4,8},{8,12},{12,16},{16,20},{20,24},{24,28},{28,32}... | collective-permute-start | bytes 884744 | tf_op jit(solution)/shard_map/while/body/eval_jaxpr/ppermute | solution.py:13
  326.8 9.5 %collective-permute-start = (bf16[2,192,384]{2,1,0:T(8,128)(2,1)S(1)}, bf16[2,192,384]{2,1,0:T(8,128)(2,1)S(1)}, u32[]{:S(2)}, u32[]{:S(2)}) collective-permute-start(bf16[2,192,384]{2,1,0:T(8,128)(2,1)S(1)} %get-tuple-element.446), channel_id=1, source_target_pairs={{252,0},{0,4},{4,8},{8,12},{12,16},{16,20},{20,24},{24,28},{28,32}... | collective-permute-start | bytes 884744 | tf_op jit(solution)/shard_map/while/body/eval_jaxpr/ppermute | solution.py:13
  337.3 9.5 %collective-permute-start = (bf16[2,192,384]{2,1,0:T(8,128)(2,1)S(1)}, bf16[2,192,384]{2,1,0:T(8,128)(2,1)S(1)}, u32[]{:S(2)}, u32[]{:S(2)}) collective-permute-start(bf16[2,192,384]{2,1,0:T(8,128)(2,1)S(1)} %get-tuple-element.446), channel_id=1, source_target_pairs={{252,0},{0,4},{4,8},{8,12},{12,16},{16,20},{20,24},{24,28},{28,32}... | collective-permute-start | bytes 884744 | tf_op jit(solution)/shard_map/while/body/eval_jaxpr/ppermute | solution.py:13
  347.9 9.5 %collective-permute-start = (bf16[2,192,384]{2,1,0:T(8,128)(2,1)S(1)}, bf16[2,192,384]{2,1,0:T(8,128)(2,1)S(1)}, u32[]{:S(2)}, u32[]{:S(2)}) collective-permute-start(bf16[2,192,384]{2,1,0:T(8,128)(2,1)S(1)} %get-tuple-element.446), channel_id=1, source_target_pairs={{252,0},{0,4},{4,8},{8,12},{12,16},{16,20},{20,24},{24,28},{28,32}... | collective-permute-start | bytes 884744 | tf_op jit(solution)/shard_map/while/body/eval_jaxpr/ppermute | solution.py:13
  358.4 9.5 %collective-permute-start = (bf16[2,192,384]{2,1,0:T(8,128)(2,1)S(1)}, bf16[2,192,384]{2,1,0:T(8,128)(2,1)S(1)}, u32[]{:S(2)}, u32[]{:S(2)}) collective-permute-start(bf16[2,192,384]{2,1,0:T(8,128)(2,1)S(1)} %get-tuple-element.446), channel_id=1, source_target_pairs={{252,0},{0,4},{4,8},{8,12},{12,16},{16,20},{20,24},{24,28},{28,32}... | collective-permute-start | bytes 884744 | tf_op jit(solution)/shard_map/while/body/eval_jaxpr/ppermute | solution.py:13
  369.0 9.5 %collective-permute-start = (bf16[2,192,384]{2,1,0:T(8,128)(2,1)S(1)}, bf16[2,192,384]{2,1,0:T(8,128)(2,1)S(1)}, u32[]{:S(2)}, u32[]{:S(2)}) collective-permute-start(bf16[2,192,384]{2,1,0:T(8,128)(2,1)S(1)} %get-tuple-element.446), channel_id=1, source_target_pairs={{252,0},{0,4},{4,8},{8,12},{12,16},{16,20},{20,24},{24,28},{28,32}... | collective-permute-start | bytes 884744 | tf_op jit(solution)/shard_map/while/body/eval_jaxpr/ppermute | solution.py:13
  379.5 9.5 %collective-permute-start = (bf16[2,192,384]{2,1,0:T(8,128)(2,1)S(1)}, bf16[2,192,384]{2,1,0:T(8,128)(2,1)S(1)}, u32[]{:S(2)}, u32[]{:S(2)}) collective-permute-start(bf16[2,192,384]{2,1,0:T(8,128)(2,1)S(1)} %get-tuple-element.446), channel_id=1, source_target_pairs={{252,0},{0,4},{4,8},{8,12},{12,16},{16,20},{20,24},{24,28},{28,32}... | collective-permute-start | bytes 884744 | tf_op jit(solution)/shard_map/while/body/eval_jaxpr/ppermute | solution.py:13
  390.1 9.5 %collective-permute-start = (bf16[2,192,384]{2,1,0:T(8,128)(2,1)S(1)}, bf16[2,192,384]{2,1,0:T(8,128)(2,1)S(1)}, u32[]{:S(2)}, u32[]{:S(2)}) collective-permute-start(bf16[2,192,384]{2,1,0:T(8,128)(2,1)S(1)} %get-tuple-element.446), channel_id=1, source_target_pairs={{252,0},{0,4},{4,8},{8,12},{12,16},{16,20},{20,24},{24,28},{28,32}... | collective-permute-start | bytes 884744 | tf_op jit(solution)/shard_map/while/body/eval_jaxpr/ppermute | solution.py:13
  400.6 9.5 %collective-permute-start = (bf16[2,192,384]{2,1,0:T(8,128)(2,1)S(1)}, bf16[2,192,384]{2,1,0:T(8,128)(2,1)S(1)}, u32[]{:S(2)}, u32[]{:S(2)}) collective-permute-start(bf16[2,192,384]{2,1,0:T(8,128)(2,1)S(1)} %get-tuple-element.446), channel_id=1, source_target_pairs={{252,0},{0,4},{4,8},{8,12},{12,16},{16,20},{20,24},{24,28},{28,32}... | collective-permute-start | bytes 884744 | tf_op jit(solution)/shard_map/while/body/eval_jaxpr/ppermute | solution.py:13
  411.2 9.5 %collective-permute-start = (bf16[2,192,384]{2,1,0:T(8,128)(2,1)S(1)}, bf16[2,192,384]{2,1,0:T(8,128)(2,1)S(1)}, u32[]{:S(2)}, u32[]{:S(2)}) collective-permute-start(bf16[2,192,384]{2,1,0:T(8,128)(2,1)S(1)} %get-tuple-element.446), channel_id=1, source_target_pairs={{252,0},{0,4},{4,8},{8,12},{12,16},{16,20},{20,24},{24,28},{28,32}... | collective-permute-start | bytes 884744 | tf_op jit(solution)/shard_map/while/body/eval_jaxpr/ppermute | solution.py:13
  421.7 9.5 %collective-permute-start = (bf16[2,192,384]{2,1,0:T(8,128)(2,1)S(1)}, bf16[2,192,384]{2,1,0:T(8,128)(2,1)S(1)}, u32[]{:S(2)}, u32[]{:S(2)}) collective-permute-start(bf16[2,192,384]{2,1,0:T(8,128)(2,1)S(1)} %get-tuple-element.446), channel_id=1, source_target_pairs={{252,0},{0,4},{4,8},{8,12},{12,16},{16,20},{20,24},{24,28},{28,32}... | collective-permute-start | bytes 884744 | tf_op jit(solution)/shard_map/while/body/eval_jaxpr/ppermute | solution.py:13
  432.3 9.5 %collective-permute-start = (bf16[2,192,384]{2,1,0:T(8,128)(2,1)S(1)}, bf16[2,192,384]{2,1,0:T(8,128)(2,1)S(1)}, u32[]{:S(2)}, u32[]{:S(2)}) collective-permute-start(bf16[2,192,384]{2,1,0:T(8,128)(2,1)S(1)} %get-tuple-element.446), channel_id=1, source_target_pairs={{252,0},{0,4},{4,8},{8,12},{12,16},{16,20},{20,24},{24,28},{28,32}... | collective-permute-start | bytes 884744 | tf_op jit(solution)/shard_map/while/body/eval_jaxpr/ppermute | solution.py:13
  442.8 9.5 %collective-permute-start = (bf16[2,192,384]{2,1,0:T(8,128)(2,1)S(1)}, bf16[2,192,384]{2,1,0:T(8,128)(2,1)S(1)}, u32[]{:S(2)}, u32[]{:S(2)}) collective-permute-start(bf16[2,192,384]{2,1,0:T(8,128)(2,1)S(1)} %get-tuple-element.446), channel_id=1, source_target_pairs={{252,0},{0,4},{4,8},{8,12},{12,16},{16,20},{20,24},{24,28},{28,32}... | collective-permute-start | bytes 884744 | tf_op jit(solution)/shard_map/while/body/eval_jaxpr/ppermute | solution.py:13
  453.3 9.5 %collective-permute-start = (bf16[2,192,384]{2,1,0:T(8,128)(2,1)S(1)}, bf16[2,192,384]{2,1,0:T(8,128)(2,1)S(1)}, u32[]{:S(2)}, u32[]{:S(2)}) collective-permute-start(bf16[2,192,384]{2,1,0:T(8,128)(2,1)S(1)} %get-tuple-element.446), channel_id=1, source_target_pairs={{252,0},{0,4},{4,8},{8,12},{12,16},{16,20},{20,24},{24,28},{28,32}... | collective-permute-start | bytes 884744 | tf_op jit(solution)/shard_map/while/body/eval_jaxpr/ppermute | solution.py:13
  463.9 9.5 %collective-permute-start = (bf16[2,192,384]{2,1,0:T(8,128)(2,1)S(1)}, bf16[2,192,384]{2,1,0:T(8,128)(2,1)S(1)}, u32[]{:S(2)}, u32[]{:S(2)}) collective-permute-start(bf16[2,192,384]{2,1,0:T(8,128)(2,1)S(1)} %get-tuple-element.446), channel_id=1, source_target_pairs={{252,0},{0,4},{4,8},{8,12},{12,16},{16,20},{20,24},{24,28},{28,32}... | collective-permute-start | bytes 884744 | tf_op jit(solution)/shard_map/while/body/eval_jaxpr/ppermute | solution.py:13
  474.4 9.5 %collective-permute-start = (bf16[2,192,384]{2,1,0:T(8,128)(2,1)S(1)}, bf16[2,192,384]{2,1,0:T(8,128)(2,1)S(1)}, u32[]{:S(2)}, u32[]{:S(2)}) collective-permute-start(bf16[2,192,384]{2,1,0:T(8,128)(2,1)S(1)} %get-tuple-element.446), channel_id=1, source_target_pairs={{252,0},{0,4},{4,8},{8,12},{12,16},{16,20},{20,24},{24,28},{28,32}... | collective-permute-start | bytes 884744 | tf_op jit(solution)/shard_map/while/body/eval_jaxpr/ppermute | solution.py:13
  485.0 9.5 %collective-permute-start = (bf16[2,192,384]{2,1,0:T(8,128)(2,1)S(1)}, bf16[2,192,384]{2,1,0:T(8,128)(2,1)S(1)}, u32[]{:S(2)}, u32[]{:S(2)}) collective-permute-start(bf16[2,192,384]{2,1,0:T(8,128)(2,1)S(1)} %get-tuple-element.446), channel_id=1, source_target_pairs={{252,0},{0,4},{4,8},{8,12},{12,16},{16,20},{20,24},{24,28},{28,32}... | collective-permute-start | bytes 884744 | tf_op jit(solution)/shard_map/while/body/eval_jaxpr/ppermute | solution.py:13
  495.5 9.5 %collective-permute-start = (bf16[2,192,384]{2,1,0:T(8,128)(2,1)S(1)}, bf16[2,192,384]{2,1,0:T(8,128)(2,1)S(1)}, u32[]{:S(2)}, u32[]{:S(2)}) collective-permute-start(bf16[2,192,384]{2,1,0:T(8,128)(2,1)S(1)} %get-tuple-element.446), channel_id=1, source_target_pairs={{252,0},{0,4},{4,8},{8,12},{12,16},{16,20},{20,24},{24,28},{28,32}... | collective-permute-start | bytes 884744 | tf_op jit(solution)/shard_map/while/body/eval_jaxpr/ppermute | solution.py:13
  506.1 9.5 %collective-permute-start = (bf16[2,192,384]{2,1,0:T(8,128)(2,1)S(1)}, bf16[2,192,384]{2,1,0:T(8,128)(2,1)S(1)}, u32[]{:S(2)}, u32[]{:S(2)}) collective-permute-start(bf16[2,192,384]{2,1,0:T(8,128)(2,1)S(1)} %get-tuple-element.446), channel_id=1, source_target_pairs={{252,0},{0,4},{4,8},{8,12},{12,16},{16,20},{20,24},{24,28},{28,32}... | collective-permute-start | bytes 884744 | tf_op jit(solution)/shard_map/while/body/eval_jaxpr/ppermute | solution.py:13
  516.6 9.5 %collective-permute-start = (bf16[2,192,384]{2,1,0:T(8,128)(2,1)S(1)}, bf16[2,192,384]{2,1,0:T(8,128)(2,1)S(1)}, u32[]{:S(2)}, u32[]{:S(2)}) collective-permute-start(bf16[2,192,384]{2,1,0:T(8,128)(2,1)S(1)} %get-tuple-element.446), channel_id=1, source_target_pairs={{252,0},{0,4},{4,8},{8,12},{12,16},{16,20},{20,24},{24,28},{28,32}... | collective-permute-start | bytes 884744 | tf_op jit(solution)/shard_map/while/body/eval_jaxpr/ppermute | solution.py:13
  527.2 9.5 %collective-permute-start = (bf16[2,192,384]{2,1,0:T(8,128)(2,1)S(1)}, bf16[2,192,384]{2,1,0:T(8,128)(2,1)S(1)}, u32[]{:S(2)}, u32[]{:S(2)}) collective-permute-start(bf16[2,192,384]{2,1,0:T(8,128)(2,1)S(1)} %get-tuple-element.446), channel_id=1, source_target_pairs={{252,0},{0,4},{4,8},{8,12},{12,16},{16,20},{20,24},{24,28},{28,32}... | collective-permute-start | bytes 884744 | tf_op jit(solution)/shard_map/while/body/eval_jaxpr/ppermute | solution.py:13
  537.7 9.5 %collective-permute-start = (bf16[2,192,384]{2,1,0:T(8,128)(2,1)S(1)}, bf16[2,192,384]{2,1,0:T(8,128)(2,1)S(1)}, u32[]{:S(2)}, u32[]{:S(2)}) collective-permute-start(bf16[2,192,384]{2,1,0:T(8,128)(2,1)S(1)} %get-tuple-element.446), channel_id=1, source_target_pairs={{252,0},{0,4},{4,8},{8,12},{12,16},{16,20},{20,24},{24,28},{28,32}... | collective-permute-start | bytes 884744 | tf_op jit(solution)/shard_map/while/body/eval_jaxpr/ppermute | solution.py:13
  548.3 9.5 %collective-permute-start = (bf16[2,192,384]{2,1,0:T(8,128)(2,1)S(1)}, bf16[2,192,384]{2,1,0:T(8,128)(2,1)S(1)}, u32[]{:S(2)}, u32[]{:S(2)}) collective-permute-start(bf16[2,192,384]{2,1,0:T(8,128)(2,1)S(1)} %get-tuple-element.446), channel_id=1, source_target_pairs={{252,0},{0,4},{4,8},{8,12},{12,16},{16,20},{20,24},{24,28},{28,32}... | collective-permute-start | bytes 884744 | tf_op jit(solution)/shard_map/while/body/eval_jaxpr/ppermute | solution.py:13
  572.3 9.5 %collective-permute-start = (bf16[2,192,384]{2,1,0:T(8,128)(2,1)S(1)}, bf16[2,192,384]{2,1,0:T(8,128)(2,1)S(1)}, u32[]{:S(2)}, u32[]{:S(2)}) collective-permute-start(bf16[2,192,384]{2,1,0:T(8,128)(2,1)S(1)} %get-tuple-element.446), channel_id=1, source_target_pairs={{252,0},{0,4},{4,8},{8,12},{12,16},{16,20},{20,24},{24,28},{28,32}... | collective-permute-start | bytes 884744 | tf_op jit(solution)/shard_map/while/body/eval_jaxpr/ppermute | solution.py:13
  581.9 9.5 %collective-permute-start = (bf16[2,192,384]{2,1,0:T(8,128)(2,1)S(1)}, bf16[2,192,384]{2,1,0:T(8,128)(2,1)S(1)}, u32[]{:S(2)}, u32[]{:S(2)}) collective-permute-start(bf16[2,192,384]{2,1,0:T(8,128)(2,1)S(1)} %get-tuple-element.446), channel_id=1, source_target_pairs={{252,0},{0,4},{4,8},{8,12},{12,16},{16,20},{20,24},{24,28},{28,32}... | collective-permute-start | bytes 884744 | tf_op jit(solution)/shard_map/while/body/eval_jaxpr/ppermute | solution.py:13
  591.5 9.5 %collective-permute-start = (bf16[2,192,384]{2,1,0:T(8,128)(2,1)S(1)}, bf16[2,192,384]{2,1,0:T(8,128)(2,1)S(1)}, u32[]{:S(2)}, u32[]{:S(2)}) collective-permute-start(bf16[2,192,384]{2,1,0:T(8,128)(2,1)S(1)} %get-tuple-element.446), channel_id=1, source_target_pairs={{252,0},{0,4},{4,8},{8,12},{12,16},{16,20},{20,24},{24,28},{28,32}... | collective-permute-start | bytes 884744 | tf_op jit(solution)/shard_map/while/body/eval_jaxpr/ppermute | solution.py:13
  601.1 9.5 %collective-permute-start = (bf16[2,192,384]{2,1,0:T(8,128)(2,1)S(1)}, bf16[2,192,384]{2,1,0:T(8,128)(2,1)S(1)}, u32[]{:S(2)}, u32[]{:S(2)}) collective-permute-start(bf16[2,192,384]{2,1,0:T(8,128)(2,1)S(1)} %get-tuple-element.446), channel_id=1, source_target_pairs={{252,0},{0,4},{4,8},{8,12},{12,16},{16,20},{20,24},{24,28},{28,32}... | collective-permute-start | bytes 884744 | tf_op jit(solution)/shard_map/while/body/eval_jaxpr/ppermute | solution.py:13
  610.7 9.5 %collective-permute-start = (bf16[2,192,384]{2,1,0:T(8,128)(2,1)S(1)}, bf16[2,192,384]{2,1,0:T(8,128)(2,1)S(1)}, u32[]{:S(2)}, u32[]{:S(2)}) collective-permute-start(bf16[2,192,384]{2,1,0:T(8,128)(2,1)S(1)} %get-tuple-element.446), channel_id=1, source_target_pairs={{252,0},{0,4},{4,8},{8,12},{12,16},{16,20},{20,24},{24,28},{28,32}... | collective-permute-start | bytes 884744 | tf_op jit(solution)/shard_map/while/body/eval_jaxpr/ppermute | solution.py:13
  620.3 9.5 %collective-permute-start = (bf16[2,192,384]{2,1,0:T(8,128)(2,1)S(1)}, bf16[2,192,384]{2,1,0:T(8,128)(2,1)S(1)}, u32[]{:S(2)}, u32[]{:S(2)}) collective-permute-start(bf16[2,192,384]{2,1,0:T(8,128)(2,1)S(1)} %get-tuple-element.446), channel_id=1, source_target_pairs={{252,0},{0,4},{4,8},{8,12},{12,16},{16,20},{20,24},{24,28},{28,32}... | collective-permute-start | bytes 884744 | tf_op jit(solution)/shard_map/while/body/eval_jaxpr/ppermute | solution.py:13
  629.9 9.5 %collective-permute-start = (bf16[2,192,384]{2,1,0:T(8,128)(2,1)S(1)}, bf16[2,192,384]{2,1,0:T(8,128)(2,1)S(1)}, u32[]{:S(2)}, u32[]{:S(2)}) collective-permute-start(bf16[2,192,384]{2,1,0:T(8,128)(2,1)S(1)} %get-tuple-element.446), channel_id=1, source_target_pairs={{252,0},{0,4},{4,8},{8,12},{12,16},{16,20},{20,24},{24,28},{28,32}... | collective-permute-start | bytes 884744 | tf_op jit(solution)/shard_map/while/body/eval_jaxpr/ppermute | solution.py:13
  639.5 9.5 %collective-permute-start = (bf16[2,192,384]{2,1,0:T(8,128)(2,1)S(1)}, bf16[2,192,384]{2,1,0:T(8,128)(2,1)S(1)}, u32[]{:S(2)}, u32[]{:S(2)}) collective-permute-start(bf16[2,192,384]{2,1,0:T(8,128)(2,1)S(1)} %get-tuple-element.446), channel_id=1, source_target_pairs={{252,0},{0,4},{4,8},{8,12},{12,16},{16,20},{20,24},{24,28},{28,32}... | collective-permute-start | bytes 884744 | tf_op jit(solution)/shard_map/while/body/eval_jaxpr/ppermute | solution.py:13
  649.1 9.5 %collective-permute-start = (bf16[2,192,384]{2,1,0:T(8,128)(2,1)S(1)}, bf16[2,192,384]{2,1,0:T(8,128)(2,1)S(1)}, u32[]{:S(2)}, u32[]{:S(2)}) collective-permute-start(bf16[2,192,384]{2,1,0:T(8,128)(2,1)S(1)} %get-tuple-element.446), channel_id=1, source_target_pairs={{252,0},{0,4},{4,8},{8,12},{12,16},{16,20},{20,24},{24,28},{28,32}... | collective-permute-start | bytes 884744 | tf_op jit(solution)/shard_map/while/body/eval_jaxpr/ppermute | solution.py:13
  (23 other events, 926.2 us)
Sparse Core Ops, SparseCore 0:
  661.5 54.5 reduce-scatter.3
where the time goes:
time: 740 us; the launch traced here: 732 us
  waiting for transfers between devices  404 us (55%)
  starting transfers between devices  171 us (23%)
  loops' own time  47.5 us (6%)
  matrix products  38.7 us (5%)
  blocking collectives  24.6 us (3%)
  local copies, waits for them, and re-layouts  20.1 us (3%)
  between operations  16.3 us (2%)
  other arithmetic  10.1 us (1%)
    ppermute x64, waiting for transfers between devices, passed_along(): return lax.ppermute(block, axis, route)  350 us
    ppermute x64, starting transfers between devices, passed_along(): return lax.ppermute(block, axis, route)  171 us
    unnamed x2, waiting for transfers between devices  53.9 us
    another operation x1, loops' own time, local(): stacked, carried = lax.fori_loop(1, slabs, pass_step, (stacked, carried))  45.7 us
    dot_general x54, matrix products, attend(): jnp.einsum('hqk,khd->hqd', exp_scores.astype(jnp.bfloat16), value_heads,...  19.6 us
    dot_general x54, matrix products, attend(): jnp.einsum('qhd,khd->hqk', queries, key_heads, preferred_element_type=jnp...  15.2 us
  transfers between devices with their start and end apart: 65, of which 65 were waited for; matrix products, arithmetic and copies ran while one was open for 0% of the time, Pallas kernels for 0%

commit v1 on v0

v1 whole, which is shorter than its diff:
```python
import functools

import jax
import jax.numpy as jnp
from jax import lax
from jax.experimental import pallas as pl
from jax.experimental.pallas import tpu as pltpu
from jax.sharding import PartitionSpec as P

D = 1536
DH = 128
LOG2E = 1.4426950408889634
LOW = -1e30
NY = 4
NZ = 8
TAIL = 16

VMEM = pl.BlockSpec(memory_space=pltpu.VMEM)
SMEM = pl.BlockSpec(memory_space=pltpu.SMEM)
PARAMS = pltpu.CompilerParams(vmem_limit_bytes=40 * 1024 * 1024)


def shift(block, axis, distance):
    n = lax.axis_size(axis)
    return lax.ppermute(block, axis, [((i - distance) % n, i) for i in range(n)])


def to_column(row, rows):
    pad = jnp.zeros((128 - row.shape[0], rows), row.dtype)
    return jnp.concatenate([row, pad], axis=0).T


def to_row(column):
    return column.T[0:8]


def lanes_of(columns, rows):
    lane = lax.broadcasted_iota(jnp.int32, (rows, 128), 1)
    out = jnp.zeros((rows, 128), jnp.float32)
    for j, column in enumerate(columns):
        out = jnp.where(lane == j, column, out)
    return out


def project_kernel(x_ref, own, one, two, three, scale_ref, shift_ref, w_ref, q_ref, k_ref, v_ref, sums_ref):
    x = x_ref[0]
    n = 4
    order = [lax.rem(x - j + n, n) for j in range(n)]
    width = own.shape[1]
    rows = own.shape[0]
    chunks = [r[...].astype(jnp.float32) for r in (own, one, two, three)]
    total = sum(jnp.sum(c, axis=1, keepdims=True) for c in chunks)
    mean = total / D
    centered = [c - mean for c in chunks]
    variance = sum(jnp.sum(c * c, axis=1, keepdims=True) for c in centered) / D
    inv = lax.rsqrt(variance + 1e-06)
    modded = []
    for j in range(n):
        sc = scale_ref[order[j]]
        sh = shift_ref[order[j]]
        modded.append((centered[j] * inv * (1.0 + sc) + sh).astype(jnp.bfloat16))
    outs = []
    for part in range(3):
        acc = None
        for j in range(n):
            start = pl.multiple_of(order[j] * width, 128)
            d = jnp.dot(modded[j], w_ref[part, pl.ds(start, width), :], preferred_element_type=jnp.float32)
            acc = d if acc is None else acc + d
        outs.append(acc)
    q_ref[...] = outs[0]
    k_ref[...] = outs[1]
    v_ref[...] = outs[2].astype(jnp.bfloat16)
    sums = [jnp.sum(o * o, axis=1, keepdims=True) for o in outs[:2]]
    sums_ref[...] = to_row(lanes_of(sums, rows))


def norm_kernel(q_ref, k_ref, v_ref, s0, s1, s2, s3, qg_ref, kg_ref, qn_ref, kv_ref):
    rows = q_ref.shape[0]
    total = s0[...] + s1[...] + s2[...] + s3[...]
    inv = to_column(lax.rsqrt(total / D + 1e-06), rows)
    qn_ref[...] = (q_ref[...] * inv[:, 0:1] * (qg_ref[...] * (LOG2E * DH ** (-0.5)))).astype(jnp.bfloat16)
    kv_ref[0] = (k_ref[...] * inv[:, 1:2] * kg_ref[...]).astype(jnp.bfloat16)
    kv_ref[1] = v_ref[...]


def attend_kernel(slabs, first, last, *refs):
    flags, qa, qb = refs[:3]
    at = 3
    keys, values = [], []
    for kind in slabs:
        if kind == 1:
            keys.append(refs[at].at[0])
            values.append(refs[at].at[1])
            at += 1
        else:
            keys.append(refs[at])
            values.append(refs[at + 1])
            at += 2
    if not first:
        acc_in, stat_in = refs[at], refs[at + 1]
        at += 2
    outs = refs[at:]
    rows = qa.shape[1]
    count = len(slabs)
    width = qa.shape[2]
    heads = width // DH
    col = lax.broadcasted_iota(jnp.int32, (1, rows * count), 1)
    ones = jnp.ones((rows * count, DH), jnp.bfloat16)

    def one_slab(q_ref, parity, k):
        bias = jnp.zeros((1, rows * count), jnp.float32)
        for j in range(count):
            inside = (col >= j * rows) & (col < (j + 1) * rows)
            bias = bias + jnp.where(inside, flags[k * count + j], 0.0)
        maxes, totals, accs = [], [], []
        stat = None if first else stat_in[parity * NY + k]
        for h in range(heads):
            lanes = slice(h * DH, (h + 1) * DH)
            q = q_ref[k, :, lanes]
            kk = jnp.concatenate([r[:, lanes] for r in keys], axis=0)
            vv = jnp.concatenate([r[:, lanes] for r in values], axis=0)
            s = lax.dot_general(q, kk, (((1,), (1,)), ((), ())), preferred_element_type=jnp.float32)
            s = s + bias
            top = jnp.max(s, axis=1, keepdims=True)
            if not first:
                old = stat[:, h : h + 1]
                top = jnp.maximum(top, old)
            e = jnp.exp2(s - top).astype(jnp.bfloat16)
            o = jnp.dot(e, jnp.concatenate([vv, ones], axis=1), preferred_element_type=jnp.float32)
            acc, tot = o[:, :DH], o[:, DH : DH + 1]
            if not first:
                fade = jnp.exp2(old - top)
                acc = acc + fade * acc_in[parity * NY + k, :, lanes]
                tot = tot + fade * stat[:, heads + h : heads + h + 1]
            maxes.append(top)
            totals.append(tot)
            accs.append(acc)
        if last:
            out = outs[parity]
            logs = []
            for h in range(heads):
                out[k, 0:rows, h * DH : (h + 1) * DH] = (accs[h] / totals[h]).astype(jnp.bfloat16)
                logs.append(maxes[h] + jnp.log2(totals[h]))
            out[k, rows : rows + TAIL, :] = pack_logs(to_row(lanes_of(logs, rows)), width)
        else:
            acc_out, stat_out = outs
            for h in range(heads):
                acc_out[parity * NY + k, :, h * DH : (h + 1) * DH] = accs[h]
            stat_out[parity * NY + k] = lanes_of(maxes + totals, rows)

    def step(k, carry):
        one_slab(qa, 0, k)
        one_slab(qb, 1, k)
        return carry

    lax.fori_loop(0, NY, step, 0)


def pack_logs(row, width):
    high = row.astype(jnp.bfloat16)
    low = (row - high.astype(jnp.float32)).astype(jnp.bfloat16)
    both = jnp.concatenate([high.astype(jnp.float32), low.astype(jnp.float32)], axis=0)
    pad = jnp.zeros((TAIL, width - row.shape[1]), jnp.float32)
    return jnp.concatenate([both, pad], axis=1).astype(jnp.bfloat16)


def merge(blocks, rows):
    logs = []
    for block in blocks:
        tail = block[rows : rows + TAIL, 0:rows].astype(jnp.float32)
        logs.append(tail[0:8] + tail[8:16])
    top = functools.reduce(jnp.maximum, logs)
    parts = [jnp.exp2(v - top) for v in logs]
    total = sum(parts)
    weights = [to_column(p / total, rows) for p in parts]
    heads = blocks[0].shape[1] // DH
    outs = []
    for h in range(heads):
        lanes = slice(h * DH, (h + 1) * DH)
        outs.append(
            sum(w[:, h : h + 1] * b[0:rows, lanes].astype(jnp.float32) for w, b in zip(weights, blocks, strict=True))
        )
    return outs, top + jnp.log2(total)


def pair_kernel(mine, other, out):
    rows = mine.shape[1] - TAIL
    for k in range(NY):
        outs, logs = merge([mine.at[k], other.at[k]], rows)
        for h, o in enumerate(outs):
            out[k, 0:rows, h * DH : (h + 1) * DH] = o.astype(jnp.bfloat16)
        out[k, rows : rows + TAIL, :] = pack_logs(logs, mine.shape[2])


def out_kernel(x_ref, a, b, c, d, w_ref, *outs):
    rows = a.shape[0] - TAIL
    width = a.shape[1]
    x = x_ref[0]
    parts, _ = merge([a, b, c, d], rows)
    attn = jnp.concatenate([p.astype(jnp.bfloat16) for p in parts], axis=1)
    n = len(outs)
    for j in range(n):
        start = pl.multiple_of(lax.rem(x + j, n) * width, 128)
        outs[j][...] = jnp.dot(attn, w_ref[:, pl.ds(start, width)], preferred_element_type=jnp.float32).astype(
            jnp.bfloat16
        )


def shape(dims, dtype):
    return jax.ShapeDtypeStruct(dims, dtype)


def call(kernel, ins, out_shape, flops, moved, exps=0):
    return pl.pallas_call(
        kernel,
        out_shape=out_shape,
        in_specs=ins,
        out_specs=jax.tree.map(lambda _: VMEM, out_shape),
        compiler_params=PARAMS,
        cost_estimate=pl.CostEstimate(flops=flops, bytes_accessed=moved, transcendentals=exps),
    )


def attend(flags, qa, qb, pieces, state, last):
    first = state is None
    slabs = tuple(1 if not isinstance(p, tuple) else 2 for p in pieces)
    flat = []
    for p in pieces:
        flat += list(p) if isinstance(p, tuple) else [p]
    slots, rows, width = qa.shape
    if last:
        out = [shape((slots, rows + TAIL, width), jnp.bfloat16)] * 2
    else:
        out = [shape((2 * slots, rows, width), jnp.float32), shape((2 * slots, rows, 128), jnp.float32)]
    scores = 2 * slots * rows * rows * len(slabs) * (width // DH)
    args = [flags, qa, qb, *flat] + ([] if first else list(state))
    return call(
        functools.partial(attend_kernel, slabs, first, last),
        [SMEM] + [VMEM] * (len(args) - 1),
        out,
        scores * DH * 4,
        4 << 20,
        scores,
    )(*args)


def local(latents, fresh_frame, noise_level, offset, mod_table, w_qkv, w_out, q_gain, k_gain):
    slabs = lax.axis_size("queue")
    frames = slabs // 2
    heads_ax = lax.axis_size("head")
    rows, width = latents.shape
    slab = lax.axis_index("queue")
    x = lax.axis_index("head")
    frame = slab // 2
    z, y = frame // NY, frame % NY
    x_arg = x.astype(jnp.int32).reshape(1)

    def place(f):
        return jnp.mod(f - offset[0], frames)

    chunks = [latents] + [shift(latents, "head", j) for j in range(1, heads_ax)]
    home_latents = shift(latents, "queue", -2)
    modulation = lax.dynamic_index_in_dim(mod_table, noise_level[place(frame)], 0, keepdims=False)
    home_level = noise_level[place(frame + 1)]
    gate = lax.dynamic_slice(mod_table, (home_level, 2, x * width), (1, 1, width)).reshape(1, width)
    modulation = modulation.reshape(3, heads_ax, 1, width)
    w3 = jnp.transpose(w_qkv, (1, 0, 2))
    q, k, v, sums = call(
        project_kernel,
        [SMEM] + [VMEM] * 7,
        [
            shape((rows, width), jnp.float32),
            shape((rows, width), jnp.float32),
            shape((rows, width), jnp.bfloat16),
            shape((8, rows), jnp.float32),
        ],
        2 * rows * D * 3 * width,
        6 << 20,
    )(x_arg, *chunks, modulation[1], modulation[0], w3)
    all_sums = [sums] + [shift(sums, "head", j) for j in range(1, heads_ax)]
    qn, kv = call(
        norm_kernel,
        [VMEM] * 9,
        [shape((rows, width), jnp.bfloat16), shape((2, rows, width), jnp.bfloat16)],
        rows * width * 8,
        2 << 20,
    )(q, k, v, *all_sums, q_gain.reshape(1, width), k_gain.reshape(1, width))

    def query_route(j):
        route = []
        for f in range(frames):
            fz, fy = f // NY, f % NY
            source = (fz * NY + (fy + j) % NY + 1) % frames
            route += [(2 * source + c, 2 * f + c) for c in range(2)]
        return route

    def key_route(distance):
        route = []
        for f in range(frames):
            fz, fy = f // NY, f % NY
            source = ((fz - distance) % NZ) * NY + fy
            route += [(2 * source + c, 2 * f + c) for c in range(2)]
        return route

    def y_route(distance):
        route = []
        for f in range(frames):
            fz, fy = f // NY, f % NY
            source = fz * NY + (fy - distance) % NY
            route += [(2 * source + c, 2 * f + c) for c in range(2)]
        return route

    swap = [(i, i ^ 1) for i in range(slabs)]

    def flags_of(distances):
        out = []
        for j in range(NY):
            q_place = place(z * NY + (y + j) % NY + 1)
            for d in distances:
                k_place = place(jnp.mod(z - d, NZ) * NY + y)
                out.append(jnp.where(k_place <= q_place, 0.0, LOW))
        return jnp.stack(out).astype(jnp.float32)

    up, down = kv, kv
    ups, downs = [kv], [kv]
    up = lax.ppermute(up, "queue", key_route(1))
    down = lax.ppermute(down, "queue", key_route(-1))
    qa = jnp.stack([lax.ppermute(qn, "queue", query_route(j)) for j in range(NY)])
    qb = lax.ppermute(qa, "queue", swap)
    ups.append(up)
    downs.append(down)
    for _ in range(2):
        ups.append(lax.ppermute(ups[-1], "queue", key_route(1)))
        downs.append(lax.ppermute(downs[-1], "queue", key_route(-1)))
    far_k = lax.ppermute(ups[3][0], "queue", key_route(1))
    far_v = lax.ppermute(downs[3][1], "queue", key_route(-1))

    state = attend(flags_of((0, 1, -1)), qa, qb, [kv, ups[1], downs[1]], None, False)
    state = attend(flags_of((2, -2)), qa, qb, [ups[2], downs[2]], state, False)
    state = attend(flags_of((3, -3)), qa, qb, [ups[3], downs[3]], state, False)
    mine, others = attend(flags_of((4,)), qa, qb, [(far_k, far_v)], state, True)

    received = lax.ppermute(others, "queue", swap)
    paired = call(
        pair_kernel, [VMEM] * 2, shape(mine.shape, jnp.bfloat16), mine.size * 4, mine.size * 6
    )(mine, received)
    parts = [paired[0]] + [lax.ppermute(paired[j], "queue", y_route(j)) for j in range(1, NY)]
    blocks = call(
        out_kernel,
        [SMEM] + [VMEM] * 5,
        [shape((rows, width), jnp.bfloat16)] * heads_ax,
        2 * rows * width * D,
        3 << 20,
    )(x_arg, *parts, w_out)
    proj = blocks[0].astype(jnp.float32)
    for j in range(1, heads_ax):
        proj = proj + shift(blocks[j], "head", j).astype(jnp.float32)
    updated = (home_latents.astype(jnp.float32) + gate * proj).astype(jnp.bfloat16)
    entry_slot = jnp.mod(offset[0] - 1, frames)
    fresh_half = lax.dynamic_slice_in_dim(fresh_frame, slab % 2 * rows, rows, 0)
    return jnp.where(frame == entry_slot, fresh_half, updated)


def solution(mesh):
    return jax.shard_map(
        local,
        mesh=mesh,
        in_specs=(
            P("queue", "head"),
            P(None, "head"),
            P(),
            P(),
            P(),
            P(None, None, "head"),
            P("head", None),
            P("head"),
            P("head"),
        ),
        out_specs=P("queue", "head"),
        check_vma=False,
    )
```

time: 740 us -> 129 us (0.17); the launches traced: 732 us -> 129 us
  waiting for transfers between devices: 404 us -> 27.1 us
  starting transfers between devices: 171 us -> 50.7 us
  loops' own time: 47.5 us -> 0 us
  Pallas kernels: 0 us -> 38.9 us
  matrix products: 38.7 us -> 0 us
  blocking collectives: 24.6 us -> 0 us
  local copies, waits for them, and re-layouts: 20.1 us -> 6.29 us
  between operations: 16.3 us -> 4.6 us
  other arithmetic: 10.1 us -> 0.97 us
    ppermute x64 -> x27, waiting for transfers between devices: 350 us -> 27.1 us  [the longest x3 10.2 us: local(): lax.ppermute(paired[j], 'queue', y_route(j))]
    ppermute x64 -> x27, starting transfers between devices: 171 us -> 50.7 us  [the longest x10 17.7 us: shift(): lax.ppermute(block, axis, [((i - distance) % n, i) for i in range(n)])]
    unnamed x2 -> x0, waiting for transfers between devices: 53.9 us -> none
    another operation x64 -> x0, loops' own time: 47.5 us -> none  [the longest x1 45.7 us: local(): stacked, carried = lax.fori_loop(1, slabs, pass_step, (stacked, carried))]
    pallas_call x0 -> x8, Pallas kernels: none -> 38.9 us  [the longest x4 35 us: attend(): call(functools.partial(attend_kernel, slabs, first, last), [SMEM] + [VMEM...]
    dot_general x110 -> x0, matrix products: 38.7 us -> none  [the longest x54 19.6 us: attend(): jnp.einsum('hqk,khd->hqd', exp_scores.astype(jnp.bfloat16), value_heads,...]
    all_gather x1 -> x0, blocking collectives: 13.7 us -> none  [local(): lax.all_gather(latents, 'head', axis=1, tiled=True).astype(jnp.float32)]
    psum x1 -> x0, blocking collectives: 10.9 us -> none  [local(): lax.psum((jnp.sum(query_raw * query_raw, axis=1), jnp.sum(key_raw * key_r...]
  transfers between devices with their start and end apart: 65 -> 27, of which waited for: 65 -> 14; matrix products, arithmetic and copies ran while one was open for 0% -> 3% of each run, Pallas kernels for 0% -> 19%
where the time goes in v1:
time: 129 us
  starting transfers between devices  50.7 us (39%)
  Pallas kernels  38.9 us (30%)
  waiting for transfers between devices  27.1 us (21%)
  local copies, waits for them, and re-layouts  6.29 us (5%)
  between operations  4.6 us (4%)
    pallas_call x4, Pallas kernels, attend(): call(functools.partial(attend_kernel, slabs, first, last), [SMEM] + [VMEM...  35 us
    ppermute x10, starting transfers between devices, shift(): lax.ppermute(block, axis, [((i - distance) % n, i) for i in range(n)])  17.7 us
    ppermute x3, waiting for transfers between devices, local(): lax.ppermute(paired[j], 'queue', y_route(j))  10.2 us
    ppermute x4, starting transfers between devices, local(): lax.ppermute(qn, 'queue', query_route(j))  9.9 us
    ppermute x2, starting transfers between devices, local(): downs.append(lax.ppermute(downs[-1], 'queue', key_route(-1)))  7.38 us
    ppermute x10, waiting for transfers between devices, shift(): lax.ppermute(block, axis, [((i - distance) % n, i) for i in range(n)])  6.27 us
    ppermute x1, starting transfers between devices, local(): down = lax.ppermute(down, 'queue', key_route(-1))  6.03 us
    ppermute x3, starting transfers between devices, local(): lax.ppermute(paired[j], 'queue', y_route(j))  5.96 us
  transfers between devices with their start and end apart: 27, of which 14 were waited for; matrix products, arithmetic and copies ran while one was open for 3% of the time, Pallas kernels for 19%

profile of v1, /device:TPU:24, one launch (start us, length us, event | category | flops | bytes accessed | tf_op | source)
XLA Modules:
  0.0 128.5 jit_solution(18375845097307437026)
XLA Ops:
  0.0 1.5 %collective-permute-start.1 = (bf16[192,384]{1,0:T(8,128)(2,1)}, bf16[192,384]{1,0:T(8,128)(2,1)S(1)}, u32[]{:S(2)}, u32[]{:S(2)}) collective-permute-start(bf16[192,384]{1,0:T(8,128)(2,1)} %own.1), channel_id=1, source_target_pairs={{3,0},{0,1},{1,2},{2,3},{7,4},{4,5},{5,6},{6,7},{11,8},{8,9},{9,10... | collective-permute-start | bytes 442376 | tf_op jit(solution)/shard_map/ppermute | solution.py:25
  1.5 2.7 %collective-permute-start.2 = (bf16[192,384]{1,0:T(8,128)(2,1)}, bf16[192,384]{1,0:T(8,128)(2,1)S(1)}, u32[]{:S(2)}, u32[]{:S(2)}) collective-permute-start(bf16[192,384]{1,0:T(8,128)(2,1)} %own.1), channel_id=1, source_target_pairs={{2,0},{3,1},{0,2},{1,3},{6,4},{7,5},{4,6},{5,7},{10,8},{11,9},{8,1... | collective-permute-start | bytes 442376 | tf_op jit(solution)/shard_map/ppermute | solution.py:25
  4.2 1.4 %collective-permute-start.3 = (bf16[192,384]{1,0:T(8,128)(2,1)}, bf16[192,384]{1,0:T(8,128)(2,1)S(1)}, u32[]{:S(2)}, u32[]{:S(2)}) collective-permute-start(bf16[192,384]{1,0:T(8,128)(2,1)} %own.1), channel_id=1, source_target_pairs={{1,0},{2,1},{3,2},{0,3},{5,4},{6,5},{7,6},{4,7},{9,8},{10,9},{11,1... | collective-permute-start | bytes 442376 | tf_op jit(solution)/shard_map/ppermute | solution.py:25
  6.4 1.4 %fusion.1 = (s32[1]{0:T(128)}, s32[1]{0:T(128)}) fusion(s32[32]{0:T(128)} %param.11, s32[]{:T(128)S(6)} %select_n.400, s32[]{:T(128)S(6)} %select_n.420), kind=kLoop, calls=%fused_computation.13 | loop fusion | bytes 24 | tf_op jit(solution)/shard_map/dynamic_slice | solution.py:264
  9.6 0.8 constant_dynamic-slice_fusion.1
  10.5 0.7 collective-permute-done.2.two
  11.2 2.0 %copy-done = bf16[1536,3,384]{2,0,1:T(8,128)(2,1)S(1)} copy-done((bf16[1536,3,384]{2,0,1:T(8,128)(2,1)S(1)}, bf16[1536,3,384]{2,0,1:T(8,128)(2,1)}, u32[]{:S(2)}) %copy-start) | copy-done | bytes 3538968
  13.2 0.9 copy-done.2
  14.1 1.6 %shard_map.91 = (f32[192,384]{1,0:T(8,128)S(1)}, f32[192,384]{1,0:T(8,128)S(1)}, bf16[192,384]{1,0:T(8,128)(2,1)S(1)}, f32[8,192]{1,0:T(8,128)S(1)}) custom-call(s32[1]{0:T(128)} %bitcast.2.x_ref, bf16[192,384]{1,0:T(8,128)(2,1)S(1)} %copy-done.2, bf16[192,384]{1,0:T(8,128)(2,1)S(1)} %collective-permute-done.1.one, ...), custom_call_target="tpu_custom_call" | custom-call | flops 679477248 | bytes 6291456 | tf_op jit(solution)/shard_map/pallas_call | solution.py:268
  15.6 1.4 %collective-permute-start.4 = (f32[8,192]{1,0:T(8,128)S(1)}, f32[8,192]{1,0:T(8,128)S(1)}, u32[]{:S(2)}, u32[]{:S(2)}) collective-permute-start(f32[8,192]{1,0:T(8,128)S(1)} %get-tuple-element.26.s0), channel_id=1, source_target_pairs={{3,0},{0,1},{1,2},{2,3},{7,4},{4,5},{5,6},{6,7},{11,8},{8,9},{9,10... | collective-permute-start | bytes 18440 | tf_op jit(solution)/shard_map/ppermute | solution.py:25
  17.1 2.4 %collective-permute-start.5 = (f32[8,192]{1,0:T(8,128)S(1)}, f32[8,192]{1,0:T(8,128)S(1)}, u32[]{:S(2)}, u32[]{:S(2)}) collective-permute-start(f32[8,192]{1,0:T(8,128)S(1)} %get-tuple-element.26.s0), channel_id=1, source_target_pairs={{2,0},{3,1},{0,2},{1,3},{6,4},{7,5},{4,6},{5,7},{10,8},{11,9},{8,1... | collective-permute-start | bytes 18440 | tf_op jit(solution)/shard_map/ppermute | solution.py:25
  19.5 1.6 %collective-permute-start.6 = (f32[8,192]{1,0:T(8,128)S(1)}, f32[8,192]{1,0:T(8,128)S(1)}, u32[]{:S(2)}, u32[]{:S(2)}) collective-permute-start(f32[8,192]{1,0:T(8,128)S(1)} %get-tuple-element.26.s0), channel_id=1, source_target_pairs={{1,0},{2,1},{3,2},{0,3},{5,4},{6,5},{7,6},{4,7},{9,8},{10,9},{11,1... | collective-permute-start | bytes 18440 | tf_op jit(solution)/shard_map/ppermute | solution.py:25
  21.0 1.2 collective-permute-done.5.s2
  22.2 0.9 collective-permute-done.6.s3
  23.1 0.3 shard_map.92
  23.4 0.8 collective-permute-start.7
  24.2 1.2 collective-permute-start.8
  25.4 7.2 %collective-permute-start.9 = (bf16[192,384]{1,0:T(8,128)(2,1)S(1)}, bf16[192,384]{1,0:T(8,128)(2,1)S(1)}, u32[]{:S(2)}, u32[]{:S(2)}) collective-permute-start(bf16[192,384]{1,0:T(8,128)(2,1)S(1)} %get-tuple-element.27), channel_id=1, source_target_pairs={{24,0},{28,4},{32,8},{36,12},{8,16},{12,20},{16,24},{20,28},{56,32... | collective-permute-start | bytes 442376 | tf_op jit(solution)/shard_map/ppermute | solution.py:328
  32.6 0.7 collective-permute-start.10
  33.4 6.0 %collective-permute-start.16 = (bf16[2,192,384]{2,1,0:T(8,128)(2,1)S(1)}, bf16[2,192,384]{2,1,0:T(8,128)(2,1)S(1)}, u32[]{:S(2)}, u32[]{:S(2)}) collective-permute-start(bf16[2,192,384]{2,1,0:T(8,128)(2,1)S(1)} %get-tuple-element.28.refs_3_), channel_id=1, source_target_pairs={{32,0},{36,4},{40,8},{44,12},{48,16},{52,20},{56,24},{60,28},{64,3... | collective-permute-start | bytes 884744 | tf_op jit(solution)/shard_map/ppermute | solution.py:327
  39.6 1.7 %collective-permute-done.12.refs_4_ = bf16[2,192,384]{2,1,0:T(8,128)(2,1)S(1)} collective-permute-done((bf16[2,192,384]{2,1,0:T(8,128)(2,1)S(1)}, bf16[2,192,384]{2,1,0:T(8,128)(2,1)S(1)}, u32[]{:S(2)}, u32[]{:S(2)}) %collective-permute-start.12) | collective-permute-done | bytes 294944 | tf_op jit(solution)/shard_map/ppermute | solution.py:326
  41.3 2.7 %collective-permute-done.16.refs_5_ = bf16[2,192,384]{2,1,0:T(8,128)(2,1)S(1)} collective-permute-done((bf16[2,192,384]{2,1,0:T(8,128)(2,1)S(1)}, bf16[2,192,384]{2,1,0:T(8,128)(2,1)S(1)}, u32[]{:S(2)}, u32[]{:S(2)}) %collective-permute-start.16) | collective-permute-done | bytes 294944 | tf_op jit(solution)/shard_map/ppermute | solution.py:327
  44.1 3.7 %collective-permute-start.17 = (bf16[2,192,384]{2,1,0:T(8,128)(2,1)S(1)}, bf16[2,192,384]{2,1,0:T(8,128)(2,1)S(1)}, u32[]{:S(2)}, u32[]{:S(2)}) collective-permute-start(bf16[2,192,384]{2,1,0:T(8,128)(2,1)S(1)} %collective-permute-done.16.refs_5_), channel_id=1, source_target_pairs={{32,0},{36,4},{40,8},{44,12},{48,16},{52,20},{56,24},{60,28},{64,3... | collective-permute-start | bytes 884744 | tf_op jit(solution)/shard_map/ppermute | solution.py:334
  47.8 2.5 %collective-permute-done.13.refs_3_ = bf16[2,192,384]{2,1,0:T(8,128)(2,1)S(1)} collective-permute-done((bf16[2,192,384]{2,1,0:T(8,128)(2,1)S(1)}, bf16[2,192,384]{2,1,0:T(8,128)(2,1)S(1)}, u32[]{:S(2)}, u32[]{:S(2)}) %collective-permute-start.13) | collective-permute-done | bytes 294944 | tf_op jit(solution)/shard_map/ppermute | solution.py:333
  50.6 1.7 %collective-permute-done.17.refs_4_ = bf16[2,192,384]{2,1,0:T(8,128)(2,1)S(1)} collective-permute-done((bf16[2,192,384]{2,1,0:T(8,128)(2,1)S(1)}, bf16[2,192,384]{2,1,0:T(8,128)(2,1)S(1)}, u32[]{:S(2)}, u32[]{:S(2)}) %collective-permute-start.17) | collective-permute-done | bytes 294944 | tf_op jit(solution)/shard_map/ppermute | solution.py:334
  52.3 3.7 %collective-permute-start.18 = (bf16[2,192,384]{2,1,0:T(8,128)(2,1)S(1)}, bf16[2,192,384]{2,1,0:T(8,128)(2,1)S(1)}, u32[]{:S(2)}, u32[]{:S(2)}) collective-permute-start(bf16[2,192,384]{2,1,0:T(8,128)(2,1)S(1)} %collective-permute-done.17.refs_4_), channel_id=1, source_target_pairs={{32,0},{36,4},{40,8},{44,12},{48,16},{52,20},{56,24},{60,28},{64,3... | collective-permute-start | bytes 884744 | tf_op jit(solution)/shard_map/ppermute | solution.py:334
  56.0 8.0 %shard_map.93 = (f32[8,192,384]{2,1,0:T(8,128)S(1)}, f32[8,192,128]{2,1,0:T(8,128)S(1)}) custom-call(f32[12]{0:T(128)S(1)} %stack.163.refs_0_, bf16[4,192,384]{2,1,0:T(8,128)(2,1)S(1)} %pad_maximum_fusion.refs_1_, bf16[4,192,384]{2,1,0:T(8,128)(2,1)S(1)} %collective-permute-done.11.refs_2_, bf16[2,192,384]{2,1,0:T(8,128)(2,1)S(1)} %get-tuple-element.28.refs_3_, ...), custom_call_target="tpu_custom_call" | custom-call | flops 1358954496 | bytes 4194304 | tf_op jit(solution)/shard_map/pallas_call | solution.py:237
  64.1 3.3 %collective-permute-start.19 = (bf16[192,384]{1,0:T(8,128)(2,1)S(1)}, bf16[192,384]{1,0:T(8,128)(2,1)S(1)}, u32[]{:S(2)}, u32[]{:S(2)}) collective-permute-start(bf16[192,384]{1,0:T(8,128)(2,1)S(1)} %slice_bitcast_fusion.4), channel_id=1, source_target_pairs={{32,0},{36,4},{40,8},{44,12},{48,16},{52,20},{56,24},{60,28},{64,3... | collective-permute-start | bytes 442376 | tf_op jit(solution)/shard_map/ppermute | solution.py:336
  67.4 7.8 %shard_map.94 = (f32[8,192,384]{2,1,0:T(8,128)S(1)}, f32[8,192,128]{2,1,0:T(8,128)S(1)}) custom-call(f32[8]{0:T(128)S(1)} %stack.150.refs_0_, bf16[4,192,384]{2,1,0:T(8,128)(2,1)S(1)} %pad_maximum_fusion.refs_1_, bf16[4,192,384]{2,1,0:T(8,128)(2,1)S(1)} %collective-permute-done.11.refs_2_, bf16[2,192,384]{2,1,0:T(8,128)(2,1)S(1)} %collective-permute-done.13.refs_3_, ...), custom_call_target="tpu_custom_call" | custom-call | flops 905969664 | bytes 4194304 | tf_op jit(solution)/shard_map/pallas_call | solution.py:237
  75.2 7.8 %shard_map.95 = (f32[8,192,384]{2,1,0:T(8,128)S(1)}, f32[8,192,128]{2,1,0:T(8,128)S(1)}) custom-call(f32[8]{0:T(128)S(1)} %stack.141.refs_0_, bf16[4,192,384]{2,1,0:T(8,128)(2,1)S(1)} %pad_maximum_fusion.refs_1_, bf16[4,192,384]{2,1,0:T(8,128)(2,1)S(1)} %collective-permute-done.11.refs_2_, bf16[2,192,384]{2,1,0:T(8,128)(2,1)S(1)} %collective-permute-done.14.refs_3_, ...), custom_call_target="tpu_custom_call" | custom-call | flops 905969664 | bytes 4194304 | tf_op jit(solution)/shard_map/pallas_call | solution.py:237
  83.0 11.5 %shard_map.96 = (bf16[4,208,384]{2,1,0:T(8,128)(2,1)S(1)}, bf16[4,208,384]{2,1,0:T(8,128)(2,1)S(1)}) custom-call(f32[4]{0:T(128)S(1)} %pad_maximum_fusion.1.refs_0_, bf16[4,192,384]{2,1,0:T(8,128)(2,1)S(1)} %pad_maximum_fusion.refs_1_, bf16[4,192,384]{2,1,0:T(8,128)(2,1)S(1)} %collective-permute-done.11.refs_2_, ...), custom_call_target="tpu_custom_call" | custom-call | flops 452984832 | bytes 4194304 | tf_op jit(solution)/shard_map/pallas_call | solution.py:237
  94.6 2.1 %collective-permute-done.20.other = bf16[4,208,384]{2,1,0:T(8,128)(2,1)S(1)} collective-permute-done((bf16[4,208,384]{2,1,0:T(8,128)(2,1)S(1)}, bf16[4,208,384]{2,1,0:T(8,128)(2,1)S(1)}, u32[]{:S(2)}, u32[]{:S(2)}) %collective-permute-start.20) | collective-permute-done | bytes 639008 | tf_op jit(solution)/shard_map/ppermute | solution.py:343
  96.7 1.0 shard_map.97
  97.7 4.8 %collective-permute-start.21 = (bf16[208,384]{1,0:T(8,128)(2,1)S(1)}, bf16[208,384]{1,0:T(8,128)(2,1)S(1)}, u32[]{:S(2)}, u32[]{:S(2)}) collective-permute-start(bf16[208,384]{1,0:T(8,128)(2,1)S(1)} %get-tuple-element.45), channel_id=1, source_target_pairs={{24,0},{28,4},{0,8},{4,12},{8,16},{12,20},{16,24},{20,28},{56,32},... | collective-permute-start | bytes 479240 | tf_op jit(solution)/shard_map/ppermute | solution.py:347
  102.5 1.2 collective-permute-start.23
  103.7 2.3 %collective-permute-start = (bf16[192,384]{1,0:T(8,128)(2,1)S(1)}, bf16[192,384]{1,0:T(8,128)(2,1)S(1)}, u32[]{:S(2)}, u32[]{:S(2)}) collective-permute-start(bf16[192,384]{1,0:T(8,128)(2,1)S(1)} %copy-done.3), channel_id=1, source_target_pairs={{8,0},{12,4},{16,8},{20,12},{24,16},{28,20},{32,24},{36,28},{40,32... | collective-permute-start | bytes 442376 | tf_op jit(solution)/shard_map/ppermute | solution.py:25
  106.0 3.6 %collective-permute-done.21.b = bf16[208,384]{1,0:T(8,128)(2,1)S(1)} collective-permute-done((bf16[208,384]{1,0:T(8,128)(2,1)S(1)}, bf16[208,384]{1,0:T(8,128)(2,1)S(1)}, u32[]{:S(2)}, u32[]{:S(2)}) %collective-permute-start.21) | collective-permute-done | bytes 159776 | tf_op jit(solution)/shard_map/ppermute | solution.py:347
  109.6 2.4 %collective-permute-done.22.c = bf16[208,384]{1,0:T(8,128)(2,1)S(1)} collective-permute-done((bf16[208,384]{1,0:T(8,128)(2,1)S(1)}, bf16[208,384]{1,0:T(8,128)(2,1)S(1)}, u32[]{:S(2)}, u32[]{:S(2)}) %collective-permute-start.22) | collective-permute-done | bytes 159776 | tf_op jit(solution)/shard_map/ppermute | solution.py:347
  112.0 4.2 %collective-permute-done.23.d = bf16[208,384]{1,0:T(8,128)(2,1)S(1)} collective-permute-done((bf16[208,384]{1,0:T(8,128)(2,1)S(1)}, bf16[208,384]{1,0:T(8,128)(2,1)S(1)}, u32[]{:S(2)}, u32[]{:S(2)}) %collective-permute-start.23) | collective-permute-done | bytes 159776 | tf_op jit(solution)/shard_map/ppermute | solution.py:347
  116.2 1.1 shard_map.98
  117.3 0.2 collective-permute-start.24
  117.5 3.5 %collective-permute-start.25 = (bf16[192,384]{1,0:T(8,128)(2,1)S(1)}, bf16[192,384]{1,0:T(8,128)(2,1)S(1)}, u32[]{:S(2)}, u32[]{:S(2)}) collective-permute-start(bf16[192,384]{1,0:T(8,128)(2,1)S(1)} %get-tuple-element.39), channel_id=1, source_target_pairs={{2,0},{3,1},{0,2},{1,3},{6,4},{7,5},{4,6},{5,7},{10,8},{11,9},{8,1... | collective-permute-start | bytes 442376 | tf_op jit(solution)/shard_map/ppermute | solution.py:25
  120.9 0.7 collective-permute-start.26
  123.4 0.8 dynamic-slice_reduce_fusion
  124.2 0.7 collective-permute-done.24
  124.9 2.6 %collective-permute-done.25 = bf16[192,384]{1,0:T(8,128)(2,1)S(1)} collective-permute-done((bf16[192,384]{1,0:T(8,128)(2,1)S(1)}, bf16[192,384]{1,0:T(8,128)(2,1)S(1)}, u32[]{:S(2)}, u32[]{:S(2)}) %collective-permute-start.25) | collective-permute-done | bytes 147488 | tf_op jit(solution)/shard_map/ppermute | solution.py:25
  127.5 0.2 collective-permute-done.26
  127.8 0.8 fusion
  (42 shorter events, 1.0 us)
Async XLA Ops:
  0.0 21.0 %copy-start.5 = (f32[384]{0:T(512)S(1)}, f32[384]{0:T(512)}, u32[]{:S(2)}) copy-start(f32[384]{0:T(512)} %param.16) | copy-start | bytes 4612
  0.0 21.0 %copy-start.6 = (f32[384]{0:T(512)S(1)}, f32[384]{0:T(512)}, u32[]{:S(2)}) copy-start(f32[384]{0:T(512)} %param.17) | copy-start | bytes 4612
  0.0 10.5 %collective-permute-start.1 = (bf16[192,384]{1,0:T(8,128)(2,1)}, bf16[192,384]{1,0:T(8,128)(2,1)S(1)}, u32[]{:S(2)}, u32[]{:S(2)}) collective-permute-start(bf16[192,384]{1,0:T(8,128)(2,1)} %own.1), channel_id=1, source_target_pairs={{3,0},{0,1},{1,2},{2,3},{7,4},{4,5},{5,6},{6,7},{11,8},{8,9},{9,10... | collective-permute-start | bytes 442376 | tf_op jit(solution)/shard_map/ppermute | solution.py:25
  1.5 9.7 %collective-permute-start.2 = (bf16[192,384]{1,0:T(8,128)(2,1)}, bf16[192,384]{1,0:T(8,128)(2,1)S(1)}, u32[]{:S(2)}, u32[]{:S(2)}) collective-permute-start(bf16[192,384]{1,0:T(8,128)(2,1)} %own.1), channel_id=1, source_target_pairs={{2,0},{3,1},{0,2},{1,3},{6,4},{7,5},{4,6},{5,7},{10,8},{11,9},{8,1... | collective-permute-start | bytes 442376 | tf_op jit(solution)/shard_map/ppermute | solution.py:25
  4.2 6.9 %collective-permute-start.3 = (bf16[192,384]{1,0:T(8,128)(2,1)}, bf16[192,384]{1,0:T(8,128)(2,1)S(1)}, u32[]{:S(2)}, u32[]{:S(2)}) collective-permute-start(bf16[192,384]{1,0:T(8,128)(2,1)} %own.1), channel_id=1, source_target_pairs={{1,0},{2,1},{3,2},{0,3},{5,4},{6,5},{7,6},{4,7},{9,8},{10,9},{11,1... | collective-permute-start | bytes 442376 | tf_op jit(solution)/shard_map/ppermute | solution.py:25
  11.2 2.0 %copy-start = (bf16[1536,3,384]{2,0,1:T(8,128)(2,1)S(1)}, bf16[1536,3,384]{2,0,1:T(8,128)(2,1)}, u32[]{:S(2)}) copy-start(bf16[1536,3,384]{2,0,1:T(8,128)(2,1)} %param.14) | copy-start | bytes 10616836
  13.2 0.9 copy-start.2
  15.6 5.4 %collective-permute-start.4 = (f32[8,192]{1,0:T(8,128)S(1)}, f32[8,192]{1,0:T(8,128)S(1)}, u32[]{:S(2)}, u32[]{:S(2)}) collective-permute-start(f32[8,192]{1,0:T(8,128)S(1)} %get-tuple-element.26.s0), channel_id=1, source_target_pairs={{3,0},{0,1},{1,2},{2,3},{7,4},{4,5},{5,6},{6,7},{11,8},{8,9},{9,10... | collective-permute-start | bytes 18440 | tf_op jit(solution)/shard_map/ppermute | solution.py:25
  17.1 5.2 %collective-permute-start.5 = (f32[8,192]{1,0:T(8,128)S(1)}, f32[8,192]{1,0:T(8,128)S(1)}, u32[]{:S(2)}, u32[]{:S(2)}) collective-permute-start(f32[8,192]{1,0:T(8,128)S(1)} %get-tuple-element.26.s0), channel_id=1, source_target_pairs={{2,0},{3,1},{0,2},{1,3},{6,4},{7,5},{4,6},{5,7},{10,8},{11,9},{8,1... | collective-permute-start | bytes 18440 | tf_op jit(solution)/shard_map/ppermute | solution.py:25
  19.5 3.7 %collective-permute-start.6 = (f32[8,192]{1,0:T(8,128)S(1)}, f32[8,192]{1,0:T(8,128)S(1)}, u32[]{:S(2)}, u32[]{:S(2)}) collective-permute-start(f32[8,192]{1,0:T(8,128)S(1)} %get-tuple-element.26.s0), channel_id=1, source_target_pairs={{1,0},{2,1},{3,2},{0,3},{5,4},{6,5},{7,6},{4,7},{9,8},{10,9},{11,1... | collective-permute-start | bytes 18440 | tf_op jit(solution)/shard_map/ppermute | solution.py:25
  23.4 10.0 %collective-permute-start.7 = (bf16[192,384]{1,0:T(8,128)(2,1)S(1)}, bf16[192,384]{1,0:T(8,128)(2,1)S(1)}, u32[]{:S(2)}, u32[]{:S(2)}) collective-permute-start(bf16[192,384]{1,0:T(8,128)(2,1)S(1)} %get-tuple-element.27), channel_id=1, source_target_pairs={{8,0},{12,4},{16,8},{20,12},{24,16},{28,20},{32,24},{36,28},{40,32... | collective-permute-start | bytes 442376 | tf_op jit(solution)/shard_map/ppermute | solution.py:328
  24.2 15.2 %collective-permute-start.8 = (bf16[192,384]{1,0:T(8,128)(2,1)S(1)}, bf16[192,384]{1,0:T(8,128)(2,1)S(1)}, u32[]{:S(2)}, u32[]{:S(2)}) collective-permute-start(bf16[192,384]{1,0:T(8,128)(2,1)S(1)} %get-tuple-element.27), channel_id=1, source_target_pairs={{16,0},{20,4},{24,8},{28,12},{32,16},{36,20},{8,24},{12,28},{48,32... | collective-permute-start | bytes 442376 | tf_op jit(solution)/shard_map/ppermute | solution.py:328
  25.4 14.0 %collective-permute-start.9 = (bf16[192,384]{1,0:T(8,128)(2,1)S(1)}, bf16[192,384]{1,0:T(8,128)(2,1)S(1)}, u32[]{:S(2)}, u32[]{:S(2)}) collective-permute-start(bf16[192,384]{1,0:T(8,128)(2,1)S(1)} %get-tuple-element.27), channel_id=1, source_target_pairs={{24,0},{28,4},{32,8},{36,12},{8,16},{12,20},{16,24},{20,28},{56,32... | collective-permute-start | bytes 442376 | tf_op jit(solution)/shard_map/ppermute | solution.py:328
  32.6 6.8 %collective-permute-start.10 = (bf16[192,384]{1,0:T(8,128)(2,1)S(1)}, bf16[192,384]{1,0:T(8,128)(2,1)S(1)}, u32[]{:S(2)}, u32[]{:S(2)}) collective-permute-start(bf16[192,384]{1,0:T(8,128)(2,1)S(1)} %get-tuple-element.27), channel_id=1, source_target_pairs={{32,0},{36,4},{8,8},{12,12},{16,16},{20,20},{24,24},{28,28},{64,32... | collective-permute-start | bytes 442376 | tf_op jit(solution)/shard_map/ppermute | solution.py:328
  33.3 8.0 %collective-permute-start.12 = (bf16[2,192,384]{2,1,0:T(8,128)(2,1)S(1)}, bf16[2,192,384]{2,1,0:T(8,128)(2,1)S(1)}, u32[]{:S(2)}, u32[]{:S(2)}) collective-permute-start(bf16[2,192,384]{2,1,0:T(8,128)(2,1)S(1)} %get-tuple-element.28.refs_3_), channel_id=1, source_target_pairs={{224,0},{228,4},{232,8},{236,12},{240,16},{244,20},{248,24},{252,2... | collective-permute-start | bytes 884744 | tf_op jit(solution)/shard_map/ppermute | solution.py:326
  33.4 10.7 %collective-permute-start.16 = (bf16[2,192,384]{2,1,0:T(8,128)(2,1)S(1)}, bf16[2,192,384]{2,1,0:T(8,128)(2,1)S(1)}, u32[]{:S(2)}, u32[]{:S(2)}) collective-permute-start(bf16[2,192,384]{2,1,0:T(8,128)(2,1)S(1)} %get-tuple-element.28.refs_3_), channel_id=1, source_target_pairs={{32,0},{36,4},{40,8},{44,12},{48,16},{52,20},{56,24},{60,28},{64,3... | collective-permute-start | bytes 884744 | tf_op jit(solution)/shard_map/ppermute | solution.py:327
  39.5 16.4 %collective-permute-start.11 = (bf16[4,192,384]{2,1,0:T(8,128)(2,1)S(1)}, bf16[4,192,384]{2,1,0:T(8,128)(2,1)S(1)}, u32[]{:S(2)}, u32[]{:S(2)}) collective-permute-start(bf16[4,192,384]{2,1,0:T(8,128)(2,1)S(1)} %pad_maximum_fusion.refs_1_), channel_id=1, source_target_pairs={{0,4},{4,0},{8,12},{12,8},{16,20},{20,16},{24,28},{28,24},{32,36},... | collective-permute-start | bytes 1769480 | tf_op jit(solution)/shard_map/ppermute | solution.py:329
  41.3 9.0 %collective-permute-start.13 = (bf16[2,192,384]{2,1,0:T(8,128)(2,1)S(1)}, bf16[2,192,384]{2,1,0:T(8,128)(2,1)S(1)}, u32[]{:S(2)}, u32[]{:S(2)}) collective-permute-start(bf16[2,192,384]{2,1,0:T(8,128)(2,1)S(1)} %collective-permute-done.12.refs_4_), channel_id=1, source_target_pairs={{224,0},{228,4},{232,8},{236,12},{240,16},{244,20},{248,24},{252,2... | collective-permute-start | bytes 884744 | tf_op jit(solution)/shard_map/ppermute | solution.py:333
  44.1 8.2 %collective-permute-start.17 = (bf16[2,192,384]{2,1,0:T(8,128)(2,1)S(1)}, bf16[2,192,384]{2,1,0:T(8,128)(2,1)S(1)}, u32[]{:S(2)}, u32[]{:S(2)}) collective-permute-start(bf16[2,192,384]{2,1,0:T(8,128)(2,1)S(1)} %collective-permute-done.16.refs_5_), channel_id=1, source_target_pairs={{32,0},{36,4},{40,8},{44,12},{48,16},{52,20},{56,24},{60,28},{64,3... | collective-permute-start | bytes 884744 | tf_op jit(solution)/shard_map/ppermute | solution.py:334
  50.3 13.7 %collective-permute-start.14 = (bf16[2,192,384]{2,1,0:T(8,128)(2,1)S(1)}, bf16[2,192,384]{2,1,0:T(8,128)(2,1)S(1)}, u32[]{:S(2)}, u32[]{:S(2)}) collective-permute-start(bf16[2,192,384]{2,1,0:T(8,128)(2,1)S(1)} %collective-permute-done.13.refs_3_), channel_id=1, source_target_pairs={{224,0},{228,4},{232,8},{236,12},{240,16},{244,20},{248,24},{252,2... | collective-permute-start | bytes 884744 | tf_op jit(solution)/shard_map/ppermute | solution.py:333
  52.3 11.8 %collective-permute-start.18 = (bf16[2,192,384]{2,1,0:T(8,128)(2,1)S(1)}, bf16[2,192,384]{2,1,0:T(8,128)(2,1)S(1)}, u32[]{:S(2)}, u32[]{:S(2)}) collective-permute-start(bf16[2,192,384]{2,1,0:T(8,128)(2,1)S(1)} %collective-permute-done.17.refs_4_), channel_id=1, source_target_pairs={{32,0},{36,4},{40,8},{44,12},{48,16},{52,20},{56,24},{60,28},{64,3... | collective-permute-start | bytes 884744 | tf_op jit(solution)/shard_map/ppermute | solution.py:334
  64.0 19.0 %collective-permute-start.15 = (bf16[192,384]{1,0:T(8,128)(2,1)S(1)}, bf16[192,384]{1,0:T(8,128)(2,1)S(1)}, u32[]{:S(2)}, u32[]{:S(2)}) collective-permute-start(bf16[192,384]{1,0:T(8,128)(2,1)S(1)} %slice_bitcast_fusion.5), channel_id=1, source_target_pairs={{224,0},{228,4},{232,8},{236,12},{240,16},{244,20},{248,24},{252,2... | collective-permute-start | bytes 442376 | tf_op jit(solution)/shard_map/ppermute | solution.py:335
  64.1 18.9 %collective-permute-start.19 = (bf16[192,384]{1,0:T(8,128)(2,1)S(1)}, bf16[192,384]{1,0:T(8,128)(2,1)S(1)}, u32[]{:S(2)}, u32[]{:S(2)}) collective-permute-start(bf16[192,384]{1,0:T(8,128)(2,1)S(1)} %slice_bitcast_fusion.4), channel_id=1, source_target_pairs={{32,0},{36,4},{40,8},{44,12},{48,16},{52,20},{56,24},{60,28},{64,3... | collective-permute-start | bytes 442376 | tf_op jit(solution)/shard_map/ppermute | solution.py:336
  94.5 9.2 %copy-start.3 = (bf16[192,384]{1,0:T(8,128)(2,1)S(1)}, bf16[192,384]{1,0:T(8,128)(2,1)}, u32[]{:S(2)}) copy-start(bf16[192,384]{1,0:T(8,128)(2,1)} %own.1) | copy-start | bytes 442372
  94.5 21.7 %copy-start.1 = (bf16[384,1536]{1,0:T(8,128)(2,1)S(1)}, bf16[384,1536]{1,0:T(8,128)(2,1)}, u32[]{:S(2)}) copy-start(bf16[384,1536]{1,0:T(8,128)(2,1)} %w_ref.1) | copy-start | bytes 3538948
  94.5 2.2 %collective-permute-start.20 = (bf16[4,208,384]{2,1,0:T(8,128)(2,1)S(1)}, bf16[4,208,384]{2,1,0:T(8,128)(2,1)S(1)}, u32[]{:S(2)}, u32[]{:S(2)}) collective-permute-start(bf16[4,208,384]{2,1,0:T(8,128)(2,1)S(1)} %get-tuple-element.36), channel_id=1, source_target_pairs={{0,4},{4,0},{8,12},{12,8},{16,20},{20,16},{24,28},{28,24},{32,36},... | collective-permute-start | bytes 1916936 | tf_op jit(solution)/shard_map/ppermute | solution.py:343
  96.7 31.1 %copy-start.4 = (bf16[384,384]{1,0:T(8,128)(2,1)S(1)}, bf16[384,384]{1,0:T(8,128)(2,1)}, u32[]{:S(2)}) copy-start(bf16[384,384]{1,0:T(8,128)(2,1)} %param.10) | copy-start | bytes 884740
  97.7 11.9 %collective-permute-start.21 = (bf16[208,384]{1,0:T(8,128)(2,1)S(1)}, bf16[208,384]{1,0:T(8,128)(2,1)S(1)}, u32[]{:S(2)}, u32[]{:S(2)}) collective-permute-start(bf16[208,384]{1,0:T(8,128)(2,1)S(1)} %get-tuple-element.45), channel_id=1, source_target_pairs={{24,0},{28,4},{0,8},{4,12},{8,16},{12,20},{16,24},{20,28},{56,32},... | collective-permute-start | bytes 479240 | tf_op jit(solution)/shard_map/ppermute | solution.py:347
  102.5 9.5 %collective-permute-start.22 = (bf16[208,384]{1,0:T(8,128)(2,1)S(1)}, bf16[208,384]{1,0:T(8,128)(2,1)S(1)}, u32[]{:S(2)}, u32[]{:S(2)}) collective-permute-start(bf16[208,384]{1,0:T(8,128)(2,1)S(1)} %get-tuple-element.44), channel_id=1, source_target_pairs={{16,0},{20,4},{24,8},{28,12},{0,16},{4,20},{8,24},{12,28},{48,32},... | collective-permute-start | bytes 479240 | tf_op jit(solution)/shard_map/ppermute | solution.py:347
  102.5 13.7 %collective-permute-start.23 = (bf16[208,384]{1,0:T(8,128)(2,1)S(1)}, bf16[208,384]{1,0:T(8,128)(2,1)S(1)}, u32[]{:S(2)}, u32[]{:S(2)}) collective-permute-start(bf16[208,384]{1,0:T(8,128)(2,1)S(1)} %get-tuple-element.43), channel_id=1, source_target_pairs={{8,0},{12,4},{16,8},{20,12},{24,16},{28,20},{0,24},{4,28},{40,32},... | collective-permute-start | bytes 479240 | tf_op jit(solution)/shard_map/ppermute | solution.py:347
  103.7 20.5 %collective-permute-start = (bf16[192,384]{1,0:T(8,128)(2,1)S(1)}, bf16[192,384]{1,0:T(8,128)(2,1)S(1)}, u32[]{:S(2)}, u32[]{:S(2)}) collective-permute-start(bf16[192,384]{1,0:T(8,128)(2,1)S(1)} %copy-done.3), channel_id=1, source_target_pairs={{8,0},{12,4},{16,8},{20,12},{24,16},{28,20},{32,24},{36,28},{40,32... | collective-permute-start | bytes 442376 | tf_op jit(solution)/shard_map/ppermute | solution.py:25
  117.3 7.7 %collective-permute-start.24 = (bf16[192,384]{1,0:T(8,128)(2,1)S(1)}, bf16[192,384]{1,0:T(8,128)(2,1)S(1)}, u32[]{:S(2)}, u32[]{:S(2)}) collective-permute-start(bf16[192,384]{1,0:T(8,128)(2,1)S(1)} %get-tuple-element.38), channel_id=1, source_target_pairs={{3,0},{0,1},{1,2},{2,3},{7,4},{4,5},{5,6},{6,7},{11,8},{8,9},{9,10... | collective-permute-start | bytes 442376 | tf_op jit(solution)/shard_map/ppermute | solution.py:25
  117.5 10.1 %collective-permute-start.25 = (bf16[192,384]{1,0:T(8,128)(2,1)S(1)}, bf16[192,384]{1,0:T(8,128)(2,1)S(1)}, u32[]{:S(2)}, u32[]{:S(2)}) collective-permute-start(bf16[192,384]{1,0:T(8,128)(2,1)S(1)} %get-tuple-element.39), channel_id=1, source_target_pairs={{2,0},{3,1},{0,2},{1,3},{6,4},{7,5},{4,6},{5,7},{10,8},{11,9},{8,1... | collective-permute-start | bytes 442376 | tf_op jit(solution)/shard_map/ppermute | solution.py:25
  120.9 6.8 %collective-permute-start.26 = (bf16[192,384]{1,0:T(8,128)(2,1)S(1)}, bf16[192,384]{1,0:T(8,128)(2,1)S(1)}, u32[]{:S(2)}, u32[]{:S(2)}) collective-permute-start(bf16[192,384]{1,0:T(8,128)(2,1)S(1)} %get-tuple-element.40), channel_id=1, source_target_pairs={{1,0},{2,1},{3,2},{0,3},{5,4},{6,5},{7,6},{4,7},{9,8},{10,9},{11,1... | collective-permute-start | bytes 442376 | tf_op jit(solution)/shard_map/ppermute | solution.py:25

commit v2 on v1

v2 whole, which is shorter than its diff:
```python
import functools

import jax
import jax.numpy as jnp
from jax import lax
from jax.experimental import pallas as pl
from jax.experimental.pallas import tpu as pltpu
from jax.sharding import PartitionSpec as P

D = 1536
DH = 128
LOG2E = 1.4426950408889634
LOW = -1e30
NY = 4
NZ = 8
GROUPS = ((0, 1, -1, 2), (-2, 3, -3, 4))
TAIL = 16

VMEM = pl.BlockSpec(memory_space=pltpu.VMEM)
SMEM = pl.BlockSpec(memory_space=pltpu.SMEM)
MIB = 1024 * 1024


def shift(block, axis, distance):
    n = lax.axis_size(axis)
    return lax.ppermute(block, axis, [((i - distance) % n, i) for i in range(n)])


def to_column(row, rows):
    pad = jnp.zeros((128 - row.shape[0], rows), row.dtype)
    return jnp.concatenate([row, pad], axis=0).T


def to_row(column):
    return column.T[0:8]


def lanes_of(columns, rows):
    lane = lax.broadcasted_iota(jnp.int32, (rows, 128), 1)
    out = jnp.zeros((rows, 128), jnp.float32)
    for j, column in enumerate(columns):
        out = jnp.where(lane == j, column, out)
    return out


def project_kernel(x_ref, own, one, two, three, scale_ref, shift_ref, w_ref, q_ref, k_ref, v_ref, sums_ref):
    x = x_ref[0]
    n = 4
    order = [lax.rem(x - j + n, n) for j in range(n)]
    width = own.shape[1]
    rows = own.shape[0]
    chunks = [r[...].astype(jnp.float32) for r in (own, one, two, three)]
    total = sum(jnp.sum(c, axis=1, keepdims=True) for c in chunks)
    mean = total / D
    centered = [c - mean for c in chunks]
    variance = sum(jnp.sum(c * c, axis=1, keepdims=True) for c in centered) / D
    inv = lax.rsqrt(variance + 1e-06)
    modded = []
    for j in range(n):
        sc = scale_ref[order[j]]
        sh = shift_ref[order[j]]
        modded.append((centered[j] * inv * (1.0 + sc) + sh).astype(jnp.bfloat16))
    outs = []
    for part in range(3):
        acc = None
        for j in range(n):
            start = pl.multiple_of(order[j] * width, 128)
            d = jnp.dot(modded[j], w_ref[part, pl.ds(start, width), :], preferred_element_type=jnp.float32)
            acc = d if acc is None else acc + d
        outs.append(acc)
    q_ref[...] = outs[0]
    k_ref[...] = outs[1]
    v_ref[...] = outs[2].astype(jnp.bfloat16)
    sums = [jnp.sum(o * o, axis=1, keepdims=True) for o in outs[:2]]
    sums_ref[...] = to_row(lanes_of(sums, rows))


def norm_kernel(q_ref, k_ref, s0, s1, s2, s3, qg_ref, kg_ref, qn_ref, kn_ref):
    rows = q_ref.shape[0]
    total = s0[...] + s1[...] + s2[...] + s3[...]
    inv = to_column(lax.rsqrt(total / D + 1e-06), rows)
    qn_ref[...] = (q_ref[...] * inv[:, 0:1] * (qg_ref[...] * (LOG2E * DH ** (-0.5)))).astype(jnp.bfloat16)
    kn_ref[...] = (k_ref[...] * inv[:, 1:2] * kg_ref[...]).astype(jnp.bfloat16)


def attend_kernel(slabs, flags, *refs):
    queries, refs = refs[:NY], refs[NY:]
    keys, values, outs = refs[:slabs], refs[slabs : 2 * slabs], refs[2 * slabs :]
    rows, width = queries[0].shape[1:]
    heads = width // DH
    col = lax.broadcasted_iota(jnp.int32, (1, rows * slabs), 1)
    ones = jnp.ones((rows * slabs, DH), jnp.bfloat16)
    biases = []
    for k in range(NY):
        bias = jnp.full((1, rows * slabs), flags[k * slabs], jnp.float32)
        for j in range(1, slabs):
            bias = jnp.where(col >= j * rows, flags[k * slabs + j], bias)
        biases.append(bias)
    for parity, out in enumerate(outs):
        logs = [[] for _ in range(NY)]
        for h in range(heads):
            lanes = slice(h * DH, (h + 1) * DH)
            q = jnp.concatenate([r[parity, :, lanes] for r in queries], axis=0)
            kk = jnp.concatenate([r[:, lanes] for r in keys], axis=0)
            vv = jnp.concatenate([r[:, lanes] for r in values], axis=0)
            s = lax.dot_general(q, kk, (((1,), (1,)), ((), ())), preferred_element_type=jnp.float32)
            tops, es = [], []
            for k in range(NY):
                part = s[k * rows : (k + 1) * rows] + biases[k]
                top = jnp.max(part, axis=1, keepdims=True)
                es.append(jnp.exp2(part - top).astype(jnp.bfloat16))
                tops.append(top)
            e = jnp.concatenate(es, axis=0)
            o = jnp.dot(e, jnp.concatenate([vv, ones], axis=1), preferred_element_type=jnp.float32)
            for k in range(NY):
                here = slice(k * rows, (k + 1) * rows)
                total = o[here, DH:]
                out[k, 0:rows, lanes] = (o[here, :DH] / total).astype(jnp.bfloat16)
                logs[k].append(tops[k] + jnp.log2(total))
        for k in range(NY):
            out[k, rows : rows + TAIL, 0:rows] = log_rows(logs[k], rows)


def log_rows(columns, rows):
    lane = lax.broadcasted_iota(jnp.int32, (rows, 128), 1)
    tile = jnp.zeros((rows, 128), jnp.float32)
    for j, column in enumerate(columns):
        high = column.astype(jnp.bfloat16).astype(jnp.float32)
        tile = jnp.where(lane == j, high, jnp.where(lane == 8 + j, column - high, tile))
    pick = lax.broadcasted_iota(jnp.int32, (TAIL, 128), 0) == lax.broadcasted_iota(jnp.int32, (TAIL, 128), 1)
    out = lax.dot_general(
        pick.astype(jnp.bfloat16), tile.astype(jnp.bfloat16), (((1,), (1,)), ((), ())), preferred_element_type=jnp.float32
    )
    return out.astype(jnp.bfloat16)


def merge(blocks, rows):
    logs = []
    for block in blocks:
        tail = block[rows : rows + TAIL, 0:rows].astype(jnp.float32)
        logs.append(tail[0:8] + tail[8:16])
    width = blocks[0].shape[1]
    top = functools.reduce(jnp.maximum, logs)
    parts = [jnp.exp2(v - top) for v in logs]
    total = sum(parts)
    inv = 1.0 / total
    row = lax.broadcasted_iota(jnp.int32, (TAIL, width), 0) % 8
    spread = (row == lax.broadcasted_iota(jnp.int32, (TAIL, width), 1) // DH).astype(jnp.bfloat16)
    out = jnp.zeros((rows, width), jnp.float32)
    for part, block in zip(parts, blocks, strict=True):
        weight = part * inv
        high = weight.astype(jnp.bfloat16).astype(jnp.float32)
        both = jnp.concatenate([high, weight - high], axis=0).astype(jnp.bfloat16)
        column = lax.dot_general(both, spread, (((0,), (0,)), ((), ())), preferred_element_type=jnp.float32)
        out = out + column * block[0:rows, :].astype(jnp.float32)
    return out, top + jnp.log2(total)


def pair_kernel(*refs):
    blocks, out = refs[:-1], refs[-1]
    rows = out.shape[1] - TAIL
    for k in range(NY):
        merged, logs = merge([b.at[k] for b in blocks], rows)
        out[k, 0:rows, :] = merged.astype(jnp.bfloat16)
        high = logs.astype(jnp.bfloat16).astype(jnp.float32)
        both = jnp.concatenate([high, logs - high], axis=0)
        out[k, rows : rows + TAIL, 0:rows] = both.astype(jnp.bfloat16)


def out_kernel(x_ref, a, b, c, d, w_ref, *outs):
    rows = a.shape[0] - TAIL
    width = a.shape[1]
    x = x_ref[0]
    merged, _ = merge([a, b, c, d], rows)
    attn = merged.astype(jnp.bfloat16)
    n = len(outs)
    for j in range(n):
        start = pl.multiple_of(lax.rem(x + j, n) * width, 128)
        outs[j][...] = jnp.dot(attn, w_ref[:, pl.ds(start, width)], preferred_element_type=jnp.float32).astype(
            jnp.bfloat16
        )


def shape(dims, dtype):
    return jax.ShapeDtypeStruct(dims, dtype)


def call(kernel, ins, out_shape, flops, moved, exps=0):
    return pl.pallas_call(
        kernel,
        out_shape=out_shape,
        in_specs=ins,
        out_specs=jax.tree.map(lambda _: VMEM, out_shape),
        compiler_params=pltpu.CompilerParams(vmem_limit_bytes=40 * MIB),
        cost_estimate=pl.CostEstimate(flops=flops, bytes_accessed=moved, transcendentals=exps),
    )


def attend(flags, queries, keys, values):
    slots = len(queries)
    rows, width = queries[0].shape[1:]
    slabs = len(keys)
    scores = 2 * slots * rows * rows * slabs * (width // DH)
    return call(
        functools.partial(attend_kernel, slabs),
        [SMEM] + [VMEM] * (slots + 2 * slabs),
        [shape((slots, rows + TAIL, width), jnp.bfloat16)] * 2,
        scores * DH * 4,
        1 << 20,
        scores,
    )(flags, *queries, *keys, *values)


def combine(blocks):
    size = blocks[0].size
    return call(
        pair_kernel, [VMEM] * len(blocks), shape(blocks[0].shape, jnp.bfloat16), size * 2 * len(blocks), size * 2 * len(blocks)
    )(*blocks)


def local(latents, fresh_frame, noise_level, offset, mod_table, w_qkv, w_out, q_gain, k_gain):
    slabs = lax.axis_size("queue")
    frames = slabs // 2
    heads_ax = lax.axis_size("head")
    rows, width = latents.shape
    slab = lax.axis_index("queue")
    x = lax.axis_index("head")
    frame = slab // 2
    z, y = frame // NY, frame % NY
    x_arg = x.astype(jnp.int32).reshape(1)

    def place(f):
        return jnp.mod(f - offset[0], frames)

    chunks = [shift(latents, "head", j) for j in range(1, heads_ax)]
    home_latents = shift(latents, "queue", -2)
    modulation = lax.dynamic_index_in_dim(mod_table, noise_level[place(frame)], 0, keepdims=False)
    home_level = noise_level[place(frame + 1)]
    gate = lax.dynamic_slice(mod_table, (home_level, 2, x * width), (1, 1, width)).reshape(1, width)
    modulation = modulation.reshape(3, heads_ax, 1, width)
    w3 = jnp.transpose(w_qkv, (1, 0, 2))
    q, k, v, sums = call(
        project_kernel,
        [SMEM] + [VMEM] * 7,
        [
            shape((rows, width), jnp.float32),
            shape((rows, width), jnp.float32),
            shape((rows, width), jnp.bfloat16),
            shape((8, rows), jnp.float32),
        ],
        2 * rows * D * 3 * width,
        6 << 20,
    )(x_arg, latents, *chunks, modulation[1], modulation[0], w3)
    all_sums = [sums] + [shift(sums, "head", j) for j in range(1, heads_ax)]
    qn, kn = call(
        norm_kernel,
        [VMEM] * 8,
        [shape((rows, width), jnp.bfloat16)] * 2,
        rows * width * 8,
        2 << 20,
    )(q, k, *all_sums, q_gain.reshape(1, width), k_gain.reshape(1, width))

    def key_route(distance):
        route = []
        for f in range(frames):
            fz, fy = f // NY, f % NY
            source = ((fz - distance) % NZ) * NY + fy
            route += [(2 * source + c, 2 * f + c) for c in range(2)]
        return route

    def y_route(distance):
        route = []
        for f in range(frames):
            fz, fy = f // NY, f % NY
            source = fz * NY + (fy - distance) % NY
            route += [(2 * source + c, 2 * f + c) for c in range(2)]
        return route

    swap = [(i, i ^ 1) for i in range(slabs)]

    def flags_of(distances):
        out = []
        for j in range(NY):
            q_place = place(z * NY + (y + j) % NY + 1)
            for d in distances:
                k_place = place(jnp.mod(z - d, NZ) * NY + y)
                out.append(jnp.where(k_place <= q_place, 0.0, LOW))
        return jnp.stack(out).astype(jnp.float32)

    both = {0: jnp.stack([kn, v])}
    for way in (1, -1):
        both[way] = lax.ppermute(both[0], "queue", key_route(way))
    home_q = [shift(qn, "queue", -2), lax.ppermute(qn, "queue", [((i + 2) % slabs ^ 1, i) for i in range(slabs)])]
    both[1], both[-1], home_q = lax.optimization_barrier((both[1], both[-1], home_q))
    for way in (1, -1):
        both[way * 2] = lax.ppermute(both[way], "queue", key_route(way))
    home_q = jnp.stack(home_q)
    qs = [home_q] + [lax.ppermute(home_q, "queue", y_route(-j)) for j in range(1, NY)]
    for way in (1, -1):
        both[way * 3] = lax.ppermute(both[way * 2], "queue", key_route(way))
    ks = {d: b[0] for d, b in both.items()}
    vs = {d: b[1] for d, b in both.items()}

    def partial(distances):
        return attend(flags_of(distances), qs, [ks[d] for d in distances], [vs[d] for d in distances])

    ks[4] = lax.ppermute(ks[3], "queue", key_route(1))
    vs[4] = lax.ppermute(vs[-3], "queue", key_route(-1))
    ks[4], vs[4], home_latents = lax.optimization_barrier((ks[4], vs[4], home_latents))
    partials = [partial(distances) for distances in GROUPS]
    mine, other = [p[0] for p in partials], [p[1] for p in partials]
    received = lax.ppermute(combine(other), "queue", swap)
    paired = combine(mine + [received])
    parts = [paired[0]] + [lax.ppermute(paired[j], "queue", y_route(j)) for j in range(1, NY)]
    blocks = call(
        out_kernel,
        [SMEM] + [VMEM] * 5,
        [shape((rows, width), jnp.bfloat16)] * heads_ax,
        2 * rows * width * D,
        3 << 20,
    )(x_arg, *parts, w_out)
    proj = blocks[0].astype(jnp.float32)
    for j in range(1, heads_ax):
        proj = proj + shift(blocks[j], "head", j).astype(jnp.float32)
    updated = (home_latents.astype(jnp.float32) + gate * proj).astype(jnp.bfloat16)
    entry_slot = jnp.mod(offset[0] - 1, frames)
    fresh_half = lax.dynamic_slice_in_dim(fresh_frame, slab % 2 * rows, rows, 0)
    return jnp.where(frame == entry_slot, fresh_half, updated)


def solution(mesh):
    return jax.shard_map(
        local,
        mesh=mesh,
        in_specs=(
            P("queue", "head"),
            P(None, "head"),
            P(),
            P(),
            P(),
            P(None, None, "head"),
            P("head", None),
            P("head"),
            P("head"),
        ),
        out_specs=P("queue", "head"),
        check_vma=False,
    )
```

time: 129 us -> 108 us (0.84)
  Pallas kernels: 38.9 us -> 16.3 us
  waiting for transfers between devices: 27.1 us -> 37.9 us
  starting transfers between devices: 50.7 us -> 41.9 us
    pallas_call x6 -> x5, Pallas kernels: 36.3 us -> 13 us  [the longest x2 11.4 us: attend(): call(functools.partial(attend_kernel, slabs), [SMEM] + [VMEM] * (slots +...]
    ppermute x10 -> x11, waiting for transfers between devices: 6.27 us -> 13.6 us  [shift(): lax.ppermute(block, axis, [((i - distance) % n, i) for i in range(n)])]
    ppermute x14 -> x13, starting transfers between devices: 27 us -> 22.4 us  [the longest x2 6.02 us: local(): both[way] = lax.ppermute(both[0], 'queue', key_route(way))]
    ppermute x14 -> x13, waiting for transfers between devices: 10.7 us -> 14.7 us  [the longest x2 8.43 us: local(): both[way * 3] = lax.ppermute(both[way * 2], 'queue', key_route(way))]
    ppermute x3, starting transfers between devices: 5.96 us -> 2.97 us  [local(): lax.ppermute(paired[j], 'queue', y_route(j))]
    ppermute x10 -> x11, starting transfers between devices: 17.7 us -> 16.5 us  [shift(): lax.ppermute(block, axis, [((i - distance) % n, i) for i in range(n)])]
    unnamed x14 -> x10, local copies, waits for them, and re-layouts: 2.93 us -> 2.02 us
  transfers between devices with their start and end apart: 27 -> 27, of which waited for: 14 -> 16; matrix products, arithmetic and copies ran while one was open for 3% -> 3% of each run, Pallas kernels for 19% -> 5%
where the time goes in v2:
time: 108 us; the launch traced here: 107 us
  starting transfers between devices  41.9 us (39%)
  waiting for transfers between devices  37.9 us (35%)
  Pallas kernels  16.3 us (15%)
  local copies, waits for them, and re-layouts  5.47 us (5%)
  between operations  4.68 us (4%)
    ppermute x11, starting transfers between devices, shift(): lax.ppermute(block, axis, [((i - distance) % n, i) for i in range(n)])  16.5 us
    ppermute x11, waiting for transfers between devices, shift(): lax.ppermute(block, axis, [((i - distance) % n, i) for i in range(n)])  13.6 us
    pallas_call x2, Pallas kernels, attend(): call(functools.partial(attend_kernel, slabs), [SMEM] + [VMEM] * (slots +...  11.4 us
    ppermute x3, waiting for transfers between devices, local(): lax.ppermute(paired[j], 'queue', y_route(j))  9.56 us
    ppermute x2, waiting for transfers between devices, local(): both[way * 3] = lax.ppermute(both[way * 2], 'queue', key_route(way))  8.43 us
    ppermute x2, starting transfers between devices, local(): both[way] = lax.ppermute(both[0], 'queue', key_route(way))  6.02 us
    ppermute x3, starting transfers between devices, local(): lax.ppermute(home_q, 'queue', y_route(-j))  5.42 us
    ppermute x2, starting transfers between devices, local(): both[way * 2] = lax.ppermute(both[way], 'queue', key_route(way))  3.62 us
  transfers between devices with their start and end apart: 27, of which 16 were waited for; matrix products, arithmetic and copies ran while one was open for 3% of the time, Pallas kernels for 5%

profile of v2, /device:TPU:24, one launch (start us, length us, event | category | flops | bytes accessed | tf_op | source)
XLA Modules:
  0.0 107.1 jit_solution(18207368171187857969)
XLA Ops:
  0.0 1.5 %collective-permute-start = (bf16[192,384]{1,0:T(8,128)(2,1)}, bf16[192,384]{1,0:T(8,128)(2,1)S(1)}, u32[]{:S(2)}, u32[]{:S(2)}) collective-permute-start(bf16[192,384]{1,0:T(8,128)(2,1)} %own.1), channel_id=1, source_target_pairs={{3,0},{0,1},{1,2},{2,3},{7,4},{4,5},{5,6},{6,7},{11,8},{8,9},{9,10... | collective-permute-start | bytes 442376 | tf_op jit(solution)/shard_map/ppermute | solution.py:26
  1.5 2.7 %collective-permute-start.1 = (bf16[192,384]{1,0:T(8,128)(2,1)}, bf16[192,384]{1,0:T(8,128)(2,1)S(1)}, u32[]{:S(2)}, u32[]{:S(2)}) collective-permute-start(bf16[192,384]{1,0:T(8,128)(2,1)} %own.1), channel_id=1, source_target_pairs={{2,0},{3,1},{0,2},{1,3},{6,4},{7,5},{4,6},{5,7},{10,8},{11,9},{8,1... | collective-permute-start | bytes 442376 | tf_op jit(solution)/shard_map/ppermute | solution.py:26
  4.2 1.4 %collective-permute-start.2 = (bf16[192,384]{1,0:T(8,128)(2,1)}, bf16[192,384]{1,0:T(8,128)(2,1)S(1)}, u32[]{:S(2)}, u32[]{:S(2)}) collective-permute-start(bf16[192,384]{1,0:T(8,128)(2,1)} %own.1), channel_id=1, source_target_pairs={{1,0},{2,1},{3,2},{0,3},{5,4},{6,5},{7,6},{4,7},{9,8},{10,9},{11,1... | collective-permute-start | bytes 442376 | tf_op jit(solution)/shard_map/ppermute | solution.py:26
  6.4 1.4 %fusion.1 = (s32[1]{0:T(128)}, s32[1]{0:T(128)}) fusion(s32[32]{0:T(128)} %param.11, s32[]{:T(128)S(6)} %select_n.371, s32[]{:T(128)S(6)} %select_n.368), kind=kLoop, calls=%fused_computation.23 | loop fusion | bytes 24 | tf_op jit(solution)/shard_map/dynamic_slice | solution.py:238
  9.6 0.8 constant_dynamic-slice_fusion.1
  10.4 0.7 collective-permute-done.1.two
  11.2 2.0 %copy-done = bf16[1536,3,384]{2,0,1:T(8,128)(2,1)S(1)} copy-done((bf16[1536,3,384]{2,0,1:T(8,128)(2,1)S(1)}, bf16[1536,3,384]{2,0,1:T(8,128)(2,1)}, u32[]{:S(2)}) %copy-start) | copy-done | bytes 3538968
  13.2 2.5 %shard_map.91 = (f32[192,384]{1,0:T(8,128)S(1)}, f32[192,384]{1,0:T(8,128)S(1)}, bf16[192,384]{1,0:T(8,128)(2,1)S(1)}, f32[8,192]{1,0:T(8,128)S(1)}) custom-call(s32[1]{0:T(128)} %bitcast.1.x_ref, bf16[192,384]{1,0:T(8,128)(2,1)} %own.1, bf16[192,384]{1,0:T(8,128)(2,1)S(1)} %collective-permute-done.one, bf16[192,384]{1,0:T(8,128)(2,1)S(1)} %collective-permute-done.1.two, ...), custom_call_target="tpu_custom_call" | custom-call | flops 679477248 | bytes 6291456 | tf_op jit(solution)/shard_map/pallas_call | solution.py:242
  15.6 1.4 %collective-permute-start.3 = (f32[8,192]{1,0:T(8,128)S(1)}, f32[8,192]{1,0:T(8,128)S(1)}, u32[]{:S(2)}, u32[]{:S(2)}) collective-permute-start(f32[8,192]{1,0:T(8,128)S(1)} %get-tuple-element.28.s0), channel_id=1, source_target_pairs={{3,0},{0,1},{1,2},{2,3},{7,4},{4,5},{5,6},{6,7},{11,8},{8,9},{9,10... | collective-permute-start | bytes 18440 | tf_op jit(solution)/shard_map/ppermute | solution.py:26
  17.1 2.4 %collective-permute-start.4 = (f32[8,192]{1,0:T(8,128)S(1)}, f32[8,192]{1,0:T(8,128)S(1)}, u32[]{:S(2)}, u32[]{:S(2)}) collective-permute-start(f32[8,192]{1,0:T(8,128)S(1)} %get-tuple-element.28.s0), channel_id=1, source_target_pairs={{2,0},{3,1},{0,2},{1,3},{6,4},{7,5},{4,6},{5,7},{10,8},{11,9},{8,1... | collective-permute-start | bytes 18440 | tf_op jit(solution)/shard_map/ppermute | solution.py:26
  19.5 1.6 %collective-permute-start.5 = (f32[8,192]{1,0:T(8,128)S(1)}, f32[8,192]{1,0:T(8,128)S(1)}, u32[]{:S(2)}, u32[]{:S(2)}) collective-permute-start(f32[8,192]{1,0:T(8,128)S(1)} %get-tuple-element.28.s0), channel_id=1, source_target_pairs={{1,0},{2,1},{3,2},{0,3},{5,4},{6,5},{7,6},{4,7},{9,8},{10,9},{11,1... | collective-permute-start | bytes 18440 | tf_op jit(solution)/shard_map/ppermute | solution.py:26
  21.0 1.2 %collective-permute-done.4.s2 = f32[8,192]{1,0:T(8,128)S(1)} collective-permute-done((f32[8,192]{1,0:T(8,128)S(1)}, f32[8,192]{1,0:T(8,128)S(1)}, u32[]{:S(2)}, u32[]{:S(2)}) %collective-permute-start.4) | collective-permute-done | bytes 6176 | tf_op jit(solution)/shard_map/ppermute | solution.py:26
  22.2 0.9 collective-permute-done.5.s3
  23.4 2.0 %collective-permute-start.6 = (bf16[2,192,384]{2,1,0:T(8,128)(2,1)S(1)}, bf16[2,192,384]{2,1,0:T(8,128)(2,1)S(1)}, u32[]{:S(2)}, u32[]{:S(2)}) collective-permute-start(bf16[2,192,384]{2,1,0:T(8,128)(2,1)S(1)} %pad_maximum_fusion), channel_id=1, source_target_pairs={{224,0},{228,4},{232,8},{236,12},{240,16},{244,20},{248,24},{252,2... | collective-permute-start | bytes 884744 | tf_op jit(solution)/shard_map/ppermute | solution.py:292
  25.4 4.0 %collective-permute-start.7 = (bf16[2,192,384]{2,1,0:T(8,128)(2,1)S(1)}, bf16[2,192,384]{2,1,0:T(8,128)(2,1)S(1)}, u32[]{:S(2)}, u32[]{:S(2)}) collective-permute-start(bf16[2,192,384]{2,1,0:T(8,128)(2,1)S(1)} %pad_maximum_fusion), channel_id=1, source_target_pairs={{32,0},{36,4},{40,8},{44,12},{48,16},{52,20},{56,24},{60,28},{64,3... | collective-permute-start | bytes 884744 | tf_op jit(solution)/shard_map/ppermute | solution.py:292
  29.5 0.7 collective-permute-start.8
  30.2 0.5 collective-permute-start.16
  30.9 7.2 %collective-permute-done.8 = bf16[192,384]{1,0:T(8,128)(2,1)S(1)} collective-permute-done((bf16[192,384]{1,0:T(8,128)(2,1)S(1)}, bf16[192,384]{1,0:T(8,128)(2,1)S(1)}, u32[]{:S(2)}, u32[]{:S(2)}) %collective-permute-start.8) | collective-permute-done | bytes 147488 | tf_op jit(solution)/shard_map/ppermute | solution.py:26
  38.5 1.4 %collective-permute-start.10 = (bf16[2,192,384]{2,1,0:T(8,128)(2,1)S(1)}, bf16[2,192,384]{2,1,0:T(8,128)(2,1)S(1)}, u32[]{:S(2)}, u32[]{:S(2)}) collective-permute-start(bf16[2,192,384]{2,1,0:T(8,128)(2,1)S(1)} %collective-permute-done.6), channel_id=1, source_target_pairs={{224,0},{228,4},{232,8},{236,12},{240,16},{244,20},{248,24},{252,2... | collective-permute-start | bytes 884744 | tf_op jit(solution)/shard_map/ppermute | solution.py:296
  39.8 2.3 %collective-permute-start.13 = (bf16[2,192,384]{2,1,0:T(8,128)(2,1)S(1)}, bf16[2,192,384]{2,1,0:T(8,128)(2,1)S(1)}, u32[]{:S(2)}, u32[]{:S(2)}) collective-permute-start(bf16[2,192,384]{2,1,0:T(8,128)(2,1)S(1)} %collective-permute-done.7), channel_id=1, source_target_pairs={{32,0},{36,4},{40,8},{44,12},{48,16},{52,20},{56,24},{60,28},{64,3... | collective-permute-start | bytes 884744 | tf_op jit(solution)/shard_map/ppermute | solution.py:296
  42.4 4.4 %collective-permute-start.18 = (bf16[2,192,384]{2,1,0:T(8,128)(2,1)S(1)}, bf16[2,192,384]{2,1,0:T(8,128)(2,1)S(1)}, u32[]{:S(2)}, u32[]{:S(2)}) collective-permute-start(bf16[2,192,384]{2,1,0:T(8,128)(2,1)S(1)} %pad_maximum_fusion.1.refs_0_), channel_id=1, source_target_pairs={{16,0},{20,4},{24,8},{28,12},{0,16},{4,20},{8,24},{12,28},{48,32},... | collective-permute-start | bytes 884744 | tf_op jit(solution)/shard_map/ppermute | solution.py:298
  46.9 0.8 collective-permute-done.10
  47.7 1.9 %collective-permute-start.11 = (bf16[2,192,384]{2,1,0:T(8,128)(2,1)S(1)}, bf16[2,192,384]{2,1,0:T(8,128)(2,1)S(1)}, u32[]{:S(2)}, u32[]{:S(2)}) collective-permute-start(bf16[2,192,384]{2,1,0:T(8,128)(2,1)S(1)} %collective-permute-done.10), channel_id=1, source_target_pairs={{224,0},{228,4},{232,8},{236,12},{240,16},{244,20},{248,24},{252,2... | collective-permute-start | bytes 884744 | tf_op jit(solution)/shard_map/ppermute | solution.py:300
  49.6 0.5 collective-permute-done.13
  50.0 1.2 %collective-permute-start.14 = (bf16[2,192,384]{2,1,0:T(8,128)(2,1)S(1)}, bf16[2,192,384]{2,1,0:T(8,128)(2,1)S(1)}, u32[]{:S(2)}, u32[]{:S(2)}) collective-permute-start(bf16[2,192,384]{2,1,0:T(8,128)(2,1)S(1)} %collective-permute-done.13), channel_id=1, source_target_pairs={{32,0},{36,4},{40,8},{44,12},{48,16},{52,20},{56,24},{60,28},{64,3... | collective-permute-start | bytes 884744 | tf_op jit(solution)/shard_map/ppermute | solution.py:300
  51.4 6.0 %collective-permute-done.11 = bf16[2,192,384]{2,1,0:T(8,128)(2,1)S(1)} collective-permute-done((bf16[2,192,384]{2,1,0:T(8,128)(2,1)S(1)}, bf16[2,192,384]{2,1,0:T(8,128)(2,1)S(1)}, u32[]{:S(2)}, u32[]{:S(2)}) %collective-permute-start.11) | collective-permute-done | bytes 294944 | tf_op jit(solution)/shard_map/ppermute | solution.py:300
  57.4 0.7 collective-permute-start.19
  58.2 2.4 %collective-permute-done.14 = bf16[2,192,384]{2,1,0:T(8,128)(2,1)S(1)} collective-permute-done((bf16[2,192,384]{2,1,0:T(8,128)(2,1)S(1)}, bf16[2,192,384]{2,1,0:T(8,128)(2,1)S(1)}, u32[]{:S(2)}, u32[]{:S(2)}) %collective-permute-start.14) | collective-permute-done | bytes 294944 | tf_op jit(solution)/shard_map/ppermute | solution.py:300
  60.6 2.5 %collective-permute-start.12 = (bf16[192,384]{1,0:T(8,128)(2,1)S(1)}, bf16[192,384]{1,0:T(8,128)(2,1)S(1)}, u32[]{:S(2)}, u32[]{:S(2)}) collective-permute-start(bf16[192,384]{1,0:T(8,128)(2,1)S(1)} %get-tuple-element.54.refs_5_), channel_id=1, source_target_pairs={{224,0},{228,4},{232,8},{236,12},{240,16},{244,20},{248,24},{252,2... | collective-permute-start | bytes 442376 | tf_op jit(solution)/shard_map/ppermute | solution.py:307
  63.1 1.1 collective-permute-start.15
  64.1 2.9 %collective-permute-done.19.refs_3_ = bf16[2,192,384]{2,1,0:T(8,128)(2,1)S(1)} collective-permute-done((bf16[2,192,384]{2,1,0:T(8,128)(2,1)S(1)}, bf16[2,192,384]{2,1,0:T(8,128)(2,1)S(1)}, u32[]{:S(2)}, u32[]{:S(2)}) %collective-permute-start.19) | collective-permute-done | bytes 294944 | tf_op jit(solution)/shard_map/ppermute | solution.py:298
  67.1 5.7 %shard_map.93 = (bf16[4,208,384]{2,1,0:T(8,128)(2,1)S(1)}, bf16[4,208,384]{2,1,0:T(8,128)(2,1)S(1)}) custom-call(f32[16]{0:T(128)S(1)} %stack.139.flags, bf16[2,192,384]{2,1,0:T(8,128)(2,1)S(1)} %pad_maximum_fusion.1.refs_0_, bf16[2,192,384]{2,1,0:T(8,128)(2,1)S(1)} %collective-permute-done.17.refs_1_, ...), custom_call_target="tpu_custom_call" | custom-call | flops 1811939328 | bytes 1048576 | tf_op jit(solution)/shard_map/pallas_call | solution.py:204
  72.8 5.7 %shard_map.94 = (bf16[4,208,384]{2,1,0:T(8,128)(2,1)S(1)}, bf16[4,208,384]{2,1,0:T(8,128)(2,1)S(1)}) custom-call(f32[16]{0:T(128)S(1)} %stack.159.flags, bf16[2,192,384]{2,1,0:T(8,128)(2,1)S(1)} %pad_maximum_fusion.1.refs_0_, bf16[2,192,384]{2,1,0:T(8,128)(2,1)S(1)} %collective-permute-done.17.refs_1_, ...), custom_call_target="tpu_custom_call" | custom-call | flops 1811939328 | bytes 1048576 | tf_op jit(solution)/shard_map/pallas_call | solution.py:204
  78.5 0.6 shard_map.95
  79.1 0.7 collective-permute-start.20
  79.8 1.7 %collective-permute-done.20.refs_2_ = bf16[4,208,384]{2,1,0:T(8,128)(2,1)S(1)} collective-permute-done((bf16[4,208,384]{2,1,0:T(8,128)(2,1)S(1)}, bf16[4,208,384]{2,1,0:T(8,128)(2,1)S(1)}, u32[]{:S(2)}, u32[]{:S(2)}) %collective-permute-start.20) | collective-permute-done | bytes 639008 | tf_op jit(solution)/shard_map/ppermute | solution.py:312
  81.5 0.7 shard_map.96
  82.3 2.0 %collective-permute-start.21 = (bf16[208,384]{1,0:T(8,128)(2,1)S(1)}, bf16[208,384]{1,0:T(8,128)(2,1)S(1)}, u32[]{:S(2)}, u32[]{:S(2)}) collective-permute-start(bf16[208,384]{1,0:T(8,128)(2,1)S(1)} %get-tuple-element.51), channel_id=1, source_target_pairs={{24,0},{28,4},{0,8},{4,12},{8,16},{12,20},{16,24},{20,28},{56,32},... | collective-permute-start | bytes 479240 | tf_op jit(solution)/shard_map/ppermute | solution.py:314
  84.3 1.0 collective-permute-start.23
  85.3 4.0 %collective-permute-done.21.b = bf16[208,384]{1,0:T(8,128)(2,1)S(1)} collective-permute-done((bf16[208,384]{1,0:T(8,128)(2,1)S(1)}, bf16[208,384]{1,0:T(8,128)(2,1)S(1)}, u32[]{:S(2)}, u32[]{:S(2)}) %collective-permute-start.21) | collective-permute-done | bytes 159776 | tf_op jit(solution)/shard_map/ppermute | solution.py:314
  89.3 3.5 %collective-permute-done.22.c = bf16[208,384]{1,0:T(8,128)(2,1)S(1)} collective-permute-done((bf16[208,384]{1,0:T(8,128)(2,1)S(1)}, bf16[208,384]{1,0:T(8,128)(2,1)S(1)}, u32[]{:S(2)}, u32[]{:S(2)}) %collective-permute-start.22) | collective-permute-done | bytes 159776 | tf_op jit(solution)/shard_map/ppermute | solution.py:314
  92.8 2.0 %collective-permute-done.23.d = bf16[208,384]{1,0:T(8,128)(2,1)S(1)} collective-permute-done((bf16[208,384]{1,0:T(8,128)(2,1)S(1)}, bf16[208,384]{1,0:T(8,128)(2,1)S(1)}, u32[]{:S(2)}, u32[]{:S(2)}) %collective-permute-start.23) | collective-permute-done | bytes 159776 | tf_op jit(solution)/shard_map/ppermute | solution.py:314
  94.8 0.9 shard_map.97
  95.7 0.5 collective-permute-start.24
  96.2 3.4 %collective-permute-start.25 = (bf16[192,384]{1,0:T(8,128)(2,1)S(1)}, bf16[192,384]{1,0:T(8,128)(2,1)S(1)}, u32[]{:S(2)}, u32[]{:S(2)}) collective-permute-start(bf16[192,384]{1,0:T(8,128)(2,1)S(1)} %get-tuple-element.45), channel_id=1, source_target_pairs={{2,0},{3,1},{0,2},{1,3},{6,4},{7,5},{4,6},{5,7},{10,8},{11,9},{8,1... | collective-permute-start | bytes 442376 | tf_op jit(solution)/shard_map/ppermute | solution.py:26
  101.9 0.8 dynamic-slice_reduce_fusion
  103.1 3.2 %collective-permute-done.25 = bf16[192,384]{1,0:T(8,128)(2,1)S(1)} collective-permute-done((bf16[192,384]{1,0:T(8,128)(2,1)S(1)}, bf16[192,384]{1,0:T(8,128)(2,1)S(1)}, u32[]{:S(2)}, u32[]{:S(2)}) %collective-permute-start.25) | collective-permute-done | bytes 147488 | tf_op jit(solution)/shard_map/ppermute | solution.py:26
  106.3 0.8 fusion
  (39 shorter events, 2.2 us)
Async XLA Ops:
  0.0 21.0 %copy-start.3 = (f32[384]{0:T(512)S(1)}, f32[384]{0:T(512)}, u32[]{:S(2)}) copy-start(f32[384]{0:T(512)} %param.16) | copy-start | bytes 4612
  0.0 21.0 %copy-start.4 = (f32[384]{0:T(512)S(1)}, f32[384]{0:T(512)}, u32[]{:S(2)}) copy-start(f32[384]{0:T(512)} %param.17) | copy-start | bytes 4612
  0.0 10.4 %collective-permute-start = (bf16[192,384]{1,0:T(8,128)(2,1)}, bf16[192,384]{1,0:T(8,128)(2,1)S(1)}, u32[]{:S(2)}, u32[]{:S(2)}) collective-permute-start(bf16[192,384]{1,0:T(8,128)(2,1)} %own.1), channel_id=1, source_target_pairs={{3,0},{0,1},{1,2},{2,3},{7,4},{4,5},{5,6},{6,7},{11,8},{8,9},{9,10... | collective-permute-start | bytes 442376 | tf_op jit(solution)/shard_map/ppermute | solution.py:26
  1.5 9.7 %collective-permute-start.1 = (bf16[192,384]{1,0:T(8,128)(2,1)}, bf16[192,384]{1,0:T(8,128)(2,1)S(1)}, u32[]{:S(2)}, u32[]{:S(2)}) collective-permute-start(bf16[192,384]{1,0:T(8,128)(2,1)} %own.1), channel_id=1, source_target_pairs={{2,0},{3,1},{0,2},{1,3},{6,4},{7,5},{4,6},{5,7},{10,8},{11,9},{8,1... | collective-permute-start | bytes 442376 | tf_op jit(solution)/shard_map/ppermute | solution.py:26
  4.2 6.9 %collective-permute-start.2 = (bf16[192,384]{1,0:T(8,128)(2,1)}, bf16[192,384]{1,0:T(8,128)(2,1)S(1)}, u32[]{:S(2)}, u32[]{:S(2)}) collective-permute-start(bf16[192,384]{1,0:T(8,128)(2,1)} %own.1), channel_id=1, source_target_pairs={{1,0},{2,1},{3,2},{0,3},{5,4},{6,5},{7,6},{4,7},{9,8},{10,9},{11,1... | collective-permute-start | bytes 442376 | tf_op jit(solution)/shard_map/ppermute | solution.py:26
  11.2 2.0 %copy-start = (bf16[1536,3,384]{2,0,1:T(8,128)(2,1)S(1)}, bf16[1536,3,384]{2,0,1:T(8,128)(2,1)}, u32[]{:S(2)}) copy-start(bf16[1536,3,384]{2,0,1:T(8,128)(2,1)} %param.14) | copy-start | bytes 10616836
  15.6 5.4 %collective-permute-start.3 = (f32[8,192]{1,0:T(8,128)S(1)}, f32[8,192]{1,0:T(8,128)S(1)}, u32[]{:S(2)}, u32[]{:S(2)}) collective-permute-start(f32[8,192]{1,0:T(8,128)S(1)} %get-tuple-element.28.s0), channel_id=1, source_target_pairs={{3,0},{0,1},{1,2},{2,3},{7,4},{4,5},{5,6},{6,7},{11,8},{8,9},{9,10... | collective-permute-start | bytes 18440 | tf_op jit(solution)/shard_map/ppermute | solution.py:26
  17.1 5.2 %collective-permute-start.4 = (f32[8,192]{1,0:T(8,128)S(1)}, f32[8,192]{1,0:T(8,128)S(1)}, u32[]{:S(2)}, u32[]{:S(2)}) collective-permute-start(f32[8,192]{1,0:T(8,128)S(1)} %get-tuple-element.28.s0), channel_id=1, source_target_pairs={{2,0},{3,1},{0,2},{1,3},{6,4},{7,5},{4,6},{5,7},{10,8},{11,9},{8,1... | collective-permute-start | bytes 18440 | tf_op jit(solution)/shard_map/ppermute | solution.py:26
  19.5 3.7 %collective-permute-start.5 = (f32[8,192]{1,0:T(8,128)S(1)}, f32[8,192]{1,0:T(8,128)S(1)}, u32[]{:S(2)}, u32[]{:S(2)}) collective-permute-start(f32[8,192]{1,0:T(8,128)S(1)} %get-tuple-element.28.s0), channel_id=1, source_target_pairs={{1,0},{2,1},{3,2},{0,3},{5,4},{6,5},{7,6},{4,7},{9,8},{10,9},{11,1... | collective-permute-start | bytes 18440 | tf_op jit(solution)/shard_map/ppermute | solution.py:26
  23.4 15.0 %collective-permute-start.6 = (bf16[2,192,384]{2,1,0:T(8,128)(2,1)S(1)}, bf16[2,192,384]{2,1,0:T(8,128)(2,1)S(1)}, u32[]{:S(2)}, u32[]{:S(2)}) collective-permute-start(bf16[2,192,384]{2,1,0:T(8,128)(2,1)S(1)} %pad_maximum_fusion), channel_id=1, source_target_pairs={{224,0},{228,4},{232,8},{236,12},{240,16},{244,20},{248,24},{252,2... | collective-permute-start | bytes 884744 | tf_op jit(solution)/shard_map/ppermute | solution.py:292
  25.4 13.0 %collective-permute-start.7 = (bf16[2,192,384]{2,1,0:T(8,128)(2,1)S(1)}, bf16[2,192,384]{2,1,0:T(8,128)(2,1)S(1)}, u32[]{:S(2)}, u32[]{:S(2)}) collective-permute-start(bf16[2,192,384]{2,1,0:T(8,128)(2,1)S(1)} %pad_maximum_fusion), channel_id=1, source_target_pairs={{32,0},{36,4},{40,8},{44,12},{48,16},{52,20},{56,24},{60,28},{64,3... | collective-permute-start | bytes 884744 | tf_op jit(solution)/shard_map/ppermute | solution.py:292
  29.5 8.7 %collective-permute-start.8 = (bf16[192,384]{1,0:T(8,128)(2,1)S(1)}, bf16[192,384]{1,0:T(8,128)(2,1)S(1)}, u32[]{:S(2)}, u32[]{:S(2)}) collective-permute-start(bf16[192,384]{1,0:T(8,128)(2,1)S(1)} %get-tuple-element.31), channel_id=1, source_target_pairs={{8,0},{12,4},{16,8},{20,12},{24,16},{28,20},{32,24},{36,28},{40,32... | collective-permute-start | bytes 442376 | tf_op jit(solution)/shard_map/ppermute | solution.py:26
  30.2 8.3 %collective-permute-start.9 = (bf16[192,384]{1,0:T(8,128)(2,1)S(1)}, bf16[192,384]{1,0:T(8,128)(2,1)S(1)}, u32[]{:S(2)}, u32[]{:S(2)}) collective-permute-start(bf16[192,384]{1,0:T(8,128)(2,1)S(1)} %get-tuple-element.31), channel_id=1, source_target_pairs={{12,0},{8,4},{20,8},{16,12},{28,16},{24,20},{36,24},{32,28},{44,32... | collective-permute-start | bytes 442376 | tf_op jit(solution)/shard_map/ppermute | solution.py:293
  30.2 42.6 %collective-permute-start.16 = (bf16[192,384]{1,0:T(8,128)(2,1)}, bf16[192,384]{1,0:T(8,128)(2,1)S(1)}, u32[]{:S(2)}, u32[]{:S(2)}) collective-permute-start(bf16[192,384]{1,0:T(8,128)(2,1)} %own.1), channel_id=1, source_target_pairs={{8,0},{12,4},{16,8},{20,12},{24,16},{28,20},{32,24},{36,28},{40,32... | collective-permute-start | bytes 442376 | tf_op jit(solution)/shard_map/ppermute | solution.py:26
  38.5 9.2 %collective-permute-start.10 = (bf16[2,192,384]{2,1,0:T(8,128)(2,1)S(1)}, bf16[2,192,384]{2,1,0:T(8,128)(2,1)S(1)}, u32[]{:S(2)}, u32[]{:S(2)}) collective-permute-start(bf16[2,192,384]{2,1,0:T(8,128)(2,1)S(1)} %collective-permute-done.6), channel_id=1, source_target_pairs={{224,0},{228,4},{232,8},{236,12},{240,16},{244,20},{248,24},{252,2... | collective-permute-start | bytes 884744 | tf_op jit(solution)/shard_map/ppermute | solution.py:296
  39.8 10.2 %collective-permute-start.13 = (bf16[2,192,384]{2,1,0:T(8,128)(2,1)S(1)}, bf16[2,192,384]{2,1,0:T(8,128)(2,1)S(1)}, u32[]{:S(2)}, u32[]{:S(2)}) collective-permute-start(bf16[2,192,384]{2,1,0:T(8,128)(2,1)S(1)} %collective-permute-done.7), channel_id=1, source_target_pairs={{32,0},{36,4},{40,8},{44,12},{48,16},{52,20},{56,24},{60,28},{64,3... | collective-permute-start | bytes 884744 | tf_op jit(solution)/shard_map/ppermute | solution.py:296
  42.1 20.9 %collective-permute-start.17 = (bf16[2,192,384]{2,1,0:T(8,128)(2,1)S(1)}, bf16[2,192,384]{2,1,0:T(8,128)(2,1)S(1)}, u32[]{:S(2)}, u32[]{:S(2)}) collective-permute-start(bf16[2,192,384]{2,1,0:T(8,128)(2,1)S(1)} %pad_maximum_fusion.1.refs_0_), channel_id=1, source_target_pairs={{8,0},{12,4},{16,8},{20,12},{24,16},{28,20},{0,24},{4,28},{40,32},... | collective-permute-start | bytes 884744 | tf_op jit(solution)/shard_map/ppermute | solution.py:298
  42.4 21.7 %collective-permute-start.18 = (bf16[2,192,384]{2,1,0:T(8,128)(2,1)S(1)}, bf16[2,192,384]{2,1,0:T(8,128)(2,1)S(1)}, u32[]{:S(2)}, u32[]{:S(2)}) collective-permute-start(bf16[2,192,384]{2,1,0:T(8,128)(2,1)S(1)} %pad_maximum_fusion.1.refs_0_), channel_id=1, source_target_pairs={{16,0},{20,4},{24,8},{28,12},{0,16},{4,20},{8,24},{12,28},{48,32},... | collective-permute-start | bytes 884744 | tf_op jit(solution)/shard_map/ppermute | solution.py:298
  47.7 9.7 %collective-permute-start.11 = (bf16[2,192,384]{2,1,0:T(8,128)(2,1)S(1)}, bf16[2,192,384]{2,1,0:T(8,128)(2,1)S(1)}, u32[]{:S(2)}, u32[]{:S(2)}) collective-permute-start(bf16[2,192,384]{2,1,0:T(8,128)(2,1)S(1)} %collective-permute-done.10), channel_id=1, source_target_pairs={{224,0},{228,4},{232,8},{236,12},{240,16},{244,20},{248,24},{252,2... | collective-permute-start | bytes 884744 | tf_op jit(solution)/shard_map/ppermute | solution.py:300
  50.0 10.5 %collective-permute-start.14 = (bf16[2,192,384]{2,1,0:T(8,128)(2,1)S(1)}, bf16[2,192,384]{2,1,0:T(8,128)(2,1)S(1)}, u32[]{:S(2)}, u32[]{:S(2)}) collective-permute-start(bf16[2,192,384]{2,1,0:T(8,128)(2,1)S(1)} %collective-permute-done.13), channel_id=1, source_target_pairs={{32,0},{36,4},{40,8},{44,12},{48,16},{52,20},{56,24},{60,28},{64,3... | collective-permute-start | bytes 884744 | tf_op jit(solution)/shard_map/ppermute | solution.py:300
  57.4 9.7 %collective-permute-start.19 = (bf16[2,192,384]{2,1,0:T(8,128)(2,1)S(1)}, bf16[2,192,384]{2,1,0:T(8,128)(2,1)S(1)}, u32[]{:S(2)}, u32[]{:S(2)}) collective-permute-start(bf16[2,192,384]{2,1,0:T(8,128)(2,1)S(1)} %pad_maximum_fusion.1.refs_0_), channel_id=1, source_target_pairs={{24,0},{28,4},{0,8},{4,12},{8,16},{12,20},{16,24},{20,28},{56,32},... | collective-permute-start | bytes 884744 | tf_op jit(solution)/shard_map/ppermute | solution.py:298
  60.6 12.2 %collective-permute-start.12 = (bf16[192,384]{1,0:T(8,128)(2,1)S(1)}, bf16[192,384]{1,0:T(8,128)(2,1)S(1)}, u32[]{:S(2)}, u32[]{:S(2)}) collective-permute-start(bf16[192,384]{1,0:T(8,128)(2,1)S(1)} %get-tuple-element.54.refs_5_), channel_id=1, source_target_pairs={{224,0},{228,4},{232,8},{236,12},{240,16},{244,20},{248,24},{252,2... | collective-permute-start | bytes 442376 | tf_op jit(solution)/shard_map/ppermute | solution.py:307
  63.1 9.7 %collective-permute-start.15 = (bf16[192,384]{1,0:T(8,128)(2,1)S(1)}, bf16[192,384]{1,0:T(8,128)(2,1)S(1)}, u32[]{:S(2)}, u32[]{:S(2)}) collective-permute-start(bf16[192,384]{1,0:T(8,128)(2,1)S(1)} %get-tuple-element.57.refs_10_), channel_id=1, source_target_pairs={{32,0},{36,4},{40,8},{44,12},{48,16},{52,20},{56,24},{60,28},{64,3... | collective-permute-start | bytes 442376 | tf_op jit(solution)/shard_map/ppermute | solution.py:308
  79.1 15.8 %copy-start.1 = (bf16[384,1536]{1,0:T(8,128)(2,1)S(1)}, bf16[384,1536]{1,0:T(8,128)(2,1)}, u32[]{:S(2)}) copy-start(bf16[384,1536]{1,0:T(8,128)(2,1)} %w_ref.1) | copy-start | bytes 3538948
  79.1 2.4 %collective-permute-start.20 = (bf16[4,208,384]{2,1,0:T(8,128)(2,1)S(1)}, bf16[4,208,384]{2,1,0:T(8,128)(2,1)S(1)}, u32[]{:S(2)}, u32[]{:S(2)}) collective-permute-start(bf16[4,208,384]{2,1,0:T(8,128)(2,1)S(1)} %shard_map.95), channel_id=1, source_target_pairs={{0,4},{4,0},{8,12},{12,8},{16,20},{20,16},{24,28},{28,24},{32,36},... | collective-permute-start | bytes 1916936 | tf_op jit(solution)/shard_map/ppermute | solution.py:312
  81.5 24.8 %copy-start.2 = (bf16[384,384]{1,0:T(8,128)(2,1)S(1)}, bf16[384,384]{1,0:T(8,128)(2,1)}, u32[]{:S(2)}) copy-start(bf16[384,384]{1,0:T(8,128)(2,1)} %param.10) | copy-start | bytes 884740
  82.3 7.0 %collective-permute-start.21 = (bf16[208,384]{1,0:T(8,128)(2,1)S(1)}, bf16[208,384]{1,0:T(8,128)(2,1)S(1)}, u32[]{:S(2)}, u32[]{:S(2)}) collective-permute-start(bf16[208,384]{1,0:T(8,128)(2,1)S(1)} %get-tuple-element.51), channel_id=1, source_target_pairs={{24,0},{28,4},{0,8},{4,12},{8,16},{12,20},{16,24},{20,28},{56,32},... | collective-permute-start | bytes 479240 | tf_op jit(solution)/shard_map/ppermute | solution.py:314
  84.3 8.5 %collective-permute-start.22 = (bf16[208,384]{1,0:T(8,128)(2,1)S(1)}, bf16[208,384]{1,0:T(8,128)(2,1)S(1)}, u32[]{:S(2)}, u32[]{:S(2)}) collective-permute-start(bf16[208,384]{1,0:T(8,128)(2,1)S(1)} %get-tuple-element.50), channel_id=1, source_target_pairs={{16,0},{20,4},{24,8},{28,12},{0,16},{4,20},{8,24},{12,28},{48,32},... | collective-permute-start | bytes 479240 | tf_op jit(solution)/shard_map/ppermute | solution.py:314
  84.3 10.5 %collective-permute-start.23 = (bf16[208,384]{1,0:T(8,128)(2,1)S(1)}, bf16[208,384]{1,0:T(8,128)(2,1)S(1)}, u32[]{:S(2)}, u32[]{:S(2)}) collective-permute-start(bf16[208,384]{1,0:T(8,128)(2,1)S(1)} %get-tuple-element.49), channel_id=1, source_target_pairs={{8,0},{12,4},{16,8},{20,12},{24,16},{28,20},{0,24},{4,28},{40,32},... | collective-permute-start | bytes 479240 | tf_op jit(solution)/shard_map/ppermute | solution.py:314
  95.7 7.4 %collective-permute-start.24 = (bf16[192,384]{1,0:T(8,128)(2,1)S(1)}, bf16[192,384]{1,0:T(8,128)(2,1)S(1)}, u32[]{:S(2)}, u32[]{:S(2)}) collective-permute-start(bf16[192,384]{1,0:T(8,128)(2,1)S(1)} %get-tuple-element.44), channel_id=1, source_target_pairs={{3,0},{0,1},{1,2},{2,3},{7,4},{4,5},{5,6},{6,7},{11,8},{8,9},{9,10... | collective-permute-start | bytes 442376 | tf_op jit(solution)/shard_map/ppermute | solution.py:26
  96.2 10.0 %collective-permute-start.25 = (bf16[192,384]{1,0:T(8,128)(2,1)S(1)}, bf16[192,384]{1,0:T(8,128)(2,1)S(1)}, u32[]{:S(2)}, u32[]{:S(2)}) collective-permute-start(bf16[192,384]{1,0:T(8,128)(2,1)S(1)} %get-tuple-element.45), channel_id=1, source_target_pairs={{2,0},{3,1},{0,2},{1,3},{6,4},{7,5},{4,6},{5,7},{10,8},{11,9},{8,1... | collective-permute-start | bytes 442376 | tf_op jit(solution)/shard_map/ppermute | solution.py:26
  99.7 6.6 %collective-permute-start.26 = (bf16[192,384]{1,0:T(8,128)(2,1)S(1)}, bf16[192,384]{1,0:T(8,128)(2,1)S(1)}, u32[]{:S(2)}, u32[]{:S(2)}) collective-permute-start(bf16[192,384]{1,0:T(8,128)(2,1)S(1)} %get-tuple-element.46), channel_id=1, source_target_pairs={{1,0},{2,1},{3,2},{0,3},{5,4},{6,5},{7,6},{4,7},{9,8},{10,9},{11,1... | collective-permute-start | bytes 442376 | tf_op jit(solution)/shard_map/ppermute | solution.py:26

commit v3 on v2

--- a/solution.py
+++ b/solution.py
@@ -41,6 +41,10 @@
     for j, column in enumerate(columns):
         out = jnp.where(lane == j, column, out)
     return out
+
+
+def early_kernel(w_in, w_out):
+    w_out[...] = w_in[...]
 
 
 def project_kernel(x_ref, own, one, two, three, scale_ref, shift_ref, w_ref, q_ref, k_ref, v_ref, sums_ref):
@@ -205,7 +209,7 @@
         functools.partial(attend_kernel, slabs),
         [SMEM] + [VMEM] * (slots + 2 * slabs),
         [shape((slots, rows + TAIL, width), jnp.bfloat16)] * 2,
-        scores * DH * 4,
+        scores * DH * 14,
         1 << 20,
         scores,
     )(flags, *queries, *keys, *values)
@@ -239,6 +243,7 @@
     gate = lax.dynamic_slice(mod_table, (home_level, 2, x * width), (1, 1, width)).reshape(1, width)
     modulation = modulation.reshape(3, heads_ax, 1, width)
     w3 = jnp.transpose(w_qkv, (1, 0, 2))
+    w_near = call(early_kernel, [VMEM], shape(w3.shape, jnp.bfloat16), 0, 8 << 20)(w3)
     q, k, v, sums = call(
         project_kernel,
         [SMEM] + [VMEM] * 7,
@@ -250,7 +255,7 @@
         ],
         2 * rows * D * 3 * width,
         6 << 20,
-    )(x_arg, latents, *chunks, modulation[1], modulation[0], w3)
+    )(x_arg, latents, *chunks, modulation[1], modulation[0], w_near)
     all_sums = [sums] + [shift(sums, "head", j) for j in range(1, heads_ax)]
     qn, kn = call(
         norm_kernel,
@@ -298,6 +303,7 @@
     qs = [home_q] + [lax.ppermute(home_q, "queue", y_route(-j)) for j in range(1, NY)]
     for way in (1, -1):
         both[way * 3] = lax.ppermute(both[way * 2], "queue", key_route(way))
+    both[3], both[-3], qs = lax.optimization_barrier((both[3], both[-3], qs))
     ks = {d: b[0] for d, b in both.items()}
     vs = {d: b[1] for d, b in both.items()}
 

time: 108 us -> 106 us (0.981)
  starting transfers between devices: 41.9 us -> 40.2 us
  waiting for transfers between devices: 37.9 us -> 36.4 us
    ppermute x2, waiting for transfers between devices: 8.43 us -> 0.01 us  [local(): both[way * 3] = lax.ppermute(both[way * 2], 'queue', key_route(way))]
    ppermute x3, waiting for transfers between devices: 2.93 us -> 7.56 us  [local(): lax.ppermute(home_q, 'queue', y_route(-j))]
    ppermute x2, waiting for transfers between devices: 1.25 us -> 3.6 us  [local(): both[way * 2] = lax.ppermute(both[way], 'queue', key_route(way))]
    ppermute x3, starting transfers between devices: 5.42 us -> 3.49 us  [local(): lax.ppermute(home_q, 'queue', y_route(-j))]
    ppermute x3, starting transfers between devices: 2.97 us -> 4.77 us  [local(): lax.ppermute(paired[j], 'queue', y_route(j))]
    ppermute x11, starting transfers between devices: 16.5 us -> 14.9 us  [shift(): lax.ppermute(block, axis, [((i - distance) % n, i) for i in range(n)])]
    ppermute x1, starting transfers between devices: 1.05 us -> 2.45 us  [local(): vs[4] = lax.ppermute(vs[-3], 'queue', key_route(-1))]
    ppermute x1, starting transfers between devices: 2.48 us -> 1.16 us  [local(): ks[4] = lax.ppermute(ks[3], 'queue', key_route(1))]
  transfers between devices with their start and end apart: 27 -> 27, of which waited for: 16 -> 13; matrix products, arithmetic and copies ran while one was open for 3% -> 3% of each run, Pallas kernels for 5% -> 6%
where the time goes in v3:
time: 106 us; the launch traced here: 105 us
  starting transfers between devices  40.2 us (38%)
  waiting for transfers between devices  36.4 us (34%)
  Pallas kernels  16.8 us (16%)
  local copies, waits for them, and re-layouts  6.38 us (6%)
  between operations  4.78 us (5%)
    ppermute x11, starting transfers between devices, shift(): lax.ppermute(block, axis, [((i - distance) % n, i) for i in range(n)])  14.9 us
    ppermute x11, waiting for transfers between devices, shift(): lax.ppermute(block, axis, [((i - distance) % n, i) for i in range(n)])  13.3 us
    pallas_call x2, Pallas kernels, attend(): call(functools.partial(attend_kernel, slabs), [SMEM] + [VMEM] * (slots +...  11.5 us
    ppermute x3, waiting for transfers between devices, local(): lax.ppermute(paired[j], 'queue', y_route(j))  9.55 us
    ppermute x3, waiting for transfers between devices, local(): lax.ppermute(home_q, 'queue', y_route(-j))  7.56 us
    ppermute x2, starting transfers between devices, local(): both[way] = lax.ppermute(both[0], 'queue', key_route(way))  6.02 us
    ppermute x3, starting transfers between devices, local(): lax.ppermute(paired[j], 'queue', y_route(j))  4.77 us
    ppermute x2, waiting for transfers between devices, local(): both[way * 2] = lax.ppermute(both[way], 'queue', key_route(way))  3.6 us
  transfers between devices with their start and end apart: 27, of which 13 were waited for; matrix products, arithmetic and copies ran while one was open for 3% of the time, Pallas kernels for 6%

profile of v3, /device:TPU:24, one launch (start us, length us, event | category | flops | bytes accessed | tf_op | source)
XLA Modules:
  0.0 105.4 jit_solution(14185893773783458546)
XLA Ops:
  0.0 1.5 %collective-permute-start = (bf16[192,384]{1,0:T(8,128)(2,1)}, bf16[192,384]{1,0:T(8,128)(2,1)}, u32[]{:S(2)}, u32[]{:S(2)}) collective-permute-start(bf16[192,384]{1,0:T(8,128)(2,1)} %own.1), channel_id=1, source_target_pairs={{3,0},{0,1},{1,2},{2,3},{7,4},{4,5},{5,6},{6,7},{11,8},{8,9},{9,10... | collective-permute-start | bytes 442376 | tf_op jit(solution)/shard_map/ppermute | solution.py:26
  1.5 2.7 %collective-permute-start.1 = (bf16[192,384]{1,0:T(8,128)(2,1)}, bf16[192,384]{1,0:T(8,128)(2,1)}, u32[]{:S(2)}, u32[]{:S(2)}) collective-permute-start(bf16[192,384]{1,0:T(8,128)(2,1)} %own.1), channel_id=1, source_target_pairs={{2,0},{3,1},{0,2},{1,3},{6,4},{7,5},{4,6},{5,7},{10,8},{11,9},{8,1... | collective-permute-start | bytes 442376 | tf_op jit(solution)/shard_map/ppermute | solution.py:26
  4.2 1.4 %collective-permute-start.2 = (bf16[192,384]{1,0:T(8,128)(2,1)}, bf16[192,384]{1,0:T(8,128)(2,1)}, u32[]{:S(2)}, u32[]{:S(2)}) collective-permute-start(bf16[192,384]{1,0:T(8,128)(2,1)} %own.1), channel_id=1, source_target_pairs={{1,0},{2,1},{3,2},{0,3},{5,4},{6,5},{7,6},{4,7},{9,8},{10,9},{11,1... | collective-permute-start | bytes 442376 | tf_op jit(solution)/shard_map/ppermute | solution.py:26
  6.4 1.3 %fusion.1 = (s32[1]{0:T(128)}, s32[1]{0:T(128)}) fusion(s32[32]{0:T(128)} %param.11, s32[]{:T(128)S(6)} %select_n.371, s32[]{:T(128)S(6)} %select_n.368), kind=kLoop, calls=%fused_computation.23 | loop fusion | bytes 24 | tf_op jit(solution)/shard_map/dynamic_slice | solution.py:242
  9.0 2.0 %copy-done = bf16[1536,3,384]{2,0,1:T(8,128)(2,1)S(1)} copy-done((bf16[1536,3,384]{2,0,1:T(8,128)(2,1)S(1)}, bf16[1536,3,384]{2,0,1:T(8,128)(2,1)}, u32[]{:S(2)}) %copy-start) | copy-done | bytes 3538968
  11.0 0.3 shard_map.91.w_ref
  12.0 0.8 constant_dynamic-slice_fusion.1
  12.9 0.9 copy-done.2
  13.8 2.6 %shard_map.92 = (f32[192,384]{1,0:T(8,128)S(1)}, f32[192,384]{1,0:T(8,128)S(1)}, bf16[192,384]{1,0:T(8,128)(2,1)S(1)}, f32[8,192]{1,0:T(8,128)S(1)}) custom-call(s32[1]{0:T(128)} %bitcast.1.x_ref, bf16[192,384]{1,0:T(8,128)(2,1)S(1)} %copy-done.2, bf16[192,384]{1,0:T(8,128)(2,1)} %collective-permute-done.one, bf16[192,384]{1,0:T(8,128)(2,1)} %collective-permute-done.1.two, ...), custom_call_target="tpu_custom_call" | custom-call | flops 679477248 | bytes 6291456 | tf_op jit(solution)/shard_map/pallas_call | solution.py:247
  16.4 0.7 collective-permute-start.3
  17.1 1.5 %collective-permute-start.4 = (f32[8,192]{1,0:T(8,128)S(1)}, f32[8,192]{1,0:T(8,128)S(1)}, u32[]{:S(2)}, u32[]{:S(2)}) collective-permute-start(f32[8,192]{1,0:T(8,128)S(1)} %get-tuple-element.34.s0), channel_id=1, source_target_pairs={{2,0},{3,1},{0,2},{1,3},{6,4},{7,5},{4,6},{5,7},{10,8},{11,9},{8,1... | collective-permute-start | bytes 18440 | tf_op jit(solution)/shard_map/ppermute | solution.py:26
  18.6 1.6 %collective-permute-start.5 = (f32[8,192]{1,0:T(8,128)S(1)}, f32[8,192]{1,0:T(8,128)S(1)}, u32[]{:S(2)}, u32[]{:S(2)}) collective-permute-start(f32[8,192]{1,0:T(8,128)S(1)} %get-tuple-element.34.s0), channel_id=1, source_target_pairs={{1,0},{2,1},{3,2},{0,3},{5,4},{6,5},{7,6},{4,7},{9,8},{10,9},{11,1... | collective-permute-start | bytes 18440 | tf_op jit(solution)/shard_map/ppermute | solution.py:26
  20.2 1.2 %collective-permute-done.3.s1 = f32[8,192]{1,0:T(8,128)S(1)} collective-permute-done((f32[8,192]{1,0:T(8,128)S(1)}, f32[8,192]{1,0:T(8,128)S(1)}, u32[]{:S(2)}, u32[]{:S(2)}) %collective-permute-start.3) | collective-permute-done | bytes 6176 | tf_op jit(solution)/shard_map/ppermute | solution.py:26
  21.4 0.9 collective-permute-done.4.s2
  22.3 0.3 shard_map.93
  22.7 2.0 %collective-permute-start.6 = (bf16[2,192,384]{2,1,0:T(8,128)(2,1)S(1)}, bf16[2,192,384]{2,1,0:T(8,128)(2,1)S(1)}, u32[]{:S(2)}, u32[]{:S(2)}) collective-permute-start(bf16[2,192,384]{2,1,0:T(8,128)(2,1)S(1)} %pad_maximum_fusion), channel_id=1, source_target_pairs={{224,0},{228,4},{232,8},{236,12},{240,16},{244,20},{248,24},{252,2... | collective-permute-start | bytes 884744 | tf_op jit(solution)/shard_map/ppermute | solution.py:297
  24.7 4.0 %collective-permute-start.7 = (bf16[2,192,384]{2,1,0:T(8,128)(2,1)S(1)}, bf16[2,192,384]{2,1,0:T(8,128)(2,1)S(1)}, u32[]{:S(2)}, u32[]{:S(2)}) collective-permute-start(bf16[2,192,384]{2,1,0:T(8,128)(2,1)S(1)} %pad_maximum_fusion), channel_id=1, source_target_pairs={{32,0},{36,4},{40,8},{44,12},{48,16},{52,20},{56,24},{60,28},{64,3... | collective-permute-start | bytes 884744 | tf_op jit(solution)/shard_map/ppermute | solution.py:297
  28.7 0.7 collective-permute-start.8
  29.6 7.7 %collective-permute-done.8 = bf16[192,384]{1,0:T(8,128)(2,1)S(1)} collective-permute-done((bf16[192,384]{1,0:T(8,128)(2,1)S(1)}, bf16[192,384]{1,0:T(8,128)(2,1)S(1)}, u32[]{:S(2)}, u32[]{:S(2)}) %collective-permute-start.8) | collective-permute-done | bytes 147488 | tf_op jit(solution)/shard_map/ppermute | solution.py:26
  37.4 0.3 collective-permute-done.9
  37.7 3.5 %collective-permute-start.12 = (bf16[2,192,384]{2,1,0:T(8,128)(2,1)S(1)}, bf16[2,192,384]{2,1,0:T(8,128)(2,1)S(1)}, u32[]{:S(2)}, u32[]{:S(2)}) collective-permute-start(bf16[2,192,384]{2,1,0:T(8,128)(2,1)S(1)} %collective-permute-done.7), channel_id=1, source_target_pairs={{32,0},{36,4},{40,8},{44,12},{48,16},{52,20},{56,24},{60,28},{64,3... | collective-permute-start | bytes 884744 | tf_op jit(solution)/shard_map/ppermute | solution.py:301
  41.2 0.3 collective-permute-start.14
  41.5 3.0 %collective-permute-start.15 = (bf16[2,192,384]{2,1,0:T(8,128)(2,1)S(1)}, bf16[2,192,384]{2,1,0:T(8,128)(2,1)S(1)}, u32[]{:S(2)}, u32[]{:S(2)}) collective-permute-start(bf16[2,192,384]{2,1,0:T(8,128)(2,1)S(1)} %pad_maximum_fusion.1.refs_0_), channel_id=1, source_target_pairs={{16,0},{20,4},{24,8},{28,12},{0,16},{4,20},{8,24},{12,28},{48,32},... | collective-permute-start | bytes 884744 | tf_op jit(solution)/shard_map/ppermute | solution.py:303
  44.5 0.3 collective-permute-start.16
  44.8 3.6 %collective-permute-done.10 = bf16[2,192,384]{2,1,0:T(8,128)(2,1)S(1)} collective-permute-done((bf16[2,192,384]{2,1,0:T(8,128)(2,1)S(1)}, bf16[2,192,384]{2,1,0:T(8,128)(2,1)S(1)}, u32[]{:S(2)}, u32[]{:S(2)}) %collective-permute-start.10) | collective-permute-done | bytes 294944 | tf_op jit(solution)/shard_map/ppermute | solution.py:301
  48.4 3.5 %collective-permute-start.13 = (bf16[2,192,384]{2,1,0:T(8,128)(2,1)S(1)}, bf16[2,192,384]{2,1,0:T(8,128)(2,1)S(1)}, u32[]{:S(2)}, u32[]{:S(2)}) collective-permute-start(bf16[2,192,384]{2,1,0:T(8,128)(2,1)S(1)} %collective-permute-done.12), channel_id=1, source_target_pairs={{32,0},{36,4},{40,8},{44,12},{48,16},{52,20},{56,24},{60,28},{64,3... | collective-permute-start | bytes 884744 | tf_op jit(solution)/shard_map/ppermute | solution.py:305
  52.0 6.8 %collective-permute-done.14.refs_1_ = bf16[2,192,384]{2,1,0:T(8,128)(2,1)S(1)} collective-permute-done((bf16[2,192,384]{2,1,0:T(8,128)(2,1)S(1)}, bf16[2,192,384]{2,1,0:T(8,128)(2,1)S(1)}, u32[]{:S(2)}, u32[]{:S(2)}) %collective-permute-start.14) | collective-permute-done | bytes 294944 | tf_op jit(solution)/shard_map/ppermute | solution.py:303
  58.9 0.7 collective-permute-done.16.refs_3_
  59.6 1.2 %collective-permute-start.17 = (bf16[192,384]{1,0:T(8,128)(2,1)S(1)}, bf16[192,384]{1,0:T(8,128)(2,1)S(1)}, u32[]{:S(2)}, u32[]{:S(2)}) collective-permute-start(bf16[192,384]{1,0:T(8,128)(2,1)S(1)} %get-tuple-element.66.refs_5_), channel_id=1, source_target_pairs={{224,0},{228,4},{232,8},{236,12},{240,16},{244,20},{248,24},{252,2... | collective-permute-start | bytes 442376 | tf_op jit(solution)/shard_map/ppermute | solution.py:313
  60.8 2.4 %collective-permute-start.18 = (bf16[192,384]{1,0:T(8,128)(2,1)S(1)}, bf16[192,384]{1,0:T(8,128)(2,1)S(1)}, u32[]{:S(2)}, u32[]{:S(2)}) collective-permute-start(bf16[192,384]{1,0:T(8,128)(2,1)S(1)} %get-tuple-element.69.refs_10_), channel_id=1, source_target_pairs={{32,0},{36,4},{40,8},{44,12},{48,16},{52,20},{56,24},{60,28},{64,3... | collective-permute-start | bytes 442376 | tf_op jit(solution)/shard_map/ppermute | solution.py:314
  63.3 5.8 %shard_map.94 = (bf16[4,208,384]{2,1,0:T(8,128)(2,1)S(1)}, bf16[4,208,384]{2,1,0:T(8,128)(2,1)S(1)}) custom-call(f32[16]{0:T(128)S(1)} %stack.142.flags, bf16[2,192,384]{2,1,0:T(8,128)(2,1)S(1)} %pad_maximum_fusion.1.refs_0_, bf16[2,192,384]{2,1,0:T(8,128)(2,1)S(1)} %collective-permute-done.14.refs_1_, ...), custom_call_target="tpu_custom_call" | custom-call | flops 6341787648 | bytes 1048576 | tf_op jit(solution)/shard_map/pallas_call | solution.py:208
  69.1 5.7 %shard_map.95 = (bf16[4,208,384]{2,1,0:T(8,128)(2,1)S(1)}, bf16[4,208,384]{2,1,0:T(8,128)(2,1)S(1)}) custom-call(f32[16]{0:T(128)S(1)} %stack.159.flags, bf16[2,192,384]{2,1,0:T(8,128)(2,1)S(1)} %pad_maximum_fusion.1.refs_0_, bf16[2,192,384]{2,1,0:T(8,128)(2,1)S(1)} %collective-permute-done.14.refs_1_, ...), custom_call_target="tpu_custom_call" | custom-call | flops 6341787648 | bytes 1048576 | tf_op jit(solution)/shard_map/pallas_call | solution.py:208
  74.8 0.6 shard_map.96
  75.4 0.4 collective-permute-start.20
  75.7 2.1 %collective-permute-done.20.refs_2_ = bf16[4,208,384]{2,1,0:T(8,128)(2,1)S(1)} collective-permute-done((bf16[4,208,384]{2,1,0:T(8,128)(2,1)S(1)}, bf16[4,208,384]{2,1,0:T(8,128)(2,1)S(1)}, u32[]{:S(2)}, u32[]{:S(2)}) %collective-permute-start.20) | collective-permute-done | bytes 639008 | tf_op jit(solution)/shard_map/ppermute | solution.py:318
  77.8 0.7 shard_map.97
  78.6 3.8 %collective-permute-start.21 = (bf16[208,384]{1,0:T(8,128)(2,1)S(1)}, bf16[208,384]{1,0:T(8,128)(2,1)S(1)}, u32[]{:S(2)}, u32[]{:S(2)}) collective-permute-start(bf16[208,384]{1,0:T(8,128)(2,1)S(1)} %get-tuple-element.63), channel_id=1, source_target_pairs={{24,0},{28,4},{0,8},{4,12},{8,16},{12,20},{16,24},{20,28},{56,32},... | collective-permute-start | bytes 479240 | tf_op jit(solution)/shard_map/ppermute | solution.py:320
  82.4 1.0 collective-permute-start.23
  83.3 6.1 %collective-permute-done.21.b = bf16[208,384]{1,0:T(8,128)(2,1)S(1)} collective-permute-done((bf16[208,384]{1,0:T(8,128)(2,1)S(1)}, bf16[208,384]{1,0:T(8,128)(2,1)S(1)}, u32[]{:S(2)}, u32[]{:S(2)}) %collective-permute-start.21) | collective-permute-done | bytes 159776 | tf_op jit(solution)/shard_map/ppermute | solution.py:320
  89.5 1.4 %collective-permute-done.22.c = bf16[208,384]{1,0:T(8,128)(2,1)S(1)} collective-permute-done((bf16[208,384]{1,0:T(8,128)(2,1)S(1)}, bf16[208,384]{1,0:T(8,128)(2,1)S(1)}, u32[]{:S(2)}, u32[]{:S(2)}) %collective-permute-start.22) | collective-permute-done | bytes 159776 | tf_op jit(solution)/shard_map/ppermute | solution.py:320
  90.9 2.0 %collective-permute-done.23.d = bf16[208,384]{1,0:T(8,128)(2,1)S(1)} collective-permute-done((bf16[208,384]{1,0:T(8,128)(2,1)S(1)}, bf16[208,384]{1,0:T(8,128)(2,1)S(1)}, u32[]{:S(2)}, u32[]{:S(2)}) %collective-permute-start.23) | collective-permute-done | bytes 159776 | tf_op jit(solution)/shard_map/ppermute | solution.py:320
  92.9 0.9 shard_map.98
  93.8 2.0 %collective-permute-start.24 = (bf16[192,384]{1,0:T(8,128)(2,1)S(1)}, bf16[192,384]{1,0:T(8,128)(2,1)S(1)}, u32[]{:S(2)}, u32[]{:S(2)}) collective-permute-start(bf16[192,384]{1,0:T(8,128)(2,1)S(1)} %get-tuple-element.56), channel_id=1, source_target_pairs={{3,0},{0,1},{1,2},{2,3},{7,4},{4,5},{5,6},{6,7},{11,8},{8,9},{9,10... | collective-permute-start | bytes 442376 | tf_op jit(solution)/shard_map/ppermute | solution.py:26
  95.8 2.3 %collective-permute-start.25 = (bf16[192,384]{1,0:T(8,128)(2,1)S(1)}, bf16[192,384]{1,0:T(8,128)(2,1)S(1)}, u32[]{:S(2)}, u32[]{:S(2)}) collective-permute-start(bf16[192,384]{1,0:T(8,128)(2,1)S(1)} %get-tuple-element.57), channel_id=1, source_target_pairs={{2,0},{3,1},{0,2},{1,3},{6,4},{7,5},{4,6},{5,7},{10,8},{11,9},{8,1... | collective-permute-start | bytes 442376 | tf_op jit(solution)/shard_map/ppermute | solution.py:26
  98.0 0.5 collective-permute-start.26
  100.4 0.8 dynamic-slice_reduce_fusion
  101.2 3.4 %collective-permute-done.25 = bf16[192,384]{1,0:T(8,128)(2,1)S(1)} collective-permute-done((bf16[192,384]{1,0:T(8,128)(2,1)S(1)}, bf16[192,384]{1,0:T(8,128)(2,1)S(1)}, u32[]{:S(2)}, u32[]{:S(2)}) %collective-permute-start.25) | collective-permute-done | bytes 147488 | tf_op jit(solution)/shard_map/ppermute | solution.py:26
  104.7 0.8 fusion
  (48 shorter events, 0.7 us)
Async XLA Ops:
  0.0 12.9 %collective-permute-start = (bf16[192,384]{1,0:T(8,128)(2,1)}, bf16[192,384]{1,0:T(8,128)(2,1)}, u32[]{:S(2)}, u32[]{:S(2)}) collective-permute-start(bf16[192,384]{1,0:T(8,128)(2,1)} %own.1), channel_id=1, source_target_pairs={{3,0},{0,1},{1,2},{2,3},{7,4},{4,5},{5,6},{6,7},{11,8},{8,9},{9,10... | collective-permute-start | bytes 442376 | tf_op jit(solution)/shard_map/ppermute | solution.py:26
  1.5 11.4 %collective-permute-start.1 = (bf16[192,384]{1,0:T(8,128)(2,1)}, bf16[192,384]{1,0:T(8,128)(2,1)}, u32[]{:S(2)}, u32[]{:S(2)}) collective-permute-start(bf16[192,384]{1,0:T(8,128)(2,1)} %own.1), channel_id=1, source_target_pairs={{2,0},{3,1},{0,2},{1,3},{6,4},{7,5},{4,6},{5,7},{10,8},{11,9},{8,1... | collective-permute-start | bytes 442376 | tf_op jit(solution)/shard_map/ppermute | solution.py:26
  4.2 8.6 %collective-permute-start.2 = (bf16[192,384]{1,0:T(8,128)(2,1)}, bf16[192,384]{1,0:T(8,128)(2,1)}, u32[]{:S(2)}, u32[]{:S(2)}) collective-permute-start(bf16[192,384]{1,0:T(8,128)(2,1)} %own.1), channel_id=1, source_target_pairs={{1,0},{2,1},{3,2},{0,3},{5,4},{6,5},{7,6},{4,7},{9,8},{10,9},{11,1... | collective-permute-start | bytes 442376 | tf_op jit(solution)/shard_map/ppermute | solution.py:26
  9.0 2.0 %copy-start = (bf16[1536,3,384]{2,0,1:T(8,128)(2,1)S(1)}, bf16[1536,3,384]{2,0,1:T(8,128)(2,1)}, u32[]{:S(2)}) copy-start(bf16[1536,3,384]{2,0,1:T(8,128)(2,1)} %param.14) | copy-start | bytes 10616836
  11.3 8.9 %copy-start.7 = (f32[384]{0:T(512)S(1)}, f32[384]{0:T(512)}, u32[]{:S(2)}) copy-start(f32[384]{0:T(512)} %param.16) | copy-start | bytes 4612
  11.3 8.9 %copy-start.8 = (f32[384]{0:T(512)S(1)}, f32[384]{0:T(512)}, u32[]{:S(2)}) copy-start(f32[384]{0:T(512)} %param.17) | copy-start | bytes 4612
  12.9 0.9 copy-start.2
  16.4 6.2 %copy-start.4 = (bf16[192,384]{1,0:T(8,128)(2,1)}, bf16[192,384]{1,0:T(8,128)(2,1)S(1)}, u32[]{:S(2)}) copy-start(bf16[192,384]{1,0:T(8,128)(2,1)S(1)} %get-tuple-element.36.refs_8_) | copy-start | bytes 442372
  16.4 4.9 %collective-permute-start.3 = (f32[8,192]{1,0:T(8,128)S(1)}, f32[8,192]{1,0:T(8,128)S(1)}, u32[]{:S(2)}, u32[]{:S(2)}) collective-permute-start(f32[8,192]{1,0:T(8,128)S(1)} %get-tuple-element.34.s0), channel_id=1, source_target_pairs={{3,0},{0,1},{1,2},{2,3},{7,4},{4,5},{5,6},{6,7},{11,8},{8,9},{9,10... | collective-permute-start | bytes 18440 | tf_op jit(solution)/shard_map/ppermute | solution.py:26
  17.1 5.2 %collective-permute-start.4 = (f32[8,192]{1,0:T(8,128)S(1)}, f32[8,192]{1,0:T(8,128)S(1)}, u32[]{:S(2)}, u32[]{:S(2)}) collective-permute-start(f32[8,192]{1,0:T(8,128)S(1)} %get-tuple-element.34.s0), channel_id=1, source_target_pairs={{2,0},{3,1},{0,2},{1,3},{6,4},{7,5},{4,6},{5,7},{10,8},{11,9},{8,1... | collective-permute-start | bytes 18440 | tf_op jit(solution)/shard_map/ppermute | solution.py:26
  18.6 3.7 %collective-permute-start.5 = (f32[8,192]{1,0:T(8,128)S(1)}, f32[8,192]{1,0:T(8,128)S(1)}, u32[]{:S(2)}, u32[]{:S(2)}) collective-permute-start(f32[8,192]{1,0:T(8,128)S(1)} %get-tuple-element.34.s0), channel_id=1, source_target_pairs={{1,0},{2,1},{3,2},{0,3},{5,4},{6,5},{7,6},{4,7},{9,8},{10,9},{11,1... | collective-permute-start | bytes 18440 | tf_op jit(solution)/shard_map/ppermute | solution.py:26
  22.6 36.2 %copy-start.3 = (bf16[192,384]{1,0:T(8,128)(2,1)S(1)}, bf16[192,384]{1,0:T(8,128)(2,1)}, u32[]{:S(2)}) copy-start(bf16[192,384]{1,0:T(8,128)(2,1)} %own.1) | copy-start | bytes 442372
  22.7 15.0 %collective-permute-start.6 = (bf16[2,192,384]{2,1,0:T(8,128)(2,1)S(1)}, bf16[2,192,384]{2,1,0:T(8,128)(2,1)S(1)}, u32[]{:S(2)}, u32[]{:S(2)}) collective-permute-start(bf16[2,192,384]{2,1,0:T(8,128)(2,1)S(1)} %pad_maximum_fusion), channel_id=1, source_target_pairs={{224,0},{228,4},{232,8},{236,12},{240,16},{244,20},{248,24},{252,2... | collective-permute-start | bytes 884744 | tf_op jit(solution)/shard_map/ppermute | solution.py:297
  24.7 13.0 %collective-permute-start.7 = (bf16[2,192,384]{2,1,0:T(8,128)(2,1)S(1)}, bf16[2,192,384]{2,1,0:T(8,128)(2,1)S(1)}, u32[]{:S(2)}, u32[]{:S(2)}) collective-permute-start(bf16[2,192,384]{2,1,0:T(8,128)(2,1)S(1)} %pad_maximum_fusion), channel_id=1, source_target_pairs={{32,0},{36,4},{40,8},{44,12},{48,16},{52,20},{56,24},{60,28},{64,3... | collective-permute-start | bytes 884744 | tf_op jit(solution)/shard_map/ppermute | solution.py:297
  28.7 8.7 %collective-permute-start.8 = (bf16[192,384]{1,0:T(8,128)(2,1)S(1)}, bf16[192,384]{1,0:T(8,128)(2,1)S(1)}, u32[]{:S(2)}, u32[]{:S(2)}) collective-permute-start(bf16[192,384]{1,0:T(8,128)(2,1)S(1)} %get-tuple-element.37), channel_id=1, source_target_pairs={{8,0},{12,4},{16,8},{20,12},{24,16},{28,20},{32,24},{36,28},{40,32... | collective-permute-start | bytes 442376 | tf_op jit(solution)/shard_map/ppermute | solution.py:26
  29.4 8.3 %collective-permute-start.9 = (bf16[192,384]{1,0:T(8,128)(2,1)S(1)}, bf16[192,384]{1,0:T(8,128)(2,1)S(1)}, u32[]{:S(2)}, u32[]{:S(2)}) collective-permute-start(bf16[192,384]{1,0:T(8,128)(2,1)S(1)} %get-tuple-element.37), channel_id=1, source_target_pairs={{12,0},{8,4},{20,8},{16,12},{28,16},{24,20},{36,24},{32,28},{44,32... | collective-permute-start | bytes 442376 | tf_op jit(solution)/shard_map/ppermute | solution.py:298
  29.4 33.9 %copy-start.5 = (bf16[192,384]{1,0:T(8,128)(2,1)S(1)}, bf16[192,384]{1,0:T(8,128)(2,1)}, u32[]{:S(2)}) copy-start(bf16[192,384]{1,0:T(8,128)(2,1)} %copy-done.4) | copy-start | bytes 442372
  37.7 10.7 %collective-permute-start.10 = (bf16[2,192,384]{2,1,0:T(8,128)(2,1)S(1)}, bf16[2,192,384]{2,1,0:T(8,128)(2,1)S(1)}, u32[]{:S(2)}, u32[]{:S(2)}) collective-permute-start(bf16[2,192,384]{2,1,0:T(8,128)(2,1)S(1)} %collective-permute-done.6), channel_id=1, source_target_pairs={{224,0},{228,4},{232,8},{236,12},{240,16},{244,20},{248,24},{252,2... | collective-permute-start | bytes 884744 | tf_op jit(solution)/shard_map/ppermute | solution.py:301
  37.7 10.7 %collective-permute-start.12 = (bf16[2,192,384]{2,1,0:T(8,128)(2,1)S(1)}, bf16[2,192,384]{2,1,0:T(8,128)(2,1)S(1)}, u32[]{:S(2)}, u32[]{:S(2)}) collective-permute-start(bf16[2,192,384]{2,1,0:T(8,128)(2,1)S(1)} %collective-permute-done.7), channel_id=1, source_target_pairs={{32,0},{36,4},{40,8},{44,12},{48,16},{52,20},{56,24},{60,28},{64,3... | collective-permute-start | bytes 884744 | tf_op jit(solution)/shard_map/ppermute | solution.py:301
  41.2 17.6 %collective-permute-start.14 = (bf16[2,192,384]{2,1,0:T(8,128)(2,1)S(1)}, bf16[2,192,384]{2,1,0:T(8,128)(2,1)S(1)}, u32[]{:S(2)}, u32[]{:S(2)}) collective-permute-start(bf16[2,192,384]{2,1,0:T(8,128)(2,1)S(1)} %pad_maximum_fusion.1.refs_0_), channel_id=1, source_target_pairs={{8,0},{12,4},{16,8},{20,12},{24,16},{28,20},{0,24},{4,28},{40,32},... | collective-permute-start | bytes 884744 | tf_op jit(solution)/shard_map/ppermute | solution.py:303
  41.5 17.3 %collective-permute-start.15 = (bf16[2,192,384]{2,1,0:T(8,128)(2,1)S(1)}, bf16[2,192,384]{2,1,0:T(8,128)(2,1)S(1)}, u32[]{:S(2)}, u32[]{:S(2)}) collective-permute-start(bf16[2,192,384]{2,1,0:T(8,128)(2,1)S(1)} %pad_maximum_fusion.1.refs_0_), channel_id=1, source_target_pairs={{16,0},{20,4},{24,8},{28,12},{0,16},{4,20},{8,24},{12,28},{48,32},... | collective-permute-start | bytes 884744 | tf_op jit(solution)/shard_map/ppermute | solution.py:303
  44.5 15.1 %collective-permute-start.16 = (bf16[2,192,384]{2,1,0:T(8,128)(2,1)S(1)}, bf16[2,192,384]{2,1,0:T(8,128)(2,1)S(1)}, u32[]{:S(2)}, u32[]{:S(2)}) collective-permute-start(bf16[2,192,384]{2,1,0:T(8,128)(2,1)S(1)} %pad_maximum_fusion.1.refs_0_), channel_id=1, source_target_pairs={{24,0},{28,4},{0,8},{4,12},{8,16},{12,20},{16,24},{20,28},{56,32},... | collective-permute-start | bytes 884744 | tf_op jit(solution)/shard_map/ppermute | solution.py:303
  48.4 11.2 %collective-permute-start.11 = (bf16[2,192,384]{2,1,0:T(8,128)(2,1)S(1)}, bf16[2,192,384]{2,1,0:T(8,128)(2,1)S(1)}, u32[]{:S(2)}, u32[]{:S(2)}) collective-permute-start(bf16[2,192,384]{2,1,0:T(8,128)(2,1)S(1)} %collective-permute-done.10), channel_id=1, source_target_pairs={{224,0},{228,4},{232,8},{236,12},{240,16},{244,20},{248,24},{252,2... | collective-permute-start | bytes 884744 | tf_op jit(solution)/shard_map/ppermute | solution.py:305
  48.4 11.2 %collective-permute-start.13 = (bf16[2,192,384]{2,1,0:T(8,128)(2,1)S(1)}, bf16[2,192,384]{2,1,0:T(8,128)(2,1)S(1)}, u32[]{:S(2)}, u32[]{:S(2)}) collective-permute-start(bf16[2,192,384]{2,1,0:T(8,128)(2,1)S(1)} %collective-permute-done.12), channel_id=1, source_target_pairs={{32,0},{36,4},{40,8},{44,12},{48,16},{52,20},{56,24},{60,28},{64,3... | collective-permute-start | bytes 884744 | tf_op jit(solution)/shard_map/ppermute | solution.py:305
  58.9 10.2 %collective-permute-start.19 = (bf16[192,384]{1,0:T(8,128)(2,1)S(1)}, bf16[192,384]{1,0:T(8,128)(2,1)S(1)}, u32[]{:S(2)}, u32[]{:S(2)}) collective-permute-start(bf16[192,384]{1,0:T(8,128)(2,1)S(1)} %copy-done.3), channel_id=1, source_target_pairs={{8,0},{12,4},{16,8},{20,12},{24,16},{28,20},{32,24},{36,28},{40,32... | collective-permute-start | bytes 442376 | tf_op jit(solution)/shard_map/ppermute | solution.py:26
  59.6 9.4 %collective-permute-start.17 = (bf16[192,384]{1,0:T(8,128)(2,1)S(1)}, bf16[192,384]{1,0:T(8,128)(2,1)S(1)}, u32[]{:S(2)}, u32[]{:S(2)}) collective-permute-start(bf16[192,384]{1,0:T(8,128)(2,1)S(1)} %get-tuple-element.66.refs_5_), channel_id=1, source_target_pairs={{224,0},{228,4},{232,8},{236,12},{240,16},{244,20},{248,24},{252,2... | collective-permute-start | bytes 442376 | tf_op jit(solution)/shard_map/ppermute | solution.py:313
  60.8 8.2 %collective-permute-start.18 = (bf16[192,384]{1,0:T(8,128)(2,1)S(1)}, bf16[192,384]{1,0:T(8,128)(2,1)S(1)}, u32[]{:S(2)}, u32[]{:S(2)}) collective-permute-start(bf16[192,384]{1,0:T(8,128)(2,1)S(1)} %get-tuple-element.69.refs_10_), channel_id=1, source_target_pairs={{32,0},{36,4},{40,8},{44,12},{48,16},{52,20},{56,24},{60,28},{64,3... | collective-permute-start | bytes 442376 | tf_op jit(solution)/shard_map/ppermute | solution.py:314
  75.3 17.5 %copy-start.1 = (bf16[384,1536]{1,0:T(8,128)(2,1)S(1)}, bf16[384,1536]{1,0:T(8,128)(2,1)}, u32[]{:S(2)}) copy-start(bf16[384,1536]{1,0:T(8,128)(2,1)} %w_ref.1) | copy-start | bytes 3538948
  75.4 2.4 %collective-permute-start.20 = (bf16[4,208,384]{2,1,0:T(8,128)(2,1)S(1)}, bf16[4,208,384]{2,1,0:T(8,128)(2,1)S(1)}, u32[]{:S(2)}, u32[]{:S(2)}) collective-permute-start(bf16[4,208,384]{2,1,0:T(8,128)(2,1)S(1)} %shard_map.96), channel_id=1, source_target_pairs={{0,4},{4,0},{8,12},{12,8},{16,20},{20,16},{24,28},{28,24},{32,36},... | collective-permute-start | bytes 1916936 | tf_op jit(solution)/shard_map/ppermute | solution.py:318
  77.8 26.9 %copy-start.6 = (bf16[384,384]{1,0:T(8,128)(2,1)S(1)}, bf16[384,384]{1,0:T(8,128)(2,1)}, u32[]{:S(2)}) copy-start(bf16[384,384]{1,0:T(8,128)(2,1)} %param.10) | copy-start | bytes 884740
  78.6 10.9 %collective-permute-start.21 = (bf16[208,384]{1,0:T(8,128)(2,1)S(1)}, bf16[208,384]{1,0:T(8,128)(2,1)S(1)}, u32[]{:S(2)}, u32[]{:S(2)}) collective-permute-start(bf16[208,384]{1,0:T(8,128)(2,1)S(1)} %get-tuple-element.63), channel_id=1, source_target_pairs={{24,0},{28,4},{0,8},{4,12},{8,16},{12,20},{16,24},{20,28},{56,32},... | collective-permute-start | bytes 479240 | tf_op jit(solution)/shard_map/ppermute | solution.py:320
  82.4 8.5 %collective-permute-start.22 = (bf16[208,384]{1,0:T(8,128)(2,1)S(1)}, bf16[208,384]{1,0:T(8,128)(2,1)S(1)}, u32[]{:S(2)}, u32[]{:S(2)}) collective-permute-start(bf16[208,384]{1,0:T(8,128)(2,1)S(1)} %get-tuple-element.62), channel_id=1, source_target_pairs={{16,0},{20,4},{24,8},{28,12},{0,16},{4,20},{8,24},{12,28},{48,32},... | collective-permute-start | bytes 479240 | tf_op jit(solution)/shard_map/ppermute | solution.py:320
  82.4 10.5 %collective-permute-start.23 = (bf16[208,384]{1,0:T(8,128)(2,1)S(1)}, bf16[208,384]{1,0:T(8,128)(2,1)S(1)}, u32[]{:S(2)}, u32[]{:S(2)}) collective-permute-start(bf16[208,384]{1,0:T(8,128)(2,1)S(1)} %get-tuple-element.61), channel_id=1, source_target_pairs={{8,0},{12,4},{16,8},{20,12},{24,16},{28,20},{0,24},{4,28},{40,32},... | collective-permute-start | bytes 479240 | tf_op jit(solution)/shard_map/ppermute | solution.py:320
  93.8 7.4 %collective-permute-start.24 = (bf16[192,384]{1,0:T(8,128)(2,1)S(1)}, bf16[192,384]{1,0:T(8,128)(2,1)S(1)}, u32[]{:S(2)}, u32[]{:S(2)}) collective-permute-start(bf16[192,384]{1,0:T(8,128)(2,1)S(1)} %get-tuple-element.56), channel_id=1, source_target_pairs={{3,0},{0,1},{1,2},{2,3},{7,4},{4,5},{5,6},{6,7},{11,8},{8,9},{9,10... | collective-permute-start | bytes 442376 | tf_op jit(solution)/shard_map/ppermute | solution.py:26
  95.8 8.9 %collective-permute-start.25 = (bf16[192,384]{1,0:T(8,128)(2,1)S(1)}, bf16[192,384]{1,0:T(8,128)(2,1)S(1)}, u32[]{:S(2)}, u32[]{:S(2)}) collective-permute-start(bf16[192,384]{1,0:T(8,128)(2,1)S(1)} %get-tuple-element.57), channel_id=1, source_target_pairs={{2,0},{3,1},{0,2},{1,3},{6,4},{7,5},{4,6},{5,7},{10,8},{11,9},{8,1... | collective-permute-start | bytes 442376 | tf_op jit(solution)/shard_map/ppermute | solution.py:26
  98.0 6.6 %collective-permute-start.26 = (bf16[192,384]{1,0:T(8,128)(2,1)S(1)}, bf16[192,384]{1,0:T(8,128)(2,1)S(1)}, u32[]{:S(2)}, u32[]{:S(2)}) collective-permute-start(bf16[192,384]{1,0:T(8,128)(2,1)S(1)} %get-tuple-element.58), channel_id=1, source_target_pairs={{1,0},{2,1},{3,2},{0,3},{5,4},{6,5},{7,6},{4,7},{9,8},{10,9},{11,1... | collective-permute-start | bytes 442376 | tf_op jit(solution)/shard_map/ppermute | solution.py:26

commit v4 on v3

--- a/solution.py
+++ b/solution.py
@@ -238,12 +238,13 @@
 
     chunks = [shift(latents, "head", j) for j in range(1, heads_ax)]
     home_latents = shift(latents, "queue", -2)
+    w3 = jnp.transpose(w_qkv, (1, 0, 2))
+    w_near = call(early_kernel, [VMEM], shape(w3.shape, jnp.bfloat16), 0, 8 << 20)(w3)
+    w_near, noise_level = lax.optimization_barrier((w_near, noise_level))
     modulation = lax.dynamic_index_in_dim(mod_table, noise_level[place(frame)], 0, keepdims=False)
     home_level = noise_level[place(frame + 1)]
     gate = lax.dynamic_slice(mod_table, (home_level, 2, x * width), (1, 1, width)).reshape(1, width)
     modulation = modulation.reshape(3, heads_ax, 1, width)
-    w3 = jnp.transpose(w_qkv, (1, 0, 2))
-    w_near = call(early_kernel, [VMEM], shape(w3.shape, jnp.bfloat16), 0, 8 << 20)(w3)
     q, k, v, sums = call(
         project_kernel,
         [SMEM] + [VMEM] * 7,
@@ -257,6 +258,7 @@
         6 << 20,
     )(x_arg, latents, *chunks, modulation[1], modulation[0], w_near)
     all_sums = [sums] + [shift(sums, "head", j) for j in range(1, heads_ax)]
+    all_sums, home_latents = lax.optimization_barrier((all_sums, home_latents))
     qn, kn = call(
         norm_kernel,
         [VMEM] * 8,
@@ -312,7 +314,6 @@
 
     ks[4] = lax.ppermute(ks[3], "queue", key_route(1))
     vs[4] = lax.ppermute(vs[-3], "queue", key_route(-1))
-    ks[4], vs[4], home_latents = lax.optimization_barrier((ks[4], vs[4], home_latents))
     partials = [partial(distances) for distances in GROUPS]
     mine, other = [p[0] for p in partials], [p[1] for p in partials]
     received = lax.ppermute(combine(other), "queue", swap)

time: 106 us -> 108 us (1.019)
  waiting for transfers between devices: 36.4 us -> 37.9 us
  starting transfers between devices: 40.2 us -> 39.1 us
    ppermute x1, waiting for transfers between devices: 0.33 us -> 7.57 us  [local(): lax.ppermute(qn, 'queue', [((i + 2) % slabs ^ 1, i) for i in range(slabs)])]
    ppermute x11, waiting for transfers between devices: 13.3 us -> 10.2 us  [shift(): lax.ppermute(block, axis, [((i - distance) % n, i) for i in range(n)])]
    ppermute x2, waiting for transfers between devices: 3.6 us -> 1.81 us  [local(): both[way * 2] = lax.ppermute(both[way], 'queue', key_route(way))]
    ppermute x3, starting transfers between devices: 4.77 us -> 3.37 us  [local(): lax.ppermute(paired[j], 'queue', y_route(j))]
    ppermute x1, starting transfers between devices: 1.16 us -> 0.08 us  [local(): ks[4] = lax.ppermute(ks[3], 'queue', key_route(1))]
    unnamed x18 -> x14, local copies, waits for them, and re-layouts: 2.94 us -> 3.26 us
  transfers between devices with their start and end apart: 27 -> 27, of which waited for: 13 -> 13; matrix products, arithmetic and copies ran while one was open for 3% -> 4% of each run, Pallas kernels for 6% -> 8%
where the time goes in v4:
time: 108 us
  starting transfers between devices  39.1 us (36%)
  waiting for transfers between devices  37.9 us (35%)
  Pallas kernels  16.8 us (16%)
  local copies, waits for them, and re-layouts  7.31 us (7%)
  between operations  4.81 us (4%)
  other arithmetic  1.77 us (2%)
    ppermute x11, starting transfers between devices, shift(): lax.ppermute(block, axis, [((i - distance) % n, i) for i in range(n)])  15.4 us
    pallas_call x2, Pallas kernels, attend(): call(functools.partial(attend_kernel, slabs), [SMEM] + [VMEM] * (slots +...  11.5 us
    ppermute x11, waiting for transfers between devices, shift(): lax.ppermute(block, axis, [((i - distance) % n, i) for i in range(n)])  10.2 us
    ppermute x3, waiting for transfers between devices, local(): lax.ppermute(paired[j], 'queue', y_route(j))  9.55 us
    ppermute x1, waiting for transfers between devices, local(): lax.ppermute(qn, 'queue', [((i + 2) % slabs ^ 1, i) for i in range(slabs)])  7.57 us
    ppermute x3, waiting for transfers between devices, local(): lax.ppermute(home_q, 'queue', y_route(-j))  6.68 us
    ppermute x2, starting transfers between devices, local(): both[way] = lax.ppermute(both[0], 'queue', key_route(way))  6.02 us
    ppermute x2, starting transfers between devices, local(): both[way * 2] = lax.ppermute(both[way], 'queue', key_route(way))  3.81 us
  transfers between devices with their start and end apart: 27, of which 13 were waited for; matrix products, arithmetic and copies ran while one was open for 4% of the time, Pallas kernels for 8%

profile of v4, /device:TPU:24, one launch (start us, length us, event | category | flops | bytes accessed | tf_op | source)
XLA Modules:
  0.0 107.7 jit_solution(14439041640881812904)
XLA Ops:
  0.0 1.5 %collective-permute-start = (bf16[192,384]{1,0:T(8,128)(2,1)}, bf16[192,384]{1,0:T(8,128)(2,1)}, u32[]{:S(2)}, u32[]{:S(2)}) collective-permute-start(bf16[192,384]{1,0:T(8,128)(2,1)} %own.1), channel_id=1, source_target_pairs={{3,0},{0,1},{1,2},{2,3},{7,4},{4,5},{5,6},{6,7},{11,8},{8,9},{9,10... | collective-permute-start | bytes 442376 | tf_op jit(solution)/shard_map/ppermute | solution.py:26
  1.5 2.7 %collective-permute-start.1 = (bf16[192,384]{1,0:T(8,128)(2,1)}, bf16[192,384]{1,0:T(8,128)(2,1)}, u32[]{:S(2)}, u32[]{:S(2)}) collective-permute-start(bf16[192,384]{1,0:T(8,128)(2,1)} %own.1), channel_id=1, source_target_pairs={{2,0},{3,1},{0,2},{1,3},{6,4},{7,5},{4,6},{5,7},{10,8},{11,9},{8,1... | collective-permute-start | bytes 442376 | tf_op jit(solution)/shard_map/ppermute | solution.py:26
  4.2 1.4 %collective-permute-start.2 = (bf16[192,384]{1,0:T(8,128)(2,1)}, bf16[192,384]{1,0:T(8,128)(2,1)}, u32[]{:S(2)}, u32[]{:S(2)}) collective-permute-start(bf16[192,384]{1,0:T(8,128)(2,1)} %own.1), channel_id=1, source_target_pairs={{1,0},{2,1},{3,2},{0,3},{5,4},{6,5},{7,6},{4,7},{9,8},{10,9},{11,1... | collective-permute-start | bytes 442376 | tf_op jit(solution)/shard_map/ppermute | solution.py:26
  5.7 0.7 collective-permute-start.6
  7.1 2.0 %copy-done = bf16[1536,3,384]{2,0,1:T(8,128)(2,1)S(1)} copy-done((bf16[1536,3,384]{2,0,1:T(8,128)(2,1)S(1)}, bf16[1536,3,384]{2,0,1:T(8,128)(2,1)}, u32[]{:S(2)}) %copy-start) | copy-done | bytes 3538968
  9.1 0.3 shard_map.91.w_ref
  9.4 0.3 copy-done.6
  9.8 0.6 fusion.1
  12.3 0.8 constant_dynamic-slice_fusion.1
  13.2 0.9 copy-done.2
  14.1 2.6 %shard_map.92 = (f32[192,384]{1,0:T(8,128)S(1)}, f32[192,384]{1,0:T(8,128)S(1)}, bf16[192,384]{1,0:T(8,128)(2,1)S(1)}, f32[8,192]{1,0:T(8,128)S(1)}) custom-call(s32[1]{0:T(128)} %bitcast.1.x_ref, bf16[192,384]{1,0:T(8,128)(2,1)S(1)} %copy-done.2, bf16[192,384]{1,0:T(8,128)(2,1)} %collective-permute-done.one, bf16[192,384]{1,0:T(8,128)(2,1)} %collective-permute-done.1.two, ...), custom_call_target="tpu_custom_call" | custom-call | flops 679477248 | bytes 6291456 | tf_op jit(solution)/shard_map/pallas_call | solution.py:248
  16.7 0.7 collective-permute-start.3
  17.4 1.2 %collective-permute-start.4 = (f32[8,192]{1,0:T(8,128)S(1)}, f32[8,192]{1,0:T(8,128)S(1)}, u32[]{:S(2)}, u32[]{:S(2)}) collective-permute-start(f32[8,192]{1,0:T(8,128)S(1)} %get-tuple-element.42.s0), channel_id=1, source_target_pairs={{2,0},{3,1},{0,2},{1,3},{6,4},{7,5},{4,6},{5,7},{10,8},{11,9},{8,1... | collective-permute-start | bytes 18440 | tf_op jit(solution)/shard_map/ppermute | solution.py:26
  18.6 1.6 %collective-permute-start.5 = (f32[8,192]{1,0:T(8,128)S(1)}, f32[8,192]{1,0:T(8,128)S(1)}, u32[]{:S(2)}, u32[]{:S(2)}) collective-permute-start(f32[8,192]{1,0:T(8,128)S(1)} %get-tuple-element.42.s0), channel_id=1, source_target_pairs={{1,0},{2,1},{3,2},{0,3},{5,4},{6,5},{7,6},{4,7},{9,8},{10,9},{11,1... | collective-permute-start | bytes 18440 | tf_op jit(solution)/shard_map/ppermute | solution.py:26
  20.2 0.7 reshape.18.qg_ref
  20.9 0.7 reshape.19.kg_ref
  21.7 0.9 collective-permute-done.4.s2
  23.0 2.0 %collective-permute-start.7 = (bf16[2,192,384]{2,1,0:T(8,128)(2,1)S(1)}, bf16[2,192,384]{2,1,0:T(8,128)(2,1)S(1)}, u32[]{:S(2)}, u32[]{:S(2)}) collective-permute-start(bf16[2,192,384]{2,1,0:T(8,128)(2,1)S(1)} %pad_maximum_fusion), channel_id=1, source_target_pairs={{224,0},{228,4},{232,8},{236,12},{240,16},{244,20},{248,24},{252,2... | collective-permute-start | bytes 884744 | tf_op jit(solution)/shard_map/ppermute | solution.py:299
  24.9 4.0 %collective-permute-start.8 = (bf16[2,192,384]{2,1,0:T(8,128)(2,1)S(1)}, bf16[2,192,384]{2,1,0:T(8,128)(2,1)S(1)}, u32[]{:S(2)}, u32[]{:S(2)}) collective-permute-start(bf16[2,192,384]{2,1,0:T(8,128)(2,1)S(1)} %pad_maximum_fusion), channel_id=1, source_target_pairs={{32,0},{36,4},{40,8},{44,12},{48,16},{52,20},{56,24},{60,28},{64,3... | collective-permute-start | bytes 884744 | tf_op jit(solution)/shard_map/ppermute | solution.py:299
  29.0 0.5 collective-permute-start.9
  29.7 7.6 %collective-permute-done.10 = bf16[192,384]{1,0:T(8,128)(2,1)S(1)} collective-permute-done((bf16[192,384]{1,0:T(8,128)(2,1)S(1)}, bf16[192,384]{1,0:T(8,128)(2,1)S(1)}, u32[]{:S(2)}, u32[]{:S(2)}) %collective-permute-start.10) | collective-permute-done | bytes 147488 | tf_op jit(solution)/shard_map/ppermute | solution.py:300
  37.2 6.2 %collective-permute-done.9 = bf16[192,384]{1,0:T(8,128)(2,1)S(1)} collective-permute-done((bf16[192,384]{1,0:T(8,128)(2,1)S(1)}, bf16[192,384]{1,0:T(8,128)(2,1)S(1)}, u32[]{:S(2)}, u32[]{:S(2)}) %collective-permute-start.9) | collective-permute-done | bytes 147488 | tf_op jit(solution)/shard_map/ppermute | solution.py:26
  43.4 3.8 %collective-permute-start.13 = (bf16[2,192,384]{2,1,0:T(8,128)(2,1)S(1)}, bf16[2,192,384]{2,1,0:T(8,128)(2,1)S(1)}, u32[]{:S(2)}, u32[]{:S(2)}) collective-permute-start(bf16[2,192,384]{2,1,0:T(8,128)(2,1)S(1)} %collective-permute-done.8), channel_id=1, source_target_pairs={{32,0},{36,4},{40,8},{44,12},{48,16},{52,20},{56,24},{60,28},{64,3... | collective-permute-start | bytes 884744 | tf_op jit(solution)/shard_map/ppermute | solution.py:303
  47.3 1.3 %collective-permute-start.16 = (bf16[2,192,384]{2,1,0:T(8,128)(2,1)S(1)}, bf16[2,192,384]{2,1,0:T(8,128)(2,1)S(1)}, u32[]{:S(2)}, u32[]{:S(2)}) collective-permute-start(bf16[2,192,384]{2,1,0:T(8,128)(2,1)S(1)} %pad_maximum_fusion.1.refs_0_), channel_id=1, source_target_pairs={{16,0},{20,4},{24,8},{28,12},{0,16},{4,20},{8,24},{12,28},{48,32},... | collective-permute-start | bytes 884744 | tf_op jit(solution)/shard_map/ppermute | solution.py:305
  48.6 1.9 %collective-permute-start.17 = (bf16[2,192,384]{2,1,0:T(8,128)(2,1)S(1)}, bf16[2,192,384]{2,1,0:T(8,128)(2,1)S(1)}, u32[]{:S(2)}, u32[]{:S(2)}) collective-permute-start(bf16[2,192,384]{2,1,0:T(8,128)(2,1)S(1)} %pad_maximum_fusion.1.refs_0_), channel_id=1, source_target_pairs={{24,0},{28,4},{0,8},{4,12},{8,16},{12,20},{16,24},{20,28},{56,32},... | collective-permute-start | bytes 884744 | tf_op jit(solution)/shard_map/ppermute | solution.py:305
  50.6 1.8 %collective-permute-done.11 = bf16[2,192,384]{2,1,0:T(8,128)(2,1)S(1)} collective-permute-done((bf16[2,192,384]{2,1,0:T(8,128)(2,1)S(1)}, bf16[2,192,384]{2,1,0:T(8,128)(2,1)S(1)}, u32[]{:S(2)}, u32[]{:S(2)}) %collective-permute-start.11) | collective-permute-done | bytes 294944 | tf_op jit(solution)/shard_map/ppermute | solution.py:303
  52.5 3.2 %collective-permute-start.14 = (bf16[2,192,384]{2,1,0:T(8,128)(2,1)S(1)}, bf16[2,192,384]{2,1,0:T(8,128)(2,1)S(1)}, u32[]{:S(2)}, u32[]{:S(2)}) collective-permute-start(bf16[2,192,384]{2,1,0:T(8,128)(2,1)S(1)} %collective-permute-done.13), channel_id=1, source_target_pairs={{32,0},{36,4},{40,8},{44,12},{48,16},{52,20},{56,24},{60,28},{64,3... | collective-permute-start | bytes 884744 | tf_op jit(solution)/shard_map/ppermute | solution.py:307
  55.8 6.1 %collective-permute-done.15.refs_1_ = bf16[2,192,384]{2,1,0:T(8,128)(2,1)S(1)} collective-permute-done((bf16[2,192,384]{2,1,0:T(8,128)(2,1)S(1)}, bf16[2,192,384]{2,1,0:T(8,128)(2,1)S(1)}, u32[]{:S(2)}, u32[]{:S(2)}) %collective-permute-start.15) | collective-permute-done | bytes 294944 | tf_op jit(solution)/shard_map/ppermute | solution.py:305
  61.8 0.6 collective-permute-done.17.refs_3_
  62.6 3.5 %collective-permute-start.19 = (bf16[192,384]{1,0:T(8,128)(2,1)S(1)}, bf16[192,384]{1,0:T(8,128)(2,1)S(1)}, u32[]{:S(2)}, u32[]{:S(2)}) collective-permute-start(bf16[192,384]{1,0:T(8,128)(2,1)S(1)} %get-tuple-element.73.refs_10_), channel_id=1, source_target_pairs={{32,0},{36,4},{40,8},{44,12},{48,16},{52,20},{56,24},{60,28},{64,3... | collective-permute-start | bytes 442376 | tf_op jit(solution)/shard_map/ppermute | solution.py:316
  66.1 5.8 %shard_map.94 = (bf16[4,208,384]{2,1,0:T(8,128)(2,1)S(1)}, bf16[4,208,384]{2,1,0:T(8,128)(2,1)S(1)}) custom-call(f32[16]{0:T(128)S(1)} %stack.136.flags, bf16[2,192,384]{2,1,0:T(8,128)(2,1)S(1)} %pad_maximum_fusion.1.refs_0_, bf16[2,192,384]{2,1,0:T(8,128)(2,1)S(1)} %collective-permute-done.15.refs_1_, ...), custom_call_target="tpu_custom_call" | custom-call | flops 6341787648 | bytes 1048576 | tf_op jit(solution)/shard_map/pallas_call | solution.py:208
  71.9 5.7 %shard_map.95 = (bf16[4,208,384]{2,1,0:T(8,128)(2,1)S(1)}, bf16[4,208,384]{2,1,0:T(8,128)(2,1)S(1)}) custom-call(f32[16]{0:T(128)S(1)} %stack.159.flags, bf16[2,192,384]{2,1,0:T(8,128)(2,1)S(1)} %pad_maximum_fusion.1.refs_0_, bf16[2,192,384]{2,1,0:T(8,128)(2,1)S(1)} %collective-permute-done.15.refs_1_, ...), custom_call_target="tpu_custom_call" | custom-call | flops 6341787648 | bytes 1048576 | tf_op jit(solution)/shard_map/pallas_call | solution.py:208
  77.6 0.6 shard_map.96
  78.2 0.4 collective-permute-start.20
  78.6 2.1 %collective-permute-done.20.refs_2_ = bf16[4,208,384]{2,1,0:T(8,128)(2,1)S(1)} collective-permute-done((bf16[4,208,384]{2,1,0:T(8,128)(2,1)S(1)}, bf16[4,208,384]{2,1,0:T(8,128)(2,1)S(1)}, u32[]{:S(2)}, u32[]{:S(2)}) %collective-permute-start.20) | collective-permute-done | bytes 639008 | tf_op jit(solution)/shard_map/ppermute | solution.py:319
  80.6 0.7 shard_map.97
  81.4 2.4 %collective-permute-start.21 = (bf16[208,384]{1,0:T(8,128)(2,1)S(1)}, bf16[208,384]{1,0:T(8,128)(2,1)S(1)}, u32[]{:S(2)}, u32[]{:S(2)}) collective-permute-start(bf16[208,384]{1,0:T(8,128)(2,1)S(1)} %get-tuple-element.71), channel_id=1, source_target_pairs={{24,0},{28,4},{0,8},{4,12},{8,16},{12,20},{16,24},{20,28},{56,32},... | collective-permute-start | bytes 479240 | tf_op jit(solution)/shard_map/ppermute | solution.py:321
  83.8 1.0 collective-permute-start.23
  84.8 6.2 %collective-permute-done.21.b = bf16[208,384]{1,0:T(8,128)(2,1)S(1)} collective-permute-done((bf16[208,384]{1,0:T(8,128)(2,1)S(1)}, bf16[208,384]{1,0:T(8,128)(2,1)S(1)}, u32[]{:S(2)}, u32[]{:S(2)}) %collective-permute-start.21) | collective-permute-done | bytes 159776 | tf_op jit(solution)/shard_map/ppermute | solution.py:321
  90.9 1.4 %collective-permute-done.22.c = bf16[208,384]{1,0:T(8,128)(2,1)S(1)} collective-permute-done((bf16[208,384]{1,0:T(8,128)(2,1)S(1)}, bf16[208,384]{1,0:T(8,128)(2,1)S(1)}, u32[]{:S(2)}, u32[]{:S(2)}) %collective-permute-start.22) | collective-permute-done | bytes 159776 | tf_op jit(solution)/shard_map/ppermute | solution.py:321
  92.3 2.0 %collective-permute-done.23.d = bf16[208,384]{1,0:T(8,128)(2,1)S(1)} collective-permute-done((bf16[208,384]{1,0:T(8,128)(2,1)S(1)}, bf16[208,384]{1,0:T(8,128)(2,1)S(1)}, u32[]{:S(2)}, u32[]{:S(2)}) %collective-permute-start.23) | collective-permute-done | bytes 159776 | tf_op jit(solution)/shard_map/ppermute | solution.py:321
  94.3 0.9 shard_map.98
  95.2 1.8 %collective-permute-start.24 = (bf16[192,384]{1,0:T(8,128)(2,1)S(1)}, bf16[192,384]{1,0:T(8,128)(2,1)S(1)}, u32[]{:S(2)}, u32[]{:S(2)}) collective-permute-start(bf16[192,384]{1,0:T(8,128)(2,1)S(1)} %get-tuple-element.64), channel_id=1, source_target_pairs={{3,0},{0,1},{1,2},{2,3},{7,4},{4,5},{5,6},{6,7},{11,8},{8,9},{9,10... | collective-permute-start | bytes 442376 | tf_op jit(solution)/shard_map/ppermute | solution.py:26
  97.0 2.4 %collective-permute-start.25 = (bf16[192,384]{1,0:T(8,128)(2,1)S(1)}, bf16[192,384]{1,0:T(8,128)(2,1)S(1)}, u32[]{:S(2)}, u32[]{:S(2)}) collective-permute-start(bf16[192,384]{1,0:T(8,128)(2,1)S(1)} %get-tuple-element.65), channel_id=1, source_target_pairs={{2,0},{3,1},{0,2},{1,3},{6,4},{7,5},{4,6},{5,7},{10,8},{11,9},{8,1... | collective-permute-start | bytes 442376 | tf_op jit(solution)/shard_map/ppermute | solution.py:26
  99.3 0.9 collective-permute-start.26
  102.2 0.8 dynamic-slice_reduce_fusion
  103.0 3.0 %collective-permute-done.25 = bf16[192,384]{1,0:T(8,128)(2,1)S(1)} collective-permute-done((bf16[192,384]{1,0:T(8,128)(2,1)S(1)}, bf16[192,384]{1,0:T(8,128)(2,1)S(1)}, u32[]{:S(2)}, u32[]{:S(2)}) %collective-permute-start.25) | collective-permute-done | bytes 147488 | tf_op jit(solution)/shard_map/ppermute | solution.py:26
  106.0 1.7 %fusion = bf16[192,384]{1,0:T(8,128)(2,1)} fusion(bf16[192,384]{1,0:T(8,128)(2,1)S(1)} %collective-permute-done.26, bf16[192,384]{1,0:T(8,128)(2,1)S(1)} %collective-permute-done.25, bf16[192,384]{1,0:T(8,128)(2,1)S(1)} %collective-permute-done.24, bf16[192,384]{1,0:T(8,128)(2,1)S(1)} %get-tuple-element.63, bf16[192,384]{1,0:T(8,128)(2,1)} %collective-permute-done.6, ...), kind=kLoop, calls=%fused_computation.7 | loop fusion | flops 884736 | bytes 1033733 | tf_op jit(solution)/shard_map/jit(_where)/select_n | solution.py:335
  (44 shorter events, 1.2 us)
Async XLA Ops:
  0.0 13.1 %collective-permute-start = (bf16[192,384]{1,0:T(8,128)(2,1)}, bf16[192,384]{1,0:T(8,128)(2,1)}, u32[]{:S(2)}, u32[]{:S(2)}) collective-permute-start(bf16[192,384]{1,0:T(8,128)(2,1)} %own.1), channel_id=1, source_target_pairs={{3,0},{0,1},{1,2},{2,3},{7,4},{4,5},{5,6},{6,7},{11,8},{8,9},{9,10... | collective-permute-start | bytes 442376 | tf_op jit(solution)/shard_map/ppermute | solution.py:26
  1.5 11.7 %collective-permute-start.1 = (bf16[192,384]{1,0:T(8,128)(2,1)}, bf16[192,384]{1,0:T(8,128)(2,1)}, u32[]{:S(2)}, u32[]{:S(2)}) collective-permute-start(bf16[192,384]{1,0:T(8,128)(2,1)} %own.1), channel_id=1, source_target_pairs={{2,0},{3,1},{0,2},{1,3},{6,4},{7,5},{4,6},{5,7},{10,8},{11,9},{8,1... | collective-permute-start | bytes 442376 | tf_op jit(solution)/shard_map/ppermute | solution.py:26
  4.2 8.9 %collective-permute-start.2 = (bf16[192,384]{1,0:T(8,128)(2,1)}, bf16[192,384]{1,0:T(8,128)(2,1)}, u32[]{:S(2)}, u32[]{:S(2)}) collective-permute-start(bf16[192,384]{1,0:T(8,128)(2,1)} %own.1), channel_id=1, source_target_pairs={{1,0},{2,1},{3,2},{0,3},{5,4},{6,5},{7,6},{4,7},{9,8},{10,9},{11,1... | collective-permute-start | bytes 442376 | tf_op jit(solution)/shard_map/ppermute | solution.py:26
  5.7 15.9 %collective-permute-start.6 = (bf16[192,384]{1,0:T(8,128)(2,1)}, bf16[192,384]{1,0:T(8,128)(2,1)}, u32[]{:S(2)}, u32[]{:S(2)}) collective-permute-start(bf16[192,384]{1,0:T(8,128)(2,1)} %own.1), channel_id=1, source_target_pairs={{8,0},{12,4},{16,8},{20,12},{24,16},{28,20},{32,24},{36,28},{40,32... | collective-permute-start | bytes 442376 | tf_op jit(solution)/shard_map/ppermute | solution.py:26
  7.1 2.0 %copy-start = (bf16[1536,3,384]{2,0,1:T(8,128)(2,1)S(1)}, bf16[1536,3,384]{2,0,1:T(8,128)(2,1)}, u32[]{:S(2)}) copy-start(bf16[1536,3,384]{2,0,1:T(8,128)(2,1)} %param.14) | copy-start | bytes 10616836
  9.1 0.7 copy-start.6
  13.2 0.9 copy-start.2
  16.7 6.2 %copy-start.3 = (bf16[192,384]{1,0:T(8,128)(2,1)}, bf16[192,384]{1,0:T(8,128)(2,1)S(1)}, u32[]{:S(2)}) copy-start(bf16[192,384]{1,0:T(8,128)(2,1)S(1)} %get-tuple-element.47.refs_8_) | copy-start | bytes 442372
  16.7 4.9 %collective-permute-start.3 = (f32[8,192]{1,0:T(8,128)S(1)}, f32[8,192]{1,0:T(8,128)S(1)}, u32[]{:S(2)}, u32[]{:S(2)}) collective-permute-start(f32[8,192]{1,0:T(8,128)S(1)} %get-tuple-element.42.s0), channel_id=1, source_target_pairs={{3,0},{0,1},{1,2},{2,3},{7,4},{4,5},{5,6},{6,7},{11,8},{8,9},{9,10... | collective-permute-start | bytes 18440 | tf_op jit(solution)/shard_map/ppermute | solution.py:26
  17.4 5.2 %collective-permute-start.4 = (f32[8,192]{1,0:T(8,128)S(1)}, f32[8,192]{1,0:T(8,128)S(1)}, u32[]{:S(2)}, u32[]{:S(2)}) collective-permute-start(f32[8,192]{1,0:T(8,128)S(1)} %get-tuple-element.42.s0), channel_id=1, source_target_pairs={{2,0},{3,1},{0,2},{1,3},{6,4},{7,5},{4,6},{5,7},{10,8},{11,9},{8,1... | collective-permute-start | bytes 18440 | tf_op jit(solution)/shard_map/ppermute | solution.py:26
  18.6 4.0 %collective-permute-start.5 = (f32[8,192]{1,0:T(8,128)S(1)}, f32[8,192]{1,0:T(8,128)S(1)}, u32[]{:S(2)}, u32[]{:S(2)}) collective-permute-start(f32[8,192]{1,0:T(8,128)S(1)} %get-tuple-element.42.s0), channel_id=1, source_target_pairs={{1,0},{2,1},{3,2},{0,3},{5,4},{6,5},{7,6},{4,7},{9,8},{10,9},{11,1... | collective-permute-start | bytes 18440 | tf_op jit(solution)/shard_map/ppermute | solution.py:26
  23.0 20.4 %collective-permute-start.7 = (bf16[2,192,384]{2,1,0:T(8,128)(2,1)S(1)}, bf16[2,192,384]{2,1,0:T(8,128)(2,1)S(1)}, u32[]{:S(2)}, u32[]{:S(2)}) collective-permute-start(bf16[2,192,384]{2,1,0:T(8,128)(2,1)S(1)} %pad_maximum_fusion), channel_id=1, source_target_pairs={{224,0},{228,4},{232,8},{236,12},{240,16},{244,20},{248,24},{252,2... | collective-permute-start | bytes 884744 | tf_op jit(solution)/shard_map/ppermute | solution.py:299
  24.9 18.4 %collective-permute-start.8 = (bf16[2,192,384]{2,1,0:T(8,128)(2,1)S(1)}, bf16[2,192,384]{2,1,0:T(8,128)(2,1)S(1)}, u32[]{:S(2)}, u32[]{:S(2)}) collective-permute-start(bf16[2,192,384]{2,1,0:T(8,128)(2,1)S(1)} %pad_maximum_fusion), channel_id=1, source_target_pairs={{32,0},{36,4},{40,8},{44,12},{48,16},{52,20},{56,24},{60,28},{64,3... | collective-permute-start | bytes 884744 | tf_op jit(solution)/shard_map/ppermute | solution.py:299
  29.0 8.3 %collective-permute-start.10 = (bf16[192,384]{1,0:T(8,128)(2,1)S(1)}, bf16[192,384]{1,0:T(8,128)(2,1)S(1)}, u32[]{:S(2)}, u32[]{:S(2)}) collective-permute-start(bf16[192,384]{1,0:T(8,128)(2,1)S(1)} %get-tuple-element.48), channel_id=1, source_target_pairs={{12,0},{8,4},{20,8},{16,12},{28,16},{24,20},{36,24},{32,28},{44,32... | collective-permute-start | bytes 442376 | tf_op jit(solution)/shard_map/ppermute | solution.py:300
  29.0 14.4 %collective-permute-start.9 = (bf16[192,384]{1,0:T(8,128)(2,1)S(1)}, bf16[192,384]{1,0:T(8,128)(2,1)S(1)}, u32[]{:S(2)}, u32[]{:S(2)}) collective-permute-start(bf16[192,384]{1,0:T(8,128)(2,1)S(1)} %get-tuple-element.48), channel_id=1, source_target_pairs={{8,0},{12,4},{16,8},{20,12},{24,16},{28,20},{32,24},{36,28},{40,32... | collective-permute-start | bytes 442376 | tf_op jit(solution)/shard_map/ppermute | solution.py:26
  29.5 36.7 %copy-start.4 = (bf16[192,384]{1,0:T(8,128)(2,1)S(1)}, bf16[192,384]{1,0:T(8,128)(2,1)}, u32[]{:S(2)}) copy-start(bf16[192,384]{1,0:T(8,128)(2,1)} %copy-done.3) | copy-start | bytes 442372
  43.4 9.0 %collective-permute-start.11 = (bf16[2,192,384]{2,1,0:T(8,128)(2,1)S(1)}, bf16[2,192,384]{2,1,0:T(8,128)(2,1)S(1)}, u32[]{:S(2)}, u32[]{:S(2)}) collective-permute-start(bf16[2,192,384]{2,1,0:T(8,128)(2,1)S(1)} %collective-permute-done.7), channel_id=1, source_target_pairs={{224,0},{228,4},{232,8},{236,12},{240,16},{244,20},{248,24},{252,2... | collective-permute-start | bytes 884744 | tf_op jit(solution)/shard_map/ppermute | solution.py:303
  43.4 9.0 %collective-permute-start.13 = (bf16[2,192,384]{2,1,0:T(8,128)(2,1)S(1)}, bf16[2,192,384]{2,1,0:T(8,128)(2,1)S(1)}, u32[]{:S(2)}, u32[]{:S(2)}) collective-permute-start(bf16[2,192,384]{2,1,0:T(8,128)(2,1)S(1)} %collective-permute-done.8), channel_id=1, source_target_pairs={{32,0},{36,4},{40,8},{44,12},{48,16},{52,20},{56,24},{60,28},{64,3... | collective-permute-start | bytes 884744 | tf_op jit(solution)/shard_map/ppermute | solution.py:303
  47.3 14.6 %collective-permute-start.15 = (bf16[2,192,384]{2,1,0:T(8,128)(2,1)S(1)}, bf16[2,192,384]{2,1,0:T(8,128)(2,1)S(1)}, u32[]{:S(2)}, u32[]{:S(2)}) collective-permute-start(bf16[2,192,384]{2,1,0:T(8,128)(2,1)S(1)} %pad_maximum_fusion.1.refs_0_), channel_id=1, source_target_pairs={{8,0},{12,4},{16,8},{20,12},{24,16},{28,20},{0,24},{4,28},{40,32},... | collective-permute-start | bytes 884744 | tf_op jit(solution)/shard_map/ppermute | solution.py:305
  47.3 14.5 %collective-permute-start.16 = (bf16[2,192,384]{2,1,0:T(8,128)(2,1)S(1)}, bf16[2,192,384]{2,1,0:T(8,128)(2,1)S(1)}, u32[]{:S(2)}, u32[]{:S(2)}) collective-permute-start(bf16[2,192,384]{2,1,0:T(8,128)(2,1)S(1)} %pad_maximum_fusion.1.refs_0_), channel_id=1, source_target_pairs={{16,0},{20,4},{24,8},{28,12},{0,16},{4,20},{8,24},{12,28},{48,32},... | collective-permute-start | bytes 884744 | tf_op jit(solution)/shard_map/ppermute | solution.py:305
  48.6 13.8 %collective-permute-start.17 = (bf16[2,192,384]{2,1,0:T(8,128)(2,1)S(1)}, bf16[2,192,384]{2,1,0:T(8,128)(2,1)S(1)}, u32[]{:S(2)}, u32[]{:S(2)}) collective-permute-start(bf16[2,192,384]{2,1,0:T(8,128)(2,1)S(1)} %pad_maximum_fusion.1.refs_0_), channel_id=1, source_target_pairs={{24,0},{28,4},{0,8},{4,12},{8,16},{12,20},{16,24},{20,28},{56,32},... | collective-permute-start | bytes 884744 | tf_op jit(solution)/shard_map/ppermute | solution.py:305
  52.4 10.0 %collective-permute-start.12 = (bf16[2,192,384]{2,1,0:T(8,128)(2,1)S(1)}, bf16[2,192,384]{2,1,0:T(8,128)(2,1)S(1)}, u32[]{:S(2)}, u32[]{:S(2)}) collective-permute-start(bf16[2,192,384]{2,1,0:T(8,128)(2,1)S(1)} %collective-permute-done.11), channel_id=1, source_target_pairs={{224,0},{228,4},{232,8},{236,12},{240,16},{244,20},{248,24},{252,2... | collective-permute-start | bytes 884744 | tf_op jit(solution)/shard_map/ppermute | solution.py:307
  52.5 10.0 %collective-permute-start.14 = (bf16[2,192,384]{2,1,0:T(8,128)(2,1)S(1)}, bf16[2,192,384]{2,1,0:T(8,128)(2,1)S(1)}, u32[]{:S(2)}, u32[]{:S(2)}) collective-permute-start(bf16[2,192,384]{2,1,0:T(8,128)(2,1)S(1)} %collective-permute-done.13), channel_id=1, source_target_pairs={{32,0},{36,4},{40,8},{44,12},{48,16},{52,20},{56,24},{60,28},{64,3... | collective-permute-start | bytes 884744 | tf_op jit(solution)/shard_map/ppermute | solution.py:307
  62.5 9.4 %collective-permute-start.18 = (bf16[192,384]{1,0:T(8,128)(2,1)S(1)}, bf16[192,384]{1,0:T(8,128)(2,1)S(1)}, u32[]{:S(2)}, u32[]{:S(2)}) collective-permute-start(bf16[192,384]{1,0:T(8,128)(2,1)S(1)} %get-tuple-element.76.refs_5_), channel_id=1, source_target_pairs={{224,0},{228,4},{232,8},{236,12},{240,16},{244,20},{248,24},{252,2... | collective-permute-start | bytes 442376 | tf_op jit(solution)/shard_map/ppermute | solution.py:315
  62.6 9.3 %collective-permute-start.19 = (bf16[192,384]{1,0:T(8,128)(2,1)S(1)}, bf16[192,384]{1,0:T(8,128)(2,1)S(1)}, u32[]{:S(2)}, u32[]{:S(2)}) collective-permute-start(bf16[192,384]{1,0:T(8,128)(2,1)S(1)} %get-tuple-element.73.refs_10_), channel_id=1, source_target_pairs={{32,0},{36,4},{40,8},{44,12},{48,16},{52,20},{56,24},{60,28},{64,3... | collective-permute-start | bytes 442376 | tf_op jit(solution)/shard_map/ppermute | solution.py:316
  78.2 16.1 %copy-start.1 = (bf16[384,1536]{1,0:T(8,128)(2,1)S(1)}, bf16[384,1536]{1,0:T(8,128)(2,1)}, u32[]{:S(2)}) copy-start(bf16[384,1536]{1,0:T(8,128)(2,1)} %w_ref.1) | copy-start | bytes 3538948
  78.2 2.4 %collective-permute-start.20 = (bf16[4,208,384]{2,1,0:T(8,128)(2,1)S(1)}, bf16[4,208,384]{2,1,0:T(8,128)(2,1)S(1)}, u32[]{:S(2)}, u32[]{:S(2)}) collective-permute-start(bf16[4,208,384]{2,1,0:T(8,128)(2,1)S(1)} %shard_map.96), channel_id=1, source_target_pairs={{0,4},{4,0},{8,12},{12,8},{16,20},{20,16},{24,28},{28,24},{32,36},... | collective-permute-start | bytes 1916936 | tf_op jit(solution)/shard_map/ppermute | solution.py:319
  80.6 25.3 %copy-start.5 = (bf16[384,384]{1,0:T(8,128)(2,1)S(1)}, bf16[384,384]{1,0:T(8,128)(2,1)}, u32[]{:S(2)}) copy-start(bf16[384,384]{1,0:T(8,128)(2,1)} %param.10) | copy-start | bytes 884740
  81.4 9.5 %collective-permute-start.21 = (bf16[208,384]{1,0:T(8,128)(2,1)S(1)}, bf16[208,384]{1,0:T(8,128)(2,1)S(1)}, u32[]{:S(2)}, u32[]{:S(2)}) collective-permute-start(bf16[208,384]{1,0:T(8,128)(2,1)S(1)} %get-tuple-element.71), channel_id=1, source_target_pairs={{24,0},{28,4},{0,8},{4,12},{8,16},{12,20},{16,24},{20,28},{56,32},... | collective-permute-start | bytes 479240 | tf_op jit(solution)/shard_map/ppermute | solution.py:321
  83.8 8.5 %collective-permute-start.22 = (bf16[208,384]{1,0:T(8,128)(2,1)S(1)}, bf16[208,384]{1,0:T(8,128)(2,1)S(1)}, u32[]{:S(2)}, u32[]{:S(2)}) collective-permute-start(bf16[208,384]{1,0:T(8,128)(2,1)S(1)} %get-tuple-element.70), channel_id=1, source_target_pairs={{16,0},{20,4},{24,8},{28,12},{0,16},{4,20},{8,24},{12,28},{48,32},... | collective-permute-start | bytes 479240 | tf_op jit(solution)/shard_map/ppermute | solution.py:321
  83.8 10.5 %collective-permute-start.23 = (bf16[208,384]{1,0:T(8,128)(2,1)S(1)}, bf16[208,384]{1,0:T(8,128)(2,1)S(1)}, u32[]{:S(2)}, u32[]{:S(2)}) collective-permute-start(bf16[208,384]{1,0:T(8,128)(2,1)S(1)} %get-tuple-element.69), channel_id=1, source_target_pairs={{8,0},{12,4},{16,8},{20,12},{24,16},{28,20},{0,24},{4,28},{40,32},... | collective-permute-start | bytes 479240 | tf_op jit(solution)/shard_map/ppermute | solution.py:321
  95.2 7.8 %collective-permute-start.24 = (bf16[192,384]{1,0:T(8,128)(2,1)S(1)}, bf16[192,384]{1,0:T(8,128)(2,1)S(1)}, u32[]{:S(2)}, u32[]{:S(2)}) collective-permute-start(bf16[192,384]{1,0:T(8,128)(2,1)S(1)} %get-tuple-element.64), channel_id=1, source_target_pairs={{3,0},{0,1},{1,2},{2,3},{7,4},{4,5},{5,6},{6,7},{11,8},{8,9},{9,10... | collective-permute-start | bytes 442376 | tf_op jit(solution)/shard_map/ppermute | solution.py:26
  97.0 9.0 %collective-permute-start.25 = (bf16[192,384]{1,0:T(8,128)(2,1)S(1)}, bf16[192,384]{1,0:T(8,128)(2,1)S(1)}, u32[]{:S(2)}, u32[]{:S(2)}) collective-permute-start(bf16[192,384]{1,0:T(8,128)(2,1)S(1)} %get-tuple-element.65), channel_id=1, source_target_pairs={{2,0},{3,1},{0,2},{1,3},{6,4},{7,5},{4,6},{5,7},{10,8},{11,9},{8,1... | collective-permute-start | bytes 442376 | tf_op jit(solution)/shard_map/ppermute | solution.py:26
  99.3 6.6 %collective-permute-start.26 = (bf16[192,384]{1,0:T(8,128)(2,1)S(1)}, bf16[192,384]{1,0:T(8,128)(2,1)S(1)}, u32[]{:S(2)}, u32[]{:S(2)}) collective-permute-start(bf16[192,384]{1,0:T(8,128)(2,1)S(1)} %get-tuple-element.66), channel_id=1, source_target_pairs={{1,0},{2,1},{3,2},{0,3},{5,4},{6,5},{7,6},{4,7},{9,8},{10,9},{11,1... | collective-permute-start | bytes 442376 | tf_op jit(solution)/shard_map/ppermute | solution.py:26

commit v5 on v3

--- a/solution.py
+++ b/solution.py
@@ -257,6 +257,7 @@
         6 << 20,
     )(x_arg, latents, *chunks, modulation[1], modulation[0], w_near)
     all_sums = [sums] + [shift(sums, "head", j) for j in range(1, heads_ax)]
+    all_sums, home_latents = lax.optimization_barrier((all_sums, home_latents))
     qn, kn = call(
         norm_kernel,
         [VMEM] * 8,
@@ -312,7 +313,6 @@
 
     ks[4] = lax.ppermute(ks[3], "queue", key_route(1))
     vs[4] = lax.ppermute(vs[-3], "queue", key_route(-1))
-    ks[4], vs[4], home_latents = lax.optimization_barrier((ks[4], vs[4], home_latents))
     partials = [partial(distances) for distances in GROUPS]
     mine, other = [p[0] for p in partials], [p[1] for p in partials]
     received = lax.ppermute(combine(other), "queue", swap)

time: 106 us -> 106 us (level)
  waiting for transfers between devices: 36.4 us -> 39.8 us
  starting transfers between devices: 40.2 us -> 38.6 us
  Pallas kernels: 16.8 us -> 15.7 us
    ppermute x1, waiting for transfers between devices: 0.33 us -> 7.57 us  [local(): lax.ppermute(qn, 'queue', [((i + 2) % slabs ^ 1, i) for i in range(slabs)])]
    ppermute x2, waiting for transfers between devices: 3.6 us -> 1.81 us  [local(): both[way * 2] = lax.ppermute(both[way], 'queue', key_route(way))]
    ppermute x3, starting transfers between devices: 4.77 us -> 3.38 us  [local(): lax.ppermute(paired[j], 'queue', y_route(j))]
    ppermute x11, waiting for transfers between devices: 13.3 us -> 12.1 us  [shift(): lax.ppermute(block, axis, [((i - distance) % n, i) for i in range(n)])]
    ppermute x1, starting transfers between devices: 1.16 us -> 0.08 us  [local(): ks[4] = lax.ppermute(ks[3], 'queue', key_route(1))]
    ppermute x1, starting transfers between devices: 2.45 us -> 3.51 us  [local(): vs[4] = lax.ppermute(vs[-3], 'queue', key_route(-1))]
    unnamed x18 -> x12, local copies, waits for them, and re-layouts: 2.94 us -> 2.57 us
  transfers between devices with their start and end apart: 27 -> 27, of which waited for: 13 -> 13; matrix products, arithmetic and copies ran while one was open for 3% -> 3% of each run, Pallas kernels for 6% -> 7%
where the time goes in v5:
time: 106 us
  waiting for transfers between devices  39.8 us (38%)
  starting transfers between devices  38.6 us (36%)
  Pallas kernels  15.7 us (15%)
  local copies, waits for them, and re-layouts  5.99 us (6%)
  between operations  4.78 us (5%)
    ppermute x11, starting transfers between devices, shift(): lax.ppermute(block, axis, [((i - distance) % n, i) for i in range(n)])  14.9 us
    ppermute x11, waiting for transfers between devices, shift(): lax.ppermute(block, axis, [((i - distance) % n, i) for i in range(n)])  12.1 us
    pallas_call x2, Pallas kernels, attend(): call(functools.partial(attend_kernel, slabs), [SMEM] + [VMEM] * (slots +...  11.4 us
    ppermute x3, waiting for transfers between devices, local(): lax.ppermute(paired[j], 'queue', y_route(j))  9.54 us
    ppermute x1, waiting for transfers between devices, local(): lax.ppermute(qn, 'queue', [((i + 2) % slabs ^ 1, i) for i in range(slabs)])  7.57 us
    ppermute x3, waiting for transfers between devices, local(): lax.ppermute(home_q, 'queue', y_route(-j))  6.68 us
    ppermute x2, starting transfers between devices, local(): both[way] = lax.ppermute(both[0], 'queue', key_route(way))  6.01 us
    ppermute x2, starting transfers between devices, local(): both[way * 2] = lax.ppermute(both[way], 'queue', key_route(way))  3.81 us
  transfers between devices with their start and end apart: 27, of which 13 were waited for; matrix products, arithmetic and copies ran while one was open for 3% of the time, Pallas kernels for 7%

profile of v5, /device:TPU:24, one launch (start us, length us, event | category | flops | bytes accessed | tf_op | source)
XLA Modules:
  0.0 105.6 jit_solution(5753400680811229483)
XLA Ops:
  0.0 1.5 %collective-permute-start = (bf16[192,384]{1,0:T(8,128)(2,1)}, bf16[192,384]{1,0:T(8,128)(2,1)S(1)}, u32[]{:S(2)}, u32[]{:S(2)}) collective-permute-start(bf16[192,384]{1,0:T(8,128)(2,1)} %own.1), channel_id=1, source_target_pairs={{3,0},{0,1},{1,2},{2,3},{7,4},{4,5},{5,6},{6,7},{11,8},{8,9},{9,10... | collective-permute-start | bytes 442376 | tf_op jit(solution)/shard_map/ppermute | solution.py:26
  1.5 2.7 %collective-permute-start.1 = (bf16[192,384]{1,0:T(8,128)(2,1)}, bf16[192,384]{1,0:T(8,128)(2,1)S(1)}, u32[]{:S(2)}, u32[]{:S(2)}) collective-permute-start(bf16[192,384]{1,0:T(8,128)(2,1)} %own.1), channel_id=1, source_target_pairs={{2,0},{3,1},{0,2},{1,3},{6,4},{7,5},{4,6},{5,7},{10,8},{11,9},{8,1... | collective-permute-start | bytes 442376 | tf_op jit(solution)/shard_map/ppermute | solution.py:26
  4.2 1.4 %collective-permute-start.2 = (bf16[192,384]{1,0:T(8,128)(2,1)}, bf16[192,384]{1,0:T(8,128)(2,1)S(1)}, u32[]{:S(2)}, u32[]{:S(2)}) collective-permute-start(bf16[192,384]{1,0:T(8,128)(2,1)} %own.1), channel_id=1, source_target_pairs={{1,0},{2,1},{3,2},{0,3},{5,4},{6,5},{7,6},{4,7},{9,8},{10,9},{11,1... | collective-permute-start | bytes 442376 | tf_op jit(solution)/shard_map/ppermute | solution.py:26
  5.7 0.7 collective-permute-start.6
  7.1 1.3 %fusion.1 = (s32[1]{0:T(128)}, s32[1]{0:T(128)}) fusion(s32[32]{0:T(128)} %param.11, s32[]{:T(128)S(6)} %select_n.371, s32[]{:T(128)S(6)} %select_n.368), kind=kLoop, calls=%fused_computation.23 | loop fusion | bytes 24 | tf_op jit(solution)/shard_map/dynamic_slice | solution.py:242
  10.4 0.8 constant_dynamic-slice_fusion.1
  11.2 2.0 %copy-done = bf16[1536,3,384]{2,0,1:T(8,128)(2,1)S(1)} copy-done((bf16[1536,3,384]{2,0,1:T(8,128)(2,1)S(1)}, bf16[1536,3,384]{2,0,1:T(8,128)(2,1)}, u32[]{:S(2)}) %copy-start) | copy-done | bytes 3538968
  13.2 0.3 shard_map.91.w_ref
  13.6 0.5 copy-done.2
  14.1 1.6 %shard_map.92 = (f32[192,384]{1,0:T(8,128)S(1)}, f32[192,384]{1,0:T(8,128)S(1)}, bf16[192,384]{1,0:T(8,128)(2,1)S(1)}, f32[8,192]{1,0:T(8,128)S(1)}) custom-call(s32[1]{0:T(128)} %bitcast.1.x_ref, bf16[192,384]{1,0:T(8,128)(2,1)S(1)} %copy-done.2, bf16[192,384]{1,0:T(8,128)(2,1)S(1)} %collective-permute-done.one, ...), custom_call_target="tpu_custom_call" | custom-call | flops 679477248 | bytes 6291456 | tf_op jit(solution)/shard_map/pallas_call | solution.py:247
  15.7 0.7 collective-permute-start.3
  16.4 0.9 collective-permute-start.4
  17.2 1.9 %collective-permute-start.5 = (f32[8,192]{1,0:T(8,128)S(1)}, f32[8,192]{1,0:T(8,128)S(1)}, u32[]{:S(2)}, u32[]{:S(2)}) collective-permute-start(f32[8,192]{1,0:T(8,128)S(1)} %get-tuple-element.38.s0), channel_id=1, source_target_pairs={{1,0},{2,1},{3,2},{0,3},{5,4},{6,5},{7,6},{4,7},{9,8},{10,9},{11,1... | collective-permute-start | bytes 18440 | tf_op jit(solution)/shard_map/ppermute | solution.py:26
  19.2 1.5 %collective-permute-done.3.s1 = f32[8,192]{1,0:T(8,128)S(1)} collective-permute-done((f32[8,192]{1,0:T(8,128)S(1)}, f32[8,192]{1,0:T(8,128)S(1)}, u32[]{:S(2)}, u32[]{:S(2)}) %collective-permute-start.3) | collective-permute-done | bytes 6176 | tf_op jit(solution)/shard_map/ppermute | solution.py:26
  20.6 0.9 collective-permute-done.4.s2
  21.6 0.3 shard_map.93
  21.9 2.0 %collective-permute-start.7 = (bf16[2,192,384]{2,1,0:T(8,128)(2,1)S(1)}, bf16[2,192,384]{2,1,0:T(8,128)(2,1)S(1)}, u32[]{:S(2)}, u32[]{:S(2)}) collective-permute-start(bf16[2,192,384]{2,1,0:T(8,128)(2,1)S(1)} %pad_maximum_fusion), channel_id=1, source_target_pairs={{224,0},{228,4},{232,8},{236,12},{240,16},{244,20},{248,24},{252,2... | collective-permute-start | bytes 884744 | tf_op jit(solution)/shard_map/ppermute | solution.py:298
  23.9 4.0 %collective-permute-start.8 = (bf16[2,192,384]{2,1,0:T(8,128)(2,1)S(1)}, bf16[2,192,384]{2,1,0:T(8,128)(2,1)S(1)}, u32[]{:S(2)}, u32[]{:S(2)}) collective-permute-start(bf16[2,192,384]{2,1,0:T(8,128)(2,1)S(1)} %pad_maximum_fusion), channel_id=1, source_target_pairs={{32,0},{36,4},{40,8},{44,12},{48,16},{52,20},{56,24},{60,28},{64,3... | collective-permute-start | bytes 884744 | tf_op jit(solution)/shard_map/ppermute | solution.py:298
  27.9 0.5 collective-permute-start.9
  28.5 0.1 stack.136.flags
  28.6 7.6 %collective-permute-done.10 = bf16[192,384]{1,0:T(8,128)(2,1)S(1)} collective-permute-done((bf16[192,384]{1,0:T(8,128)(2,1)S(1)}, bf16[192,384]{1,0:T(8,128)(2,1)S(1)}, u32[]{:S(2)}, u32[]{:S(2)}) %collective-permute-start.10) | collective-permute-done | bytes 147488 | tf_op jit(solution)/shard_map/ppermute | solution.py:299
  36.2 6.2 %collective-permute-done.9 = bf16[192,384]{1,0:T(8,128)(2,1)S(1)} collective-permute-done((bf16[192,384]{1,0:T(8,128)(2,1)S(1)}, bf16[192,384]{1,0:T(8,128)(2,1)S(1)}, u32[]{:S(2)}, u32[]{:S(2)}) %collective-permute-start.9) | collective-permute-done | bytes 147488 | tf_op jit(solution)/shard_map/ppermute | solution.py:26
  42.4 3.8 %collective-permute-start.13 = (bf16[2,192,384]{2,1,0:T(8,128)(2,1)S(1)}, bf16[2,192,384]{2,1,0:T(8,128)(2,1)S(1)}, u32[]{:S(2)}, u32[]{:S(2)}) collective-permute-start(bf16[2,192,384]{2,1,0:T(8,128)(2,1)S(1)} %collective-permute-done.8), channel_id=1, source_target_pairs={{32,0},{36,4},{40,8},{44,12},{48,16},{52,20},{56,24},{60,28},{64,3... | collective-permute-start | bytes 884744 | tf_op jit(solution)/shard_map/ppermute | solution.py:302
  46.3 1.3 %collective-permute-start.16 = (bf16[2,192,384]{2,1,0:T(8,128)(2,1)S(1)}, bf16[2,192,384]{2,1,0:T(8,128)(2,1)S(1)}, u32[]{:S(2)}, u32[]{:S(2)}) collective-permute-start(bf16[2,192,384]{2,1,0:T(8,128)(2,1)S(1)} %pad_maximum_fusion.1.refs_0_), channel_id=1, source_target_pairs={{16,0},{20,4},{24,8},{28,12},{0,16},{4,20},{8,24},{12,28},{48,32},... | collective-permute-start | bytes 884744 | tf_op jit(solution)/shard_map/ppermute | solution.py:304
  47.6 1.9 %collective-permute-start.17 = (bf16[2,192,384]{2,1,0:T(8,128)(2,1)S(1)}, bf16[2,192,384]{2,1,0:T(8,128)(2,1)S(1)}, u32[]{:S(2)}, u32[]{:S(2)}) collective-permute-start(bf16[2,192,384]{2,1,0:T(8,128)(2,1)S(1)} %pad_maximum_fusion.1.refs_0_), channel_id=1, source_target_pairs={{24,0},{28,4},{0,8},{4,12},{8,16},{12,20},{16,24},{20,28},{56,32},... | collective-permute-start | bytes 884744 | tf_op jit(solution)/shard_map/ppermute | solution.py:304
  49.6 1.8 %collective-permute-done.11 = bf16[2,192,384]{2,1,0:T(8,128)(2,1)S(1)} collective-permute-done((bf16[2,192,384]{2,1,0:T(8,128)(2,1)S(1)}, bf16[2,192,384]{2,1,0:T(8,128)(2,1)S(1)}, u32[]{:S(2)}, u32[]{:S(2)}) %collective-permute-start.11) | collective-permute-done | bytes 294944 | tf_op jit(solution)/shard_map/ppermute | solution.py:302
  51.4 3.2 %collective-permute-start.14 = (bf16[2,192,384]{2,1,0:T(8,128)(2,1)S(1)}, bf16[2,192,384]{2,1,0:T(8,128)(2,1)S(1)}, u32[]{:S(2)}, u32[]{:S(2)}) collective-permute-start(bf16[2,192,384]{2,1,0:T(8,128)(2,1)S(1)} %collective-permute-done.13), channel_id=1, source_target_pairs={{32,0},{36,4},{40,8},{44,12},{48,16},{52,20},{56,24},{60,28},{64,3... | collective-permute-start | bytes 884744 | tf_op jit(solution)/shard_map/ppermute | solution.py:306
  54.7 6.1 %collective-permute-done.15.refs_1_ = bf16[2,192,384]{2,1,0:T(8,128)(2,1)S(1)} collective-permute-done((bf16[2,192,384]{2,1,0:T(8,128)(2,1)S(1)}, bf16[2,192,384]{2,1,0:T(8,128)(2,1)S(1)}, u32[]{:S(2)}, u32[]{:S(2)}) %collective-permute-start.15) | collective-permute-done | bytes 294944 | tf_op jit(solution)/shard_map/ppermute | solution.py:304
  60.8 0.6 collective-permute-done.17.refs_3_
  61.6 3.5 %collective-permute-start.19 = (bf16[192,384]{1,0:T(8,128)(2,1)S(1)}, bf16[192,384]{1,0:T(8,128)(2,1)S(1)}, u32[]{:S(2)}, u32[]{:S(2)}) collective-permute-start(bf16[192,384]{1,0:T(8,128)(2,1)S(1)} %get-tuple-element.69.refs_10_), channel_id=1, source_target_pairs={{32,0},{36,4},{40,8},{44,12},{48,16},{52,20},{56,24},{60,28},{64,3... | collective-permute-start | bytes 442376 | tf_op jit(solution)/shard_map/ppermute | solution.py:315
  65.1 5.7 %shard_map.94 = (bf16[4,208,384]{2,1,0:T(8,128)(2,1)S(1)}, bf16[4,208,384]{2,1,0:T(8,128)(2,1)S(1)}) custom-call(f32[16]{0:T(128)S(1)} %stack.136.flags, bf16[2,192,384]{2,1,0:T(8,128)(2,1)S(1)} %pad_maximum_fusion.1.refs_0_, bf16[2,192,384]{2,1,0:T(8,128)(2,1)S(1)} %collective-permute-done.15.refs_1_, ...), custom_call_target="tpu_custom_call" | custom-call | flops 6341787648 | bytes 1048576 | tf_op jit(solution)/shard_map/pallas_call | solution.py:208
  70.8 5.7 %shard_map.95 = (bf16[4,208,384]{2,1,0:T(8,128)(2,1)S(1)}, bf16[4,208,384]{2,1,0:T(8,128)(2,1)S(1)}) custom-call(f32[16]{0:T(128)S(1)} %stack.159.flags, bf16[2,192,384]{2,1,0:T(8,128)(2,1)S(1)} %pad_maximum_fusion.1.refs_0_, bf16[2,192,384]{2,1,0:T(8,128)(2,1)S(1)} %collective-permute-done.15.refs_1_, ...), custom_call_target="tpu_custom_call" | custom-call | flops 6341787648 | bytes 1048576 | tf_op jit(solution)/shard_map/pallas_call | solution.py:208
  76.5 0.6 shard_map.96
  77.1 0.4 collective-permute-start.20
  77.5 2.1 %collective-permute-done.20.refs_2_ = bf16[4,208,384]{2,1,0:T(8,128)(2,1)S(1)} collective-permute-done((bf16[4,208,384]{2,1,0:T(8,128)(2,1)S(1)}, bf16[4,208,384]{2,1,0:T(8,128)(2,1)S(1)}, u32[]{:S(2)}, u32[]{:S(2)}) %collective-permute-start.20) | collective-permute-done | bytes 639008 | tf_op jit(solution)/shard_map/ppermute | solution.py:318
  79.5 0.7 shard_map.97
  80.3 2.4 %collective-permute-start.21 = (bf16[208,384]{1,0:T(8,128)(2,1)S(1)}, bf16[208,384]{1,0:T(8,128)(2,1)S(1)}, u32[]{:S(2)}, u32[]{:S(2)}) collective-permute-start(bf16[208,384]{1,0:T(8,128)(2,1)S(1)} %get-tuple-element.67), channel_id=1, source_target_pairs={{24,0},{28,4},{0,8},{4,12},{8,16},{12,20},{16,24},{20,28},{56,32},... | collective-permute-start | bytes 479240 | tf_op jit(solution)/shard_map/ppermute | solution.py:320
  82.7 1.0 collective-permute-start.23
  83.7 6.2 %collective-permute-done.21.b = bf16[208,384]{1,0:T(8,128)(2,1)S(1)} collective-permute-done((bf16[208,384]{1,0:T(8,128)(2,1)S(1)}, bf16[208,384]{1,0:T(8,128)(2,1)S(1)}, u32[]{:S(2)}, u32[]{:S(2)}) %collective-permute-start.21) | collective-permute-done | bytes 159776 | tf_op jit(solution)/shard_map/ppermute | solution.py:320
  89.9 1.4 %collective-permute-done.22.c = bf16[208,384]{1,0:T(8,128)(2,1)S(1)} collective-permute-done((bf16[208,384]{1,0:T(8,128)(2,1)S(1)}, bf16[208,384]{1,0:T(8,128)(2,1)S(1)}, u32[]{:S(2)}, u32[]{:S(2)}) %collective-permute-start.22) | collective-permute-done | bytes 159776 | tf_op jit(solution)/shard_map/ppermute | solution.py:320
  91.2 2.0 %collective-permute-done.23.d = bf16[208,384]{1,0:T(8,128)(2,1)S(1)} collective-permute-done((bf16[208,384]{1,0:T(8,128)(2,1)S(1)}, bf16[208,384]{1,0:T(8,128)(2,1)S(1)}, u32[]{:S(2)}, u32[]{:S(2)}) %collective-permute-start.23) | collective-permute-done | bytes 159776 | tf_op jit(solution)/shard_map/ppermute | solution.py:320
  93.2 0.9 shard_map.98
  94.1 1.8 %collective-permute-start.24 = (bf16[192,384]{1,0:T(8,128)(2,1)S(1)}, bf16[192,384]{1,0:T(8,128)(2,1)S(1)}, u32[]{:S(2)}, u32[]{:S(2)}) collective-permute-start(bf16[192,384]{1,0:T(8,128)(2,1)S(1)} %get-tuple-element.60), channel_id=1, source_target_pairs={{3,0},{0,1},{1,2},{2,3},{7,4},{4,5},{5,6},{6,7},{11,8},{8,9},{9,10... | collective-permute-start | bytes 442376 | tf_op jit(solution)/shard_map/ppermute | solution.py:26
  95.9 2.4 %collective-permute-start.25 = (bf16[192,384]{1,0:T(8,128)(2,1)S(1)}, bf16[192,384]{1,0:T(8,128)(2,1)S(1)}, u32[]{:S(2)}, u32[]{:S(2)}) collective-permute-start(bf16[192,384]{1,0:T(8,128)(2,1)S(1)} %get-tuple-element.61), channel_id=1, source_target_pairs={{2,0},{3,1},{0,2},{1,3},{6,4},{7,5},{4,6},{5,7},{10,8},{11,9},{8,1... | collective-permute-start | bytes 442376 | tf_op jit(solution)/shard_map/ppermute | solution.py:26
  98.3 0.4 collective-permute-start.26
  100.6 0.8 dynamic-slice_reduce_fusion
  101.4 3.5 %collective-permute-done.25 = bf16[192,384]{1,0:T(8,128)(2,1)S(1)} collective-permute-done((bf16[192,384]{1,0:T(8,128)(2,1)S(1)}, bf16[192,384]{1,0:T(8,128)(2,1)S(1)}, u32[]{:S(2)}, u32[]{:S(2)}) %collective-permute-start.25) | collective-permute-done | bytes 147488 | tf_op jit(solution)/shard_map/ppermute | solution.py:26
  104.9 0.8 fusion
  (42 shorter events, 0.7 us)
Async XLA Ops:
  0.0 13.6 %collective-permute-start = (bf16[192,384]{1,0:T(8,128)(2,1)}, bf16[192,384]{1,0:T(8,128)(2,1)S(1)}, u32[]{:S(2)}, u32[]{:S(2)}) collective-permute-start(bf16[192,384]{1,0:T(8,128)(2,1)} %own.1), channel_id=1, source_target_pairs={{3,0},{0,1},{1,2},{2,3},{7,4},{4,5},{5,6},{6,7},{11,8},{8,9},{9,10... | collective-permute-start | bytes 442376 | tf_op jit(solution)/shard_map/ppermute | solution.py:26
  1.5 12.1 %collective-permute-start.1 = (bf16[192,384]{1,0:T(8,128)(2,1)}, bf16[192,384]{1,0:T(8,128)(2,1)S(1)}, u32[]{:S(2)}, u32[]{:S(2)}) collective-permute-start(bf16[192,384]{1,0:T(8,128)(2,1)} %own.1), channel_id=1, source_target_pairs={{2,0},{3,1},{0,2},{1,3},{6,4},{7,5},{4,6},{5,7},{10,8},{11,9},{8,1... | collective-permute-start | bytes 442376 | tf_op jit(solution)/shard_map/ppermute | solution.py:26
  4.2 9.4 %collective-permute-start.2 = (bf16[192,384]{1,0:T(8,128)(2,1)}, bf16[192,384]{1,0:T(8,128)(2,1)S(1)}, u32[]{:S(2)}, u32[]{:S(2)}) collective-permute-start(bf16[192,384]{1,0:T(8,128)(2,1)} %own.1), channel_id=1, source_target_pairs={{1,0},{2,1},{3,2},{0,3},{5,4},{6,5},{7,6},{4,7},{9,8},{10,9},{11,1... | collective-permute-start | bytes 442376 | tf_op jit(solution)/shard_map/ppermute | solution.py:26
  5.7 13.5 %collective-permute-start.6 = (bf16[192,384]{1,0:T(8,128)(2,1)}, bf16[192,384]{1,0:T(8,128)(2,1)S(1)}, u32[]{:S(2)}, u32[]{:S(2)}) collective-permute-start(bf16[192,384]{1,0:T(8,128)(2,1)} %own.1), channel_id=1, source_target_pairs={{8,0},{12,4},{16,8},{20,12},{24,16},{28,20},{32,24},{36,28},{40,32... | collective-permute-start | bytes 442376 | tf_op jit(solution)/shard_map/ppermute | solution.py:26
  11.2 2.0 %copy-start = (bf16[1536,3,384]{2,0,1:T(8,128)(2,1)S(1)}, bf16[1536,3,384]{2,0,1:T(8,128)(2,1)}, u32[]{:S(2)}) copy-start(bf16[1536,3,384]{2,0,1:T(8,128)(2,1)} %param.14) | copy-start | bytes 10616836
  13.2 0.9 copy-start.2
  13.5 5.6 %copy-start.4 = (f32[384]{0:T(512)S(1)}, f32[384]{0:T(512)}, u32[]{:S(2)}) copy-start(f32[384]{0:T(512)} %param.16) | copy-start | bytes 4612
  13.5 5.6 %copy-start.5 = (f32[384]{0:T(512)S(1)}, f32[384]{0:T(512)}, u32[]{:S(2)}) copy-start(f32[384]{0:T(512)} %param.17) | copy-start | bytes 4612
  15.7 4.9 %collective-permute-start.3 = (f32[8,192]{1,0:T(8,128)S(1)}, f32[8,192]{1,0:T(8,128)S(1)}, u32[]{:S(2)}, u32[]{:S(2)}) collective-permute-start(f32[8,192]{1,0:T(8,128)S(1)} %get-tuple-element.38.s0), channel_id=1, source_target_pairs={{3,0},{0,1},{1,2},{2,3},{7,4},{4,5},{5,6},{6,7},{11,8},{8,9},{9,10... | collective-permute-start | bytes 18440 | tf_op jit(solution)/shard_map/ppermute | solution.py:26
  16.4 5.2 %collective-permute-start.4 = (f32[8,192]{1,0:T(8,128)S(1)}, f32[8,192]{1,0:T(8,128)S(1)}, u32[]{:S(2)}, u32[]{:S(2)}) collective-permute-start(f32[8,192]{1,0:T(8,128)S(1)} %get-tuple-element.38.s0), channel_id=1, source_target_pairs={{2,0},{3,1},{0,2},{1,3},{6,4},{7,5},{4,6},{5,7},{10,8},{11,9},{8,1... | collective-permute-start | bytes 18440 | tf_op jit(solution)/shard_map/ppermute | solution.py:26
  17.2 4.3 %collective-permute-start.5 = (f32[8,192]{1,0:T(8,128)S(1)}, f32[8,192]{1,0:T(8,128)S(1)}, u32[]{:S(2)}, u32[]{:S(2)}) collective-permute-start(f32[8,192]{1,0:T(8,128)S(1)} %get-tuple-element.38.s0), channel_id=1, source_target_pairs={{1,0},{2,1},{3,2},{0,3},{5,4},{6,5},{7,6},{4,7},{9,8},{10,9},{11,1... | collective-permute-start | bytes 18440 | tf_op jit(solution)/shard_map/ppermute | solution.py:26
  21.9 20.4 %collective-permute-start.7 = (bf16[2,192,384]{2,1,0:T(8,128)(2,1)S(1)}, bf16[2,192,384]{2,1,0:T(8,128)(2,1)S(1)}, u32[]{:S(2)}, u32[]{:S(2)}) collective-permute-start(bf16[2,192,384]{2,1,0:T(8,128)(2,1)S(1)} %pad_maximum_fusion), channel_id=1, source_target_pairs={{224,0},{228,4},{232,8},{236,12},{240,16},{244,20},{248,24},{252,2... | collective-permute-start | bytes 884744 | tf_op jit(solution)/shard_map/ppermute | solution.py:298
  23.9 18.4 %collective-permute-start.8 = (bf16[2,192,384]{2,1,0:T(8,128)(2,1)S(1)}, bf16[2,192,384]{2,1,0:T(8,128)(2,1)S(1)}, u32[]{:S(2)}, u32[]{:S(2)}) collective-permute-start(bf16[2,192,384]{2,1,0:T(8,128)(2,1)S(1)} %pad_maximum_fusion), channel_id=1, source_target_pairs={{32,0},{36,4},{40,8},{44,12},{48,16},{52,20},{56,24},{60,28},{64,3... | collective-permute-start | bytes 884744 | tf_op jit(solution)/shard_map/ppermute | solution.py:298
  27.9 8.3 %collective-permute-start.10 = (bf16[192,384]{1,0:T(8,128)(2,1)S(1)}, bf16[192,384]{1,0:T(8,128)(2,1)S(1)}, u32[]{:S(2)}, u32[]{:S(2)}) collective-permute-start(bf16[192,384]{1,0:T(8,128)(2,1)S(1)} %get-tuple-element.44), channel_id=1, source_target_pairs={{12,0},{8,4},{20,8},{16,12},{28,16},{24,20},{36,24},{32,28},{44,32... | collective-permute-start | bytes 442376 | tf_op jit(solution)/shard_map/ppermute | solution.py:299
  27.9 14.4 %collective-permute-start.9 = (bf16[192,384]{1,0:T(8,128)(2,1)S(1)}, bf16[192,384]{1,0:T(8,128)(2,1)S(1)}, u32[]{:S(2)}, u32[]{:S(2)}) collective-permute-start(bf16[192,384]{1,0:T(8,128)(2,1)S(1)} %get-tuple-element.44), channel_id=1, source_target_pairs={{8,0},{12,4},{16,8},{20,12},{24,16},{28,20},{32,24},{36,28},{40,32... | collective-permute-start | bytes 442376 | tf_op jit(solution)/shard_map/ppermute | solution.py:26
  42.4 9.0 %collective-permute-start.11 = (bf16[2,192,384]{2,1,0:T(8,128)(2,1)S(1)}, bf16[2,192,384]{2,1,0:T(8,128)(2,1)S(1)}, u32[]{:S(2)}, u32[]{:S(2)}) collective-permute-start(bf16[2,192,384]{2,1,0:T(8,128)(2,1)S(1)} %collective-permute-done.7), channel_id=1, source_target_pairs={{224,0},{228,4},{232,8},{236,12},{240,16},{244,20},{248,24},{252,2... | collective-permute-start | bytes 884744 | tf_op jit(solution)/shard_map/ppermute | solution.py:302
  42.4 9.0 %collective-permute-start.13 = (bf16[2,192,384]{2,1,0:T(8,128)(2,1)S(1)}, bf16[2,192,384]{2,1,0:T(8,128)(2,1)S(1)}, u32[]{:S(2)}, u32[]{:S(2)}) collective-permute-start(bf16[2,192,384]{2,1,0:T(8,128)(2,1)S(1)} %collective-permute-done.8), channel_id=1, source_target_pairs={{32,0},{36,4},{40,8},{44,12},{48,16},{52,20},{56,24},{60,28},{64,3... | collective-permute-start | bytes 884744 | tf_op jit(solution)/shard_map/ppermute | solution.py:302
  46.2 14.6 %collective-permute-start.15 = (bf16[2,192,384]{2,1,0:T(8,128)(2,1)S(1)}, bf16[2,192,384]{2,1,0:T(8,128)(2,1)S(1)}, u32[]{:S(2)}, u32[]{:S(2)}) collective-permute-start(bf16[2,192,384]{2,1,0:T(8,128)(2,1)S(1)} %pad_maximum_fusion.1.refs_0_), channel_id=1, source_target_pairs={{8,0},{12,4},{16,8},{20,12},{24,16},{28,20},{0,24},{4,28},{40,32},... | collective-permute-start | bytes 884744 | tf_op jit(solution)/shard_map/ppermute | solution.py:304
  46.3 14.5 %collective-permute-start.16 = (bf16[2,192,384]{2,1,0:T(8,128)(2,1)S(1)}, bf16[2,192,384]{2,1,0:T(8,128)(2,1)S(1)}, u32[]{:S(2)}, u32[]{:S(2)}) collective-permute-start(bf16[2,192,384]{2,1,0:T(8,128)(2,1)S(1)} %pad_maximum_fusion.1.refs_0_), channel_id=1, source_target_pairs={{16,0},{20,4},{24,8},{28,12},{0,16},{4,20},{8,24},{12,28},{48,32},... | collective-permute-start | bytes 884744 | tf_op jit(solution)/shard_map/ppermute | solution.py:304
  47.6 13.8 %collective-permute-start.17 = (bf16[2,192,384]{2,1,0:T(8,128)(2,1)S(1)}, bf16[2,192,384]{2,1,0:T(8,128)(2,1)S(1)}, u32[]{:S(2)}, u32[]{:S(2)}) collective-permute-start(bf16[2,192,384]{2,1,0:T(8,128)(2,1)S(1)} %pad_maximum_fusion.1.refs_0_), channel_id=1, source_target_pairs={{24,0},{28,4},{0,8},{4,12},{8,16},{12,20},{16,24},{20,28},{56,32},... | collective-permute-start | bytes 884744 | tf_op jit(solution)/shard_map/ppermute | solution.py:304
  51.4 10.0 %collective-permute-start.12 = (bf16[2,192,384]{2,1,0:T(8,128)(2,1)S(1)}, bf16[2,192,384]{2,1,0:T(8,128)(2,1)S(1)}, u32[]{:S(2)}, u32[]{:S(2)}) collective-permute-start(bf16[2,192,384]{2,1,0:T(8,128)(2,1)S(1)} %collective-permute-done.11), channel_id=1, source_target_pairs={{224,0},{228,4},{232,8},{236,12},{240,16},{244,20},{248,24},{252,2... | collective-permute-start | bytes 884744 | tf_op jit(solution)/shard_map/ppermute | solution.py:306
  51.4 10.0 %collective-permute-start.14 = (bf16[2,192,384]{2,1,0:T(8,128)(2,1)S(1)}, bf16[2,192,384]{2,1,0:T(8,128)(2,1)S(1)}, u32[]{:S(2)}, u32[]{:S(2)}) collective-permute-start(bf16[2,192,384]{2,1,0:T(8,128)(2,1)S(1)} %collective-permute-done.13), channel_id=1, source_target_pairs={{32,0},{36,4},{40,8},{44,12},{48,16},{52,20},{56,24},{60,28},{64,3... | collective-permute-start | bytes 884744 | tf_op jit(solution)/shard_map/ppermute | solution.py:306
  61.5 9.4 %collective-permute-start.18 = (bf16[192,384]{1,0:T(8,128)(2,1)S(1)}, bf16[192,384]{1,0:T(8,128)(2,1)S(1)}, u32[]{:S(2)}, u32[]{:S(2)}) collective-permute-start(bf16[192,384]{1,0:T(8,128)(2,1)S(1)} %get-tuple-element.72.refs_5_), channel_id=1, source_target_pairs={{224,0},{228,4},{232,8},{236,12},{240,16},{244,20},{248,24},{252,2... | collective-permute-start | bytes 442376 | tf_op jit(solution)/shard_map/ppermute | solution.py:314
  61.6 9.2 %collective-permute-start.19 = (bf16[192,384]{1,0:T(8,128)(2,1)S(1)}, bf16[192,384]{1,0:T(8,128)(2,1)S(1)}, u32[]{:S(2)}, u32[]{:S(2)}) collective-permute-start(bf16[192,384]{1,0:T(8,128)(2,1)S(1)} %get-tuple-element.69.refs_10_), channel_id=1, source_target_pairs={{32,0},{36,4},{40,8},{44,12},{48,16},{52,20},{56,24},{60,28},{64,3... | collective-permute-start | bytes 442376 | tf_op jit(solution)/shard_map/ppermute | solution.py:315
  77.1 16.1 %copy-start.1 = (bf16[384,1536]{1,0:T(8,128)(2,1)S(1)}, bf16[384,1536]{1,0:T(8,128)(2,1)}, u32[]{:S(2)}) copy-start(bf16[384,1536]{1,0:T(8,128)(2,1)} %w_ref.1) | copy-start | bytes 3538948
  77.1 2.4 %collective-permute-start.20 = (bf16[4,208,384]{2,1,0:T(8,128)(2,1)S(1)}, bf16[4,208,384]{2,1,0:T(8,128)(2,1)S(1)}, u32[]{:S(2)}, u32[]{:S(2)}) collective-permute-start(bf16[4,208,384]{2,1,0:T(8,128)(2,1)S(1)} %shard_map.96), channel_id=1, source_target_pairs={{0,4},{4,0},{8,12},{12,8},{16,20},{20,16},{24,28},{28,24},{32,36},... | collective-permute-start | bytes 1916936 | tf_op jit(solution)/shard_map/ppermute | solution.py:318
  79.5 25.3 %copy-start.3 = (bf16[384,384]{1,0:T(8,128)(2,1)S(1)}, bf16[384,384]{1,0:T(8,128)(2,1)}, u32[]{:S(2)}) copy-start(bf16[384,384]{1,0:T(8,128)(2,1)} %param.10) | copy-start | bytes 884740
  80.3 9.5 %collective-permute-start.21 = (bf16[208,384]{1,0:T(8,128)(2,1)S(1)}, bf16[208,384]{1,0:T(8,128)(2,1)S(1)}, u32[]{:S(2)}, u32[]{:S(2)}) collective-permute-start(bf16[208,384]{1,0:T(8,128)(2,1)S(1)} %get-tuple-element.67), channel_id=1, source_target_pairs={{24,0},{28,4},{0,8},{4,12},{8,16},{12,20},{16,24},{20,28},{56,32},... | collective-permute-start | bytes 479240 | tf_op jit(solution)/shard_map/ppermute | solution.py:320
  82.7 8.5 %collective-permute-start.22 = (bf16[208,384]{1,0:T(8,128)(2,1)S(1)}, bf16[208,384]{1,0:T(8,128)(2,1)S(1)}, u32[]{:S(2)}, u32[]{:S(2)}) collective-permute-start(bf16[208,384]{1,0:T(8,128)(2,1)S(1)} %get-tuple-element.66), channel_id=1, source_target_pairs={{16,0},{20,4},{24,8},{28,12},{0,16},{4,20},{8,24},{12,28},{48,32},... | collective-permute-start | bytes 479240 | tf_op jit(solution)/shard_map/ppermute | solution.py:320
  82.7 10.5 %collective-permute-start.23 = (bf16[208,384]{1,0:T(8,128)(2,1)S(1)}, bf16[208,384]{1,0:T(8,128)(2,1)S(1)}, u32[]{:S(2)}, u32[]{:S(2)}) collective-permute-start(bf16[208,384]{1,0:T(8,128)(2,1)S(1)} %get-tuple-element.65), channel_id=1, source_target_pairs={{8,0},{12,4},{16,8},{20,12},{24,16},{28,20},{0,24},{4,28},{40,32},... | collective-permute-start | bytes 479240 | tf_op jit(solution)/shard_map/ppermute | solution.py:320
  94.1 7.3 %collective-permute-start.24 = (bf16[192,384]{1,0:T(8,128)(2,1)S(1)}, bf16[192,384]{1,0:T(8,128)(2,1)S(1)}, u32[]{:S(2)}, u32[]{:S(2)}) collective-permute-start(bf16[192,384]{1,0:T(8,128)(2,1)S(1)} %get-tuple-element.60), channel_id=1, source_target_pairs={{3,0},{0,1},{1,2},{2,3},{7,4},{4,5},{5,6},{6,7},{11,8},{8,9},{9,10... | collective-permute-start | bytes 442376 | tf_op jit(solution)/shard_map/ppermute | solution.py:26
  95.9 9.0 %collective-permute-start.25 = (bf16[192,384]{1,0:T(8,128)(2,1)S(1)}, bf16[192,384]{1,0:T(8,128)(2,1)S(1)}, u32[]{:S(2)}, u32[]{:S(2)}) collective-permute-start(bf16[192,384]{1,0:T(8,128)(2,1)S(1)} %get-tuple-element.61), channel_id=1, source_target_pairs={{2,0},{3,1},{0,2},{1,3},{6,4},{7,5},{4,6},{5,7},{10,8},{11,9},{8,1... | collective-permute-start | bytes 442376 | tf_op jit(solution)/shard_map/ppermute | solution.py:26
  98.3 6.6 %collective-permute-start.26 = (bf16[192,384]{1,0:T(8,128)(2,1)S(1)}, bf16[192,384]{1,0:T(8,128)(2,1)S(1)}, u32[]{:S(2)}, u32[]{:S(2)}) collective-permute-start(bf16[192,384]{1,0:T(8,128)(2,1)S(1)} %get-tuple-element.62), channel_id=1, source_target_pairs={{1,0},{2,1},{3,2},{0,3},{5,4},{6,5},{7,6},{4,7},{9,8},{10,9},{11,1... | collective-permute-start | bytes 442376 | tf_op jit(solution)/shard_map/ppermute | solution.py:26
